TPU v7x, 128 devices: a whole 4x4x4 slice. The times are simulated.
128 devices in a mesh: ctx: 32 (over x, y, core), wt: 4 (over z).
Axes of the slice: x: 4, y: 4, z: 4, core: 2. Of those that a mesh axis runs over, the one named last changes fastest.
Arguments:
- tokens_in: bfloat16 [8, 2, 1024, 768], P('wt', None, 'ctx'), may hold values from -6 to 6
- cotangent: bfloat16 [8, 2, 1024, 768], P('wt', None, 'ctx'), may hold values from -6 to 6
- ln_gain_attn: bfloat16 [2, 768], P(None, 'wt'), may hold values from 0.5 to 1.5
- ln_shift_attn: bfloat16 [2, 768], P(None, 'wt'), may hold values from -1.5 to 1.5
- ln_gain_mlp: bfloat16 [2, 768], P(None, 'wt'), may hold values from 0.5 to 1.5
- ln_shift_mlp: bfloat16 [2, 768], P(None, 'wt'), may hold values from -1.5 to 1.5
- w_qkv: bfloat16 [2, 768, 2304], P(None, 'wt'), may hold values from -0.21875 to 0.21875
- b_qv: bfloat16 [2, 1536], P(None, 'wt'), may hold values from -2.5 to 2.5
- w_out: bfloat16 [2, 768, 768], P(None, 'wt'), may hold values from -6 to 6
- b_out: bfloat16 [2, 768], P(None, 'wt'), may hold values from -1.5 to 1.5
- w_up: bfloat16 [2, 768, 3072], P(None, 'wt'), may hold values from -0.21875 to 0.21875
- b_up: bfloat16 [2, 3072], P(None, 'wt'), may hold values from -2.5 to 2.5
- w_down: bfloat16 [2, 3072, 768], P(None, 'wt'), may hold values from -0.109375 to 0.109375
- b_down: bfloat16 [2, 768], P(None, 'wt'), may hold values from -1.5 to 1.5
Outputs:
- out_tokens: bfloat16 [8, 2, 1024, 768], P('wt', None, 'ctx')
- grad_tokens: float32 [8, 2, 1024, 768], P('wt', None, 'ctx')
- grad_ln_gain_attn: float32 [2, 768], P(None, 'wt')
- grad_ln_shift_attn: float32 [2, 768], P(None, 'wt')
- grad_ln_gain_mlp: float32 [2, 768], P(None, 'wt')
- grad_ln_shift_mlp: float32 [2, 768], P(None, 'wt')
- grad_w_qkv: float32 [2, 768, 2304], P(None, 'wt')
- grad_b_qv: float32 [2, 1536], P(None, 'wt')
- grad_w_out: float32 [2, 768, 768], P(None, 'wt')
- grad_b_out: float32 [2, 768], P(None, 'wt')
- grad_w_up: float32 [2, 768, 3072], P(None, 'wt')
- grad_b_up: float32 [2, 3072], P(None, 'wt')
- grad_w_down: float32 [2, 3072, 768], P(None, 'wt')
- grad_b_down: float32 [2, 768], P(None, 'wt')
All inputs are finite; a program needn't handle non-finite values.
Results may differ from a plain program's by a relative error of at most 0.02.
Values may be sent and summed in bfloat16 or wider, within the bound.
No kernel may reach another device: no remote copies, remote signals or barrier semaphores. Data moves between devices by JAX's collectives and lax.ppermute only.
A program may use at most 256 MiB of HBM per device.

v0:
```python
from functools import partial

import jax
import jax.numpy as jnp
from jax import lax
from jax.sharding import PartitionSpec as P

HEADS = 12
HEAD_DIM = 64
ROT = 16
LAYERS = 2


norm_epsilon = 1e-05


def normalize(values, gain, shift):
    centre = jnp.mean(values, axis=-1, keepdims=True)
    centred = values - centre
    spread = jnp.mean(centred * centred, axis=-1, keepdims=True)
    return centred * lax.rsqrt(spread + norm_epsilon) * gain + shift


def rotate(values, positions):
    halfway = ROT // 2
    frequency = 10000.0 ** (-jnp.arange(halfway, dtype=jnp.float32) * 2.0 / ROT)
    angles = positions.astype(jnp.float32)[:, None] * frequency[None, :]
    cosine = jnp.cos(angles)[:, None, :]
    sine_part = jnp.sin(angles)[:, None, :]
    leading = values[..., :halfway]
    trailing = values[..., halfway:ROT]
    return jnp.concatenate(
        [
            leading * cosine - trailing * sine_part,
            trailing * cosine + leading * sine_part,
            values[..., ROT:],
        ],
        axis=-1,
    )


def token_positions(block_rows):
    device = lax.axis_index("ctx")
    devices = lax.axis_size("ctx")
    seq_total = 2 * block_rows * devices
    offsets = jnp.arange(block_rows, dtype=jnp.int32)
    query_pos = jnp.concatenate(
        [device * block_rows + offsets, seq_total - (device + 1) * block_rows + offsets]
    )
    every = jnp.arange(devices * block_rows, dtype=jnp.int32)
    late_pos = seq_total - (every // block_rows + 1) * block_rows + every % block_rows
    key_pos = jnp.concatenate([every, late_pos])
    return (query_pos, key_pos)


def to_heads(flat, seq_count):
    return flat.reshape(seq_count, -1, HEADS, HEAD_DIM).transpose(0, 2, 1, 3)


def from_heads(split):
    return split.transpose(0, 2, 1, 3).reshape(-1, HEADS * HEAD_DIM)


def forward_heads(head_query, head_key, head_value, allowed):
    scaling = HEAD_DIM ** (-0.5)
    scores = (
        jnp.einsum("hqd,hkd->hqk", head_query, head_key, preferred_element_type=jnp.float32)
        * scaling
    )
    scores = jnp.where(allowed[None], scores, -1e30)
    top_score = jnp.max(scores, axis=2, keepdims=True)
    raised = jnp.exp(scores - top_score)
    row_total = jnp.sum(raised, axis=2, keepdims=True)
    attn_probs = raised / row_total
    context = jnp.einsum(
        "hqk,hkd->hqd",
        attn_probs.astype(jnp.bfloat16),
        head_value,
        preferred_element_type=jnp.float32,
    )
    return (context, top_score[..., 0] + jnp.log(row_total[..., 0]))


def forward_rows(operands, allowed):
    head_query, head_key, head_value = operands
    block_rows = head_query.shape[1] // 2
    half_keys = head_key.shape[1] // 2
    early_ctx, early_lse = forward_heads(
        head_query[:, :block_rows],
        head_key[:, :half_keys],
        head_value[:, :half_keys],
        allowed[:block_rows, :half_keys],
    )
    late_ctx, late_lse = forward_heads(
        head_query[:, block_rows:], head_key, head_value, allowed[block_rows:]
    )
    return (
        jnp.concatenate([early_ctx, late_ctx], axis=1),
        jnp.concatenate([early_lse, late_lse], axis=1),
    )


def query_part(head_query, head_key, head_value, head_grad, head_lse, allowed):
    scaling = HEAD_DIM ** (-0.5)
    scores = (
        jnp.einsum("hqd,hkd->hqk", head_query, head_key, preferred_element_type=jnp.float32)
        * scaling
    )
    scores = jnp.where(allowed[None], scores, -1e30)
    attn_probs = jnp.exp(scores - head_lse[..., None])
    grad_probs = jnp.einsum(
        "hqd,hkd->hqk", head_grad, head_value, preferred_element_type=jnp.float32
    )
    row_delta = jnp.sum(grad_probs * attn_probs, axis=2)
    grad_scores = (attn_probs * (grad_probs - row_delta[..., None])).astype(jnp.bfloat16)
    grad_query = (
        jnp.einsum("hqk,hkd->hqd", grad_scores, head_key, preferred_element_type=jnp.float32)
        * scaling
    )
    grad_key = (
        jnp.einsum("hqk,hqd->hkd", grad_scores, head_query, preferred_element_type=jnp.float32)
        * scaling
    )
    grad_value = jnp.einsum(
        "hqk,hqd->hkd",
        attn_probs.astype(jnp.bfloat16),
        head_grad,
        preferred_element_type=jnp.float32,
    )
    return (grad_query, grad_key, grad_value)


def query_rows(operands, allowed, with_keys):
    head_query, head_key, head_value, head_grad, head_lse = operands
    block_rows = head_query.shape[1] // 2
    half_keys = head_key.shape[1] // 2
    early = query_part(
        head_query[:, :block_rows],
        head_key[:, :half_keys],
        head_value[:, :half_keys],
        head_grad[:, :block_rows],
        head_lse[:, :block_rows],
        allowed[:block_rows, :half_keys],
    )
    late = query_part(
        head_query[:, block_rows:],
        head_key,
        head_value,
        head_grad[:, block_rows:],
        head_lse[:, block_rows:],
        allowed[block_rows:],
    )
    grad_query = jnp.concatenate([early[0], late[0]], axis=1)
    padding = ((0, 0), (0, half_keys), (0, 0))
    grad_key = late[1] + jnp.pad(early[1], padding)
    grad_value = late[2] + jnp.pad(early[2], padding)
    return (grad_query, grad_key, grad_value)


def layer_forward(residual, weights, query_pos, allowed):
    (
        gain_attn,
        shift_attn,
        gain_mlp,
        shift_mlp,
        w_qkv,
        b_qv,
        w_out,
        b_out,
        w_up,
        b_up,
        w_down,
        b_down,
    ) = weights
    row_count, model_width = residual.shape
    block_rows = query_pos.shape[0] // 2
    seq_count = row_count // query_pos.shape[0]
    row_pos = jnp.tile(query_pos, seq_count)
    normed_attn = normalize(
        residual, gain_attn.astype(jnp.float32), shift_attn.astype(jnp.float32)
    ).astype(jnp.bfloat16)
    normed_mlp = normalize(
        residual, gain_mlp.astype(jnp.float32), shift_mlp.astype(jnp.float32)
    ).astype(jnp.bfloat16)
    qkv_bias = jnp.concatenate(
        [b_qv[:model_width], jnp.zeros((model_width,), jnp.bfloat16), b_qv[model_width:]]
    ).astype(jnp.float32)
    projected = jnp.dot(normed_attn, w_qkv, preferred_element_type=jnp.float32) + qkv_bias
    split_heads = projected.reshape(row_count, 3, HEADS, HEAD_DIM)
    query_rot = (
        rotate(split_heads[:, 0], row_pos).astype(jnp.bfloat16).reshape(row_count, model_width)
    )
    key_rot = (
        rotate(split_heads[:, 1], row_pos).astype(jnp.bfloat16).reshape(row_count, model_width)
    )
    value_low = split_heads[:, 2].astype(jnp.bfloat16).reshape(row_count, model_width)
    key_every, value_every = (
        lax.all_gather(
            key_rot.reshape(seq_count, 2, block_rows, model_width), "ctx", axis=2, tiled=True
        ),
        lax.all_gather(
            value_low.reshape(seq_count, 2, block_rows, model_width), "ctx", axis=2, tiled=True
        ),
    )
    key_heads = to_heads(key_every.reshape(-1, model_width), seq_count)
    value_heads = to_heads(value_every.reshape(-1, model_width), seq_count)
    query_heads = to_heads(query_rot, seq_count)
    contexts, row_lse = lax.map(
        partial(forward_rows, allowed=allowed), (query_heads, key_heads, value_heads)
    )
    context = from_heads(contexts).astype(jnp.bfloat16)
    branch_attn = jnp.dot(context, w_out, preferred_element_type=jnp.float32) + b_out.astype(
        jnp.float32
    )
    hidden = jnp.dot(normed_mlp, w_up, preferred_element_type=jnp.float32) + b_up.astype(
        jnp.float32
    )
    active = jax.nn.gelu(hidden, approximate=False).astype(jnp.bfloat16)
    branch_mlp = jnp.dot(active, w_down, preferred_element_type=jnp.float32) + b_down.astype(
        jnp.float32
    )
    stored = (
        residual,
        normed_attn,
        normed_mlp,
        query_heads,
        key_heads,
        value_heads,
        to_heads(key_rot, seq_count),
        to_heads(value_low, seq_count),
        context,
        row_lse,
        hidden,
        active,
    )
    return (residual + branch_attn + branch_mlp, stored)


def layer_backward(upstream, weights, stored, query_pos, allowed):
    (
        gain_attn,
        shift_attn,
        gain_mlp,
        shift_mlp,
        w_qkv,
        b_qv,
        w_out,
        b_out,
        w_up,
        b_up,
        w_down,
        b_down,
    ) = weights
    (
        residual,
        normed_attn,
        normed_mlp,
        query_heads,
        key_heads,
        value_heads,
        local_keys,
        local_values,
        context,
        row_lse,
        hidden,
        active,
    ) = stored
    row_count, model_width = residual.shape
    seq_count = row_count // query_pos.shape[0]
    row_pos = jnp.tile(query_pos, seq_count)
    upstream_low = upstream.astype(jnp.bfloat16)
    branch_bias = jnp.sum(upstream_low.astype(jnp.float32), axis=0)
    grad_w_down = jnp.einsum("rf,rd->fd", active, upstream_low, preferred_element_type=jnp.float32)
    grad_active = jnp.einsum("rd,fd->rf", upstream_low, w_down, preferred_element_type=jnp.float32)
    gelu_pull = jax.vjp(partial(jax.nn.gelu, approximate=False), hidden)[1]
    grad_hidden = gelu_pull(grad_active)[0].astype(jnp.bfloat16)
    grad_b_up = jnp.sum(grad_hidden.astype(jnp.float32), axis=0)
    grad_w_up = jnp.einsum("rd,rf->df", normed_mlp, grad_hidden, preferred_element_type=jnp.float32)
    grad_normed_mlp = jnp.einsum("rf,df->rd", grad_hidden, w_up, preferred_element_type=jnp.float32)
    grad_w_out = jnp.einsum("re,rd->ed", context, upstream_low, preferred_element_type=jnp.float32)
    grad_context = jnp.einsum(
        "rd,ed->re", upstream_low, w_out, preferred_element_type=jnp.float32
    ).astype(jnp.bfloat16)
    grad_heads = to_heads(grad_context, seq_count)
    grad_query, grad_key, grad_value = lax.map(
        partial(query_rows, allowed=allowed, with_keys=True),
        (query_heads, key_heads, value_heads, grad_heads, row_lse),
    )
    key_sum, value_sum = (
        lax.psum_scatter(
            from_heads(grad_key).reshape(seq_count, 2, -1, model_width).astype(jnp.bfloat16),
            "ctx",
            scatter_dimension=2,
            tiled=True,
        ).astype(jnp.float32),
        lax.psum_scatter(
            from_heads(grad_value).reshape(seq_count, 2, -1, model_width).astype(jnp.bfloat16),
            "ctx",
            scatter_dimension=2,
            tiled=True,
        ).astype(jnp.float32),
    )
    key_grad = key_sum.reshape(row_count, HEADS, HEAD_DIM)
    value_grad = value_sum.reshape(row_count, model_width)
    query_rows_grad = grad_query.transpose(0, 2, 1, 3).reshape(row_count, HEADS, HEAD_DIM)
    rotate_pull = jax.vjp(
        partial(rotate, positions=row_pos), jnp.zeros((row_count, HEADS, HEAD_DIM), jnp.float32)
    )[1]
    query_back = rotate_pull(query_rows_grad)[0].reshape(row_count, model_width)
    key_back = rotate_pull(key_grad)[0].reshape(row_count, model_width)
    grad_mixed = jnp.concatenate([query_back, key_back, value_grad], axis=1).astype(jnp.bfloat16)
    mixed_sums = jnp.sum(grad_mixed.astype(jnp.float32), axis=0)
    grad_b_qv = jnp.concatenate([mixed_sums[:model_width], mixed_sums[2 * model_width :]])
    grad_w_qkv = jnp.einsum(
        "rd,rc->dc", normed_attn, grad_mixed, preferred_element_type=jnp.float32
    )
    grad_normed_attn = jnp.einsum(
        "rc,dc->rd", grad_mixed, w_qkv, preferred_element_type=jnp.float32
    )
    attn_pull = jax.vjp(
        normalize, residual, gain_attn.astype(jnp.float32), shift_attn.astype(jnp.float32)
    )[1]
    back_attn, grad_gain_attn, grad_shift_attn = attn_pull(grad_normed_attn)
    mlp_pull = jax.vjp(
        normalize, residual, gain_mlp.astype(jnp.float32), shift_mlp.astype(jnp.float32)
    )[1]
    back_mlp, grad_gain_mlp, grad_shift_mlp = mlp_pull(grad_normed_mlp)
    downstream = upstream + back_attn + back_mlp
    grads = (
        grad_gain_attn,
        grad_shift_attn,
        grad_gain_mlp,
        grad_shift_mlp,
        grad_w_qkv,
        grad_b_qv,
        grad_w_out,
        branch_bias,
        grad_w_up,
        grad_b_up,
        grad_w_down,
        branch_bias,
    )
    return (downstream, grads)


def local(
    tokens_in,
    cotangent,
    ln_gain_attn,
    ln_shift_attn,
    ln_gain_mlp,
    ln_shift_mlp,
    w_qkv,
    b_qv,
    w_out,
    b_out,
    w_up,
    b_up,
    w_down,
    b_down,
):
    stacked = (
        ln_gain_attn,
        ln_shift_attn,
        ln_gain_mlp,
        ln_shift_mlp,
        w_qkv,
        b_qv,
        w_out,
        b_out,
        w_up,
        b_up,
        w_down,
        b_down,
    )
    seq_here = tokens_in.shape[0]
    block_rows = tokens_in.shape[2]
    model_width = tokens_in.shape[3]
    row_count = seq_here * 2 * block_rows
    query_pos, key_pos = token_positions(block_rows)
    allowed = key_pos[None, :] <= query_pos[:, None]
    residual = tokens_in.reshape(row_count, model_width).astype(jnp.float32)
    keeping = []
    for layer_index in range(LAYERS):
        shards = tuple((param[layer_index] for param in stacked))
        weights = (
            lax.all_gather(shards[0], "wt", axis=0, tiled=True),
            lax.all_gather(shards[1], "wt", axis=0, tiled=True),
            lax.all_gather(shards[2], "wt", axis=0, tiled=True),
            lax.all_gather(shards[3], "wt", axis=0, tiled=True),
            lax.all_gather(shards[4], "wt", axis=0, tiled=True),
            lax.all_gather(shards[5], "wt", axis=0, tiled=True),
            lax.all_gather(shards[6], "wt", axis=0, tiled=True),
            lax.all_gather(shards[7], "wt", axis=0, tiled=True),
            lax.all_gather(shards[8], "wt", axis=0, tiled=True),
            lax.all_gather(shards[9], "wt", axis=0, tiled=True),
            lax.all_gather(shards[10], "wt", axis=0, tiled=True),
            lax.all_gather(shards[11], "wt", axis=0, tiled=True),
        )
        residual, stored = layer_forward(residual, weights, query_pos, allowed)
        keeping.append((shards, weights, stored))
    out_tokens = residual.astype(jnp.bfloat16).reshape(tokens_in.shape)
    upstream = cotangent.reshape(row_count, model_width).astype(jnp.float32)
    layer_totals = [None] * LAYERS
    for layer_index in reversed(range(LAYERS)):
        shards, weights, stored = keeping[layer_index]
        weights = (
            lax.all_gather(shards[0], "wt", axis=0, tiled=True),
            lax.all_gather(shards[1], "wt", axis=0, tiled=True),
            lax.all_gather(shards[2], "wt", axis=0, tiled=True),
            lax.all_gather(shards[3], "wt", axis=0, tiled=True),
            lax.all_gather(shards[4], "wt", axis=0, tiled=True),
            lax.all_gather(shards[5], "wt", axis=0, tiled=True),
            lax.all_gather(shards[6], "wt", axis=0, tiled=True),
            lax.all_gather(shards[7], "wt", axis=0, tiled=True),
            lax.all_gather(shards[8], "wt", axis=0, tiled=True),
            lax.all_gather(shards[9], "wt", axis=0, tiled=True),
            lax.all_gather(shards[10], "wt", axis=0, tiled=True),
            lax.all_gather(shards[11], "wt", axis=0, tiled=True),
        )
        upstream, grads = layer_backward(upstream, weights, stored, query_pos, allowed)
        shard_sums = (
            lax.psum_scatter(
                grads[0].astype(jnp.bfloat16), "wt", scatter_dimension=0, tiled=True
            ).astype(jnp.float32),
            lax.psum_scatter(
                grads[1].astype(jnp.bfloat16), "wt", scatter_dimension=0, tiled=True
            ).astype(jnp.float32),
            lax.psum_scatter(
                grads[2].astype(jnp.bfloat16), "wt", scatter_dimension=0, tiled=True
            ).astype(jnp.float32),
            lax.psum_scatter(
                grads[3].astype(jnp.bfloat16), "wt", scatter_dimension=0, tiled=True
            ).astype(jnp.float32),
            lax.psum_scatter(
                grads[4].astype(jnp.bfloat16), "wt", scatter_dimension=0, tiled=True
            ).astype(jnp.float32),
            lax.psum_scatter(
                grads[5].astype(jnp.bfloat16), "wt", scatter_dimension=0, tiled=True
            ).astype(jnp.float32),
            lax.psum_scatter(
                grads[6].astype(jnp.bfloat16), "wt", scatter_dimension=0, tiled=True
            ).astype(jnp.float32),
            lax.psum_scatter(
                grads[7].astype(jnp.bfloat16), "wt", scatter_dimension=0, tiled=True
            ).astype(jnp.float32),
            lax.psum_scatter(
                grads[8].astype(jnp.bfloat16), "wt", scatter_dimension=0, tiled=True
            ).astype(jnp.float32),
            lax.psum_scatter(
                grads[9].astype(jnp.bfloat16), "wt", scatter_dimension=0, tiled=True
            ).astype(jnp.float32),
            lax.psum_scatter(
                grads[10].astype(jnp.bfloat16), "wt", scatter_dimension=0, tiled=True
            ).astype(jnp.float32),
            lax.psum_scatter(
                grads[11].astype(jnp.bfloat16), "wt", scatter_dimension=0, tiled=True
            ).astype(jnp.float32),
        )
        layer_totals[layer_index] = (
            lax.psum(shard_sums[0].astype(jnp.bfloat16), "ctx").astype(jnp.float32),
            lax.psum(shard_sums[1].astype(jnp.bfloat16), "ctx").astype(jnp.float32),
            lax.psum(shard_sums[2].astype(jnp.bfloat16), "ctx").astype(jnp.float32),
            lax.psum(shard_sums[3].astype(jnp.bfloat16), "ctx").astype(jnp.float32),
            lax.psum(shard_sums[4].astype(jnp.bfloat16), "ctx").astype(jnp.float32),
            lax.psum(shard_sums[5].astype(jnp.bfloat16), "ctx").astype(jnp.float32),
            lax.psum(shard_sums[6].astype(jnp.bfloat16), "ctx").astype(jnp.float32),
            lax.psum(shard_sums[7].astype(jnp.bfloat16), "ctx").astype(jnp.float32),
            lax.psum(shard_sums[8].astype(jnp.bfloat16), "ctx").astype(jnp.float32),
            lax.psum(shard_sums[9].astype(jnp.bfloat16), "ctx").astype(jnp.float32),
            lax.psum(shard_sums[10].astype(jnp.bfloat16), "ctx").astype(jnp.float32),
            lax.psum(shard_sums[11].astype(jnp.bfloat16), "ctx").astype(jnp.float32),
        )
    grad_tokens = upstream.reshape(tokens_in.shape)
    stacked_grads = [
        jnp.stack([layer_totals[layer_index][member] for layer_index in range(LAYERS)])
        for member in range(12)
    ]
    return (
        out_tokens,
        grad_tokens,
        stacked_grads[0],
        stacked_grads[1],
        stacked_grads[2],
        stacked_grads[3],
        stacked_grads[4],
        stacked_grads[5],
        stacked_grads[6],
        stacked_grads[7],
        stacked_grads[8],
        stacked_grads[9],
        stacked_grads[10],
        stacked_grads[11],
    )


def solution(mesh):
    return jax.shard_map(
        local,
        mesh=mesh,
        in_specs=(
            P("wt", None, "ctx", None),
            P("wt", None, "ctx", None),
            P(None, "wt"),
            P(None, "wt"),
            P(None, "wt"),
            P(None, "wt"),
            P(None, "wt", None),
            P(None, "wt"),
            P(None, "wt", None),
            P(None, "wt"),
            P(None, "wt", None),
            P(None, "wt"),
            P(None, "wt", None),
            P(None, "wt"),
        ),
        out_specs=(
            P("wt", None, "ctx", None),
            P("wt", None, "ctx", None),
            P(None, "wt"),
            P(None, "wt"),
            P(None, "wt"),
            P(None, "wt"),
            P(None, "wt", None),
            P(None, "wt"),
            P(None, "wt", None),
            P(None, "wt"),
            P(None, "wt", None),
            P(None, "wt"),
            P(None, "wt", None),
            P(None, "wt"),
        ),
        check_vma=False,
    )
```

profile of v0, /device:TPU:1, one launch (start us, length us, event | category | flops | bytes accessed | tf_op | source)
XLA Modules:
  0.0 1610.9 jit_solution(3006835393650029133)
XLA Ops:
  79.1 33.2 %all-gather.49.cloned.1.call-done = bf16[1,768,3072]{2,1,0:T(8,128)(2,1)} async-done(((bf16[1,192,3072]{2,1,0:T(8,128)(2,1)}), bf16[1,768,3072]{2,1,0:T(8,128)(2,1)}) %all-gather.49.cloned.1.call-update) | async-done | bytes 4718608 | tf_op jit(solution)/shard_map/all_gather | solution.py:395
  120.5 47.1 %all-gather.51.cloned.1.call-done = bf16[1,3072,768]{2,1,0:T(8,128)(2,1)} async-done(((bf16[1,768,768]{2,1,0:T(8,128)(2,1)}), bf16[1,3072,768]{2,1,0:T(8,128)(2,1)}) %all-gather.51.cloned.1.call-update) | async-done | bytes 4718608 | tf_op jit(solution)/shard_map/all_gather | solution.py:397
  170.8 49.3 %all-gather.37.cloned.1.call-done = bf16[2,2,1024,768]{3,2,1,0:T(8,128)(2,1)} async-done(((bf16[2,2,32,768]{3,2,1,0:T(8,128)(2,1)}), bf16[2,2,1024,768]{3,2,1,0:T(8,128)(2,1)}) %all-gather.37.cloned.1.call-update) | async-done | bytes 6291472 | tf_op jit(solution)/shard_map/all_gather | solution.py:198
  247.5 22.7 %all-gather.39.cloned.1.call-done = bf16[2,2,1024,768]{3,2,1,0:T(8,128)(2,1)} async-done(((bf16[2,2,32,768]{3,2,1,0:T(8,128)(2,1)}), bf16[2,2,1024,768]{3,2,1,0:T(8,128)(2,1)}) %all-gather.39.cloned.1.call-update) | async-done | bytes 6291472 | tf_op jit(solution)/shard_map/all_gather | solution.py:201
  316.8 23.4 %all-gather.53.cloned.1.call-done = bf16[1,768,2304]{2,1,0:T(8,128)(2,1)} async-done(((bf16[1,192,2304]{2,1,0:T(8,128)(2,1)}), bf16[1,768,2304]{2,1,0:T(8,128)(2,1)}) %all-gather.53.cloned.1.call-update) | async-done | bytes 3538960 | tf_op jit(solution)/shard_map/all_gather | solution.py:391
  369.6 49.7 %all-gather.41.cloned.1.call-done = bf16[2,2,1024,768]{3,2,1,0:T(8,128)(2,1)} async-done(((bf16[2,2,32,768]{3,2,1,0:T(8,128)(2,1)}), bf16[2,2,1024,768]{3,2,1,0:T(8,128)(2,1)}) %all-gather.41.cloned.1.call-update) | async-done | bytes 6291472 | tf_op jit(solution)/shard_map/all_gather | solution.py:198
  446.8 23.3 %all-gather.43.cloned.1.call-done = bf16[2,2,1024,768]{3,2,1,0:T(8,128)(2,1)} async-done(((bf16[2,2,32,768]{3,2,1,0:T(8,128)(2,1)}), bf16[2,2,1024,768]{3,2,1,0:T(8,128)(2,1)}) %all-gather.43.cloned.1.call-update) | async-done | bytes 6291472 | tf_op jit(solution)/shard_map/all_gather | solution.py:201
  520.2 34.6 %while.58 = (s32[]{:T(128)}, f32[2,12,64,64]{3,2,1,0:T(8,128)S(1)}, bf16[2,12,2048,64]{2,3,1,0:T(8,128)(2,1)}, bf16[2,12,2048,64]{2,3,1,0:T(8,128)(2,1)}, pred[6...) while((s32[]{:T(128)}, f32[2,12,64,64]{3,2,1,0:T(8,128)S(1)}, ...), condition=%wide.region_19.20_spmd, body=%wide.region_16.19_spmd.sunk | while | flops 771194112 | bytes 177867056 | solution.py:285
  566.0 21.1 %copy.129 = bf16[2,2,1024,768]{3,1,0,2:T(2,128)(2,1)} copy(bf16[2,2,1024,768]{2,1,3,0:T(2,128)(2,1)} %convert_element_type.464) | data formatting | bytes 12582912 | tf_op jit(solution)/shard_map/convert_element_type | solution.py:297
  644.1 57.8 %all-reduce.52.cloned.1.call-done = bf16[2,2,1024,768]{3,1,0,2:T(2,128)(2,1)} async-done(((bf16[2,2,1024,768]{3,1,0,2:T(2,128)(2,1)}), bf16[2,2,1024,768]{3,1,0,2:T(2,128)(2,1)}) %all-reduce.52.cloned.1.call-update) | async-done | bytes 6291472
  703.2 86.5 %reduce-scatter.11.cloned.1.call-done = bf16[2,2,32,768]{3,2,1,0:T(8,128)(2,1)} async-done(((bf16[2,2,1024,768]{3,2,1,0:T(8,128)(2,1)}), bf16[2,2,32,768]{3,2,1,0:T(8,128)(2,1)}) %reduce-scatter.11.cloned.1.call-update) | async-done | bytes 196624 | tf_op jit(solution)/shard_map/reduce_scatter | solution.py:290
  813.6 34.0 %while.59 = (s32[]{:T(128)}, f32[2,12,64,64]{3,2,1,0:T(8,128)S(1)}, bf16[2,12,2048,64]{2,3,1,0:T(8,128)(2,1)}, bf16[2,12,2048,64]{2,3,1,0:T(8,128)(2,1)}, pred[6...) while((s32[]{:T(128)}, f32[2,12,64,64]{3,2,1,0:T(8,128)S(1)}, ...), condition=%wide.region_29.30_spmd, body=%wide.region_26.29_spmd.sunk | while | flops 771194112 | bytes 177867056 | solution.py:285
  858.7 21.1 %copy.140 = bf16[2,2,1024,768]{3,1,0,2:T(2,128)(2,1)} copy(bf16[2,2,1024,768]{2,1,3,0:T(2,128)(2,1)} %convert_element_type.473) | data formatting | bytes 12582912 | tf_op jit(solution)/shard_map/convert_element_type | solution.py:297
  939.6 57.1 %all-reduce.54.cloned.1.call-done = bf16[2,2,1024,768]{3,1,0,2:T(2,128)(2,1)} async-done(((bf16[2,2,1024,768]{3,1,0,2:T(2,128)(2,1)}), bf16[2,2,1024,768]{3,1,0,2:T(2,128)(2,1)}) %all-reduce.54.cloned.1.call-update) | async-done | bytes 6291472
  998.6 86.3 %reduce-scatter.13.cloned.1.call-done = bf16[2,2,32,768]{3,2,1,0:T(8,128)(2,1)} async-done(((bf16[2,2,1024,768]{3,2,1,0:T(8,128)(2,1)}), bf16[2,2,32,768]{3,2,1,0:T(8,128)(2,1)}) %reduce-scatter.13.cloned.1.call-update) | async-done | bytes 196624 | tf_op jit(solution)/shard_map/reduce_scatter | solution.py:290
  1104.1 36.0 %reduce-scatter.25.cloned.1.call-done = bf16[192,3072]{1,0:T(8,128)(2,1)} async-done(((bf16[768,3072]{1,0:T(8,128)(2,1)}), bf16[192,3072]{1,0:T(8,128)(2,1)}) %reduce-scatter.25.cloned.1.call-update) | async-done | bytes 1179664 | tf_op jit(solution)/shard_map/reduce_scatter | solution.py:447
  1140.1 53.2 %reduce-scatter.29.cloned.1.call-done = bf16[768,768]{1,0:T(8,128)(2,1)} async-done(((bf16[3072,768]{1,0:T(8,128)(2,1)}), bf16[768,768]{1,0:T(8,128)(2,1)}) %reduce-scatter.29.cloned.1.call-update) | async-done | bytes 1179664 | tf_op jit(solution)/shard_map/reduce_scatter | solution.py:453
  1193.3 25.8 %reduce-scatter.21.cloned.1.call-done = bf16[192,768]{1,0:T(8,128)(2,1)} async-done(((bf16[768,768]{1,0:T(8,128)(2,1)}), bf16[192,768]{1,0:T(8,128)(2,1)}) %reduce-scatter.21.cloned.1.call-update) | async-done | bytes 294928 | tf_op jit(solution)/shard_map/reduce_scatter | solution.py:441
  1219.1 26.1 %reduce-scatter.19.cloned.1.call-done = bf16[192,768]{1,0:T(8,128)(2,1)} async-done(((bf16[768,768]{1,0:T(8,128)(2,1)}), bf16[192,768]{1,0:T(8,128)(2,1)}) %reduce-scatter.19.cloned.1.call-update) | async-done | bytes 294928 | tf_op jit(solution)/shard_map/reduce_scatter | solution.py:441
  1245.3 45.4 %reduce-scatter.17.cloned.1.call-done = bf16[192,2304]{1,0:T(8,128)(2,1)} async-done(((bf16[768,2304]{1,0:T(8,128)(2,1)}), bf16[192,2304]{1,0:T(8,128)(2,1)}) %reduce-scatter.17.cloned.1.call-update) | async-done | bytes 884752 | tf_op jit(solution)/shard_map/reduce_scatter | solution.py:435
  1290.7 53.9 %reduce-scatter.23.cloned.1.call-done = bf16[192,3072]{1,0:T(8,128)(2,1)} async-done(((bf16[768,3072]{1,0:T(8,128)(2,1)}), bf16[192,3072]{1,0:T(8,128)(2,1)}) %reduce-scatter.23.cloned.1.call-update) | async-done | bytes 1179664 | tf_op jit(solution)/shard_map/reduce_scatter | solution.py:447
  1344.6 53.3 %reduce-scatter.27.cloned.1.call-done = bf16[768,768]{1,0:T(8,128)(2,1)} async-done(((bf16[3072,768]{1,0:T(8,128)(2,1)}), bf16[768,768]{1,0:T(8,128)(2,1)}) %reduce-scatter.27.cloned.1.call-update) | async-done | bytes 1179664 | tf_op jit(solution)/shard_map/reduce_scatter | solution.py:453
  1397.9 43.6 %reduce-scatter.15.cloned.1.call-done = bf16[192,2304]{1,0:T(8,128)(2,1)} async-done(((bf16[768,2304]{1,0:T(8,128)(2,1)}), bf16[192,2304]{1,0:T(8,128)(2,1)}) %reduce-scatter.15.cloned.1.call-update) | async-done | bytes 884752 | tf_op jit(solution)/shard_map/reduce_scatter | solution.py:435
  1460.1 123.8 %all-reduce.44 = (bf16[1,192]{1,0:T(2,128)(2,1)S(1)}, bf16[1,192]{1,0:T(2,128)(2,1)S(1)}, bf16[1,192]{1,0:T(2,128)(2,1)S(1)}, bf16[1,192]{1,0:T(2,128)(2,1)S(1)}...) all-reduce(bf16[1,192]{1,0:T(2,128)(2,1)S(1)} %stack.158, ...), channel_id=1, replica_groups=mesh['ctx'=32,'wt'=4] {'ctx'}, use_global_device_ids=true, to_apply=%region_41.42 | all-reduce | flops 4224 | bytes 16896 | tf_op jit(solution)/shard_map/psum | solution.py:461
  (744 shorter events, 581.0 us)
Async XLA Ops:
  10.2 102.1 %all-gather.49.cloned.1.call-start = ((), (), s32[]{:S(2)}) async-start(), calls=%async_computation.26 | async-start | bytes 5898240 | tf_op jit(solution)/shard_map/all_gather | solution.py:395
  11.9 155.7 %all-gather.51.cloned.1.call-start = ((), (), s32[]{:S(2)}) async-start(), calls=%async_computation.27 | async-start | bytes 5898240 | tf_op jit(solution)/shard_map/all_gather | solution.py:397
  15.2 204.8 %all-gather.37.cloned.1.call-start = ((), (), s32[]{:S(2)}) async-start(), calls=%async_computation.10 | async-start | bytes 6488064 | tf_op jit(solution)/shard_map/all_gather | solution.py:198
  62.5 207.7 %all-gather.39.cloned.1.call-start = ((), (), s32[]{:S(2)}) async-start(), calls=%async_computation.11 | async-start | bytes 6488064 | tf_op jit(solution)/shard_map/all_gather | solution.py:201
  64.0 250.7 %all-gather.47.cloned.1.call-start = ((), (), s32[]{:S(2)}) async-start(), calls=%async_computation.25 | async-start | bytes 1474560 | tf_op jit(solution)/shard_map/all_gather | solution.py:393
  65.0 275.2 %all-gather.53.cloned.1.call-start = ((), (), s32[]{:S(2)}) async-start(), calls=%async_computation.28 | async-start | bytes 4423680 | tf_op jit(solution)/shard_map/all_gather | solution.py:391
  65.7 299.9 %all-gather.55.cloned.1.call-start = ((), (), s32[]{:S(2)}) async-start(), calls=%async_computation.29 | async-start | bytes 1474560 | tf_op jit(solution)/shard_map/all_gather | solution.py:393
  66.5 352.8 %all-gather.41.cloned.1.call-start = ((), (), s32[]{:S(2)}) async-start(), calls=%async_computation.12 | async-start | bytes 6488064 | tf_op jit(solution)/shard_map/all_gather | solution.py:198
  344.9 125.2 %all-gather.43.cloned.1.call-start = ((), (), s32[]{:S(2)}) async-start(), calls=%async_computation.13 | async-start | bytes 6488064 | tf_op jit(solution)/shard_map/all_gather | solution.py:201
  346.4 280.5 %all-gather.57.cloned.1.call-start = ((), (), s32[]{:S(2)}) async-start(), calls=%async_computation.30 | async-start | bytes 5898240 | tf_op jit(solution)/shard_map/all_gather | solution.py:395
  347.2 288.7 %all-gather.59.cloned.1.call-start = ((), (), s32[]{:S(2)}) async-start(), calls=%async_computation.31 | async-start | bytes 5898240 | tf_op jit(solution)/shard_map/all_gather | solution.py:397
  347.8 354.2 %all-reduce.52.cloned.1.call-start = ((), (), s32[]{:S(2)}) async-start(), calls=%async_computation.32 | async-start | bytes 12582912
  587.2 202.5 %reduce-scatter.11.cloned.1.call-start = ((), (), s32[]{:S(2)}) async-start(), calls=%async_computation.14 | async-start | bytes 6488064 | tf_op jit(solution)/shard_map/reduce_scatter | solution.py:290
  614.7 381.9 %all-reduce.54.cloned.1.call-start = ((), (), s32[]{:S(2)}) async-start(), calls=%async_computation.33 | async-start | bytes 12582912
  879.8 205.1 %reduce-scatter.13.cloned.1.call-start = ((), (), s32[]{:S(2)}) async-start(), calls=%async_computation.15 | async-start | bytes 6488064 | tf_op jit(solution)/shard_map/reduce_scatter | solution.py:290
  907.4 232.8 %reduce-scatter.25.cloned.1.call-start = ((), (), s32[]{:S(2)}) async-start(), calls=%async_computation.21 | async-start | bytes 5898240 | tf_op jit(solution)/shard_map/reduce_scatter | solution.py:447
  912.2 281.1 %reduce-scatter.29.cloned.1.call-start = ((), (), s32[]{:S(2)}) async-start(), calls=%async_computation.23 | async-start | bytes 5898240 | tf_op jit(solution)/shard_map/reduce_scatter | solution.py:453
  917.0 302.1 %reduce-scatter.21.cloned.1.call-start = ((), (), s32[]{:S(2)}) async-start(), calls=%async_computation.19 | async-start | bytes 1474560 | tf_op jit(solution)/shard_map/reduce_scatter | solution.py:441
  920.3 324.9 %reduce-scatter.19.cloned.1.call-start = ((), (), s32[]{:S(2)}) async-start(), calls=%async_computation.18 | async-start | bytes 1474560 | tf_op jit(solution)/shard_map/reduce_scatter | solution.py:441
  921.9 368.8 %reduce-scatter.17.cloned.1.call-start = ((), (), s32[]{:S(2)}) async-start(), calls=%async_computation.17 | async-start | bytes 4423680 | tf_op jit(solution)/shard_map/reduce_scatter | solution.py:435
  925.1 419.5 %reduce-scatter.23.cloned.1.call-start = ((), (), s32[]{:S(2)}) async-start(), calls=%async_computation.20 | async-start | bytes 5898240 | tf_op jit(solution)/shard_map/reduce_scatter | solution.py:447
  933.9 464.0 %reduce-scatter.27.cloned.1.call-start = ((), (), s32[]{:S(2)}) async-start(), calls=%async_computation.22 | async-start | bytes 5898240 | tf_op jit(solution)/shard_map/reduce_scatter | solution.py:453
  938.5 503.0 %reduce-scatter.15.cloned.1.call-start = ((), (), s32[]{:S(2)}) async-start(), calls=%async_computation.16 | async-start | bytes 4423680 | tf_op jit(solution)/shard_map/reduce_scatter | solution.py:435
  1096.6 496.4 %all-reduce.56.cloned.1.call-start = ((), (), s32[]{:S(2)}) async-start(), calls=%async_computation.34 | async-start | bytes 14155776 | tf_op jit(solution)/shard_map/psum | solution.py:465
  (144 other events, 2210.7 us)
Sparse Core Ops, SparseCore 0:
  10.3 46.9 all-gather.44
  59.5 52.6 all-gather.48
  114.5 53.0 all-gather.50
  170.3 49.6 all-gather.36
  222.2 47.9 all-gather.38
  295.7 44.4 all-gather.52
  341.8 23.7 all-gather.54
  368.5 50.7 all-gather.40
  422.0 47.9 all-gather.42
  472.3 51.4 all-gather.56
  525.3 53.0 all-gather.58
  587.3 114.5 all-reduce.51
  705.5 84.0 reduce-scatter.10
  879.9 116.6 all-reduce.53
  1000.7 84.1 reduce-scatter.12
  1087.7 52.3 reduce-scatter.24
  1142.4 50.8 reduce-scatter.28
  1196.3 22.7 reduce-scatter.20
  1221.4 23.8 reduce-scatter.18
  1248.3 42.3 reduce-scatter.16
  1293.7 50.8 reduce-scatter.22
  1347.0 50.8 reduce-scatter.26
  1400.2 41.2 reduce-scatter.14
  1445.7 118.5 all-reduce.55
  (1 shorter events, 22.2 us)
where the time goes:
time: 1630 us; the launch traced here: 1610 us
  waiting for transfers between devices  894 us (55%)
  local copies, waits for them, and re-layouts  347 us (21%)
  blocking collectives  192 us (12%)
  matrix products  126 us (8%)
  other arithmetic  28.4 us (2%)
  between operations  20.2 us (1%)
    reduce_scatter x2, waiting for transfers between devices, layer_backward(): lax.psum_scatter(from_heads(grad_key).reshape(seq_count, 2, -1, model_wid...  173 us
    psum x1, blocking collectives, local(): lax.psum(shard_sums[0].astype(jnp.bfloat16), 'ctx').astype(jnp.float32)  124 us
    unnamed x27, waiting for transfers between devices  118 us
    reduce_scatter x2, waiting for transfers between devices, local(): lax.psum_scatter(grads[10].astype(jnp.bfloat16), 'wt', scatter_dimension=...  107 us
    all_gather x2, waiting for transfers between devices, layer_forward(): lax.all_gather(key_rot.reshape(seq_count, 2, block_rows, model_width), 'c...  99 us
    reduce_scatter x2, waiting for transfers between devices, local(): lax.psum_scatter(grads[8].astype(jnp.bfloat16), 'wt', scatter_dimension=0...  89.9 us
    reduce_scatter x2, waiting for transfers between devices, local(): lax.psum_scatter(grads[4].astype(jnp.bfloat16), 'wt', scatter_dimension=0...  89 us
    convert_element_type x4, local copies, waits for them, and re-layouts, layer_backward(): from_heads(grad_value).reshape(seq_count, 2, -1, model_width)  64.5 us
  transfers between devices with their start and end apart: 25, of which 20 were waited for; matrix products, arithmetic and copies ran while one was open for 24% of the time, Pallas kernels for 0%

commit v1 on v0

v1 whole, which is shorter than its diff:
```python
import jax
import jax.numpy as jnp
from jax import lax
from jax.experimental import pallas as pl
from jax.experimental.pallas import tpu as pltpu
from jax.sharding import PartitionSpec as P

HEADS = 12
HEAD_DIM = 64
ROT = 16
LAYERS = 2
BLK = 32
EPS = 1e-05

F32 = jnp.float32
BF16 = jnp.bfloat16
NT = (((1,), (1,)), ((), ()))
NN = (((1,), (0,)), ((), ()))
TILE = 512


def dot(left, right, dims=NN):
    return lax.dot_general(left, right, dims, preferred_element_type=F32)


def exchange(chunks, axis):
    return lax.all_to_all(chunks, axis, 0, 0, tiled=True)


def spread(value, axis):
    count = lax.axis_size(axis)
    return exchange(jnp.broadcast_to(value[None], (count,) + value.shape), axis)


def tile_list(size):
    tiles = []
    for start in range(0, size, TILE):
        keys = [(0, k, k == start) for k in range(0, start + TILE, TILE)]
        tiles.append((0, start, keys))
    for start in range(0, size, TILE):
        keys = [(0, k, False) for k in range(0, size, TILE)]
        keys += [(1, k, k == start) for k in range(start, size, TILE)]
        tiles.append((1, start, keys))
    return tiles


def tile_mask(half):
    row = lax.broadcasted_iota(jnp.int32, (TILE, TILE), 0)
    col = lax.broadcasted_iota(jnp.int32, (TILE, TILE), 1)
    if half:
        shift = BLK.bit_length() - 1
        row_pos = (row & (BLK - 1)) - ((row >> shift) << shift)
        col_pos = (col & (BLK - 1)) - ((col >> shift) << shift)
        return row_pos <= col_pos
    return row <= col


def forward_kernel(in_ref, out_ref, full_ref, lse_ref, q_scr, k_scr, vt_scr):
    count = in_ref.shape[0]
    size = count * BLK
    for half in range(2):
        both = in_ref[:, half * BLK : (half + 1) * BLK, :].reshape(size, 128)
        q_scr[half] = both[:, :64] * jnp.asarray(HEAD_DIM ** -0.5, BF16)
        k_scr[half] = both[:, 64:]
    values = in_ref[:, 2 * BLK : 3 * BLK, :].reshape(size, 128)
    vt_scr[...] = values.astype(F32).T.astype(BF16)
    for half, start, keys in tile_list(size):
        query = q_scr[half, start : start + TILE, :]
        top = jnp.full((1, TILE), -1e30, F32)
        total = jnp.zeros((1, TILE), F32)
        acc = jnp.zeros((64, TILE), F32)
        for key_half, key_start, masked in keys:
            key = k_scr[key_half, key_start : key_start + TILE, :]
            scores = dot(key, query, NT)
            if masked:
                scores = jnp.where(tile_mask(half), scores, -1e30)
            new_top = jnp.maximum(top, jnp.max(scores, axis=0, keepdims=True))
            raised = jnp.exp(scores - new_top)
            keep = jnp.exp(top - new_top)
            total = total * keep + jnp.sum(raised, axis=0, keepdims=True)
            value = vt_scr[key_half * 64 : (key_half + 1) * 64, key_start : key_start + TILE]
            acc = acc * keep + dot(value, raised.astype(BF16))
            top = new_top
        full_ref[half * 64 : (half + 1) * 64, start : start + TILE] = acc / total
        lse_ref[half : half + 1, start : start + TILE] = top + jnp.log(total)
    out_ref[...] = full_ref[...].T.astype(BF16).reshape(count, BLK, 128)


def backward_kernel(in_ref, grad_ref, full_ref, lse_ref, out_ref, q_scr, k_scr, kt_scr, v_scr, do_scr, delta_scr, dq_scr, dk_scr, dv_scr):
    count = in_ref.shape[0]
    size = count * BLK
    grads = grad_ref[...].reshape(size, 128)
    grads_t = grads.astype(F32).T
    product = grads_t * full_ref[...]
    values = in_ref[:, 2 * BLK : 3 * BLK, :].reshape(size, 128)
    for half in range(2):
        both = in_ref[:, half * BLK : (half + 1) * BLK, :].reshape(size, 128)
        q_scr[half] = both[:, :64] * jnp.asarray(HEAD_DIM ** -0.5, BF16)
        k_scr[half] = both[:, 64:]
        kt_scr[half] = both.astype(F32).T[64:, :].astype(BF16)
        lanes = slice(half * 64, (half + 1) * 64)
        v_scr[half] = values[:, lanes]
        do_scr[half] = grads[:, lanes]
        delta_scr[half : half + 1, :] = jnp.sum(product[lanes, :], axis=0, keepdims=True)
    dk_scr[...] = jnp.zeros_like(dk_scr)
    dv_scr[...] = jnp.zeros_like(dv_scr)
    for half, start, keys in tile_list(size):
        rows = slice(start, start + TILE)
        query = q_scr[half, rows, :]
        grad = do_scr[half, rows, :]
        lse = lse_ref[half : half + 1, rows]
        delta = delta_scr[half : half + 1, rows]
        acc = jnp.zeros((64, TILE), F32)
        for key_half, key_start, masked in keys:
            key_rows = slice(key_start, key_start + TILE)
            scores = dot(k_scr[key_half, key_rows, :], query, NT)
            if masked:
                scores = jnp.where(tile_mask(half), scores, -1e30)
            probs = jnp.exp(scores - lse)
            grad_probs = dot(v_scr[key_half, key_rows, :], grad, NT)
            grad_scores = (probs * (grad_probs - delta)).astype(BF16)
            dv_scr[key_half, key_rows, :] += dot(probs.astype(BF16), grad)
            dk_scr[key_half, key_rows, :] += dot(grad_scores, query)
            acc += dot(kt_scr[key_half, :, key_rows], grad_scores)
        dq_scr[half * 64 : (half + 1) * 64, rows] = acc * (HEAD_DIM ** -0.5)
    queries = dq_scr[...].T
    for half in range(2):
        both = jnp.concatenate([queries[:, half * 64 : (half + 1) * 64], dk_scr[half]], axis=1)
        out_ref[:, half * BLK : (half + 1) * BLK, :] = both.astype(BF16).reshape(count, BLK, 128)
    both = jnp.concatenate([dv_scr[0], dv_scr[1]], axis=1)
    out_ref[:, 2 * BLK : 3 * BLK, :] = both.astype(BF16).reshape(count, BLK, 128)


def attend(packed):
    count = packed.shape[0]
    size = count * BLK
    return pl.pallas_call(
        forward_kernel,
        out_shape=(
            jax.ShapeDtypeStruct((count, BLK, 128), BF16),
            jax.ShapeDtypeStruct((128, size), F32),
            jax.ShapeDtypeStruct((8, size), F32),
        ),
        in_specs=[pl.BlockSpec(memory_space=pltpu.VMEM)],
        out_specs=[pl.BlockSpec(memory_space=pltpu.VMEM)] * 3,
        scratch_shapes=[
            pltpu.VMEM((2, size, 64), BF16),
            pltpu.VMEM((2, size, 64), BF16),
            pltpu.VMEM((128, size), BF16),
        ],
        compiler_params=pltpu.CompilerParams(vmem_limit_bytes=48 << 20),
        cost_estimate=pl.CostEstimate(flops=20_000_000_000, bytes_accessed=20_000_000, transcendentals=2_600_000),
        name="attend",
    )(packed)


def attend_back(packed, grads, full, lse):
    count = packed.shape[0]
    size = count * BLK
    return pl.pallas_call(
        backward_kernel,
        out_shape=jax.ShapeDtypeStruct((count, 3 * BLK, 128), BF16),
        in_specs=[pl.BlockSpec(memory_space=pltpu.VMEM)] * 4,
        out_specs=pl.BlockSpec(memory_space=pltpu.VMEM),
        scratch_shapes=[
            pltpu.VMEM((2, size, 64), BF16),
            pltpu.VMEM((2, size, 64), BF16),
            pltpu.VMEM((2, 64, size), BF16),
            pltpu.VMEM((2, size, 64), BF16),
            pltpu.VMEM((2, size, 64), BF16),
            pltpu.VMEM((8, size), F32),
            pltpu.VMEM((128, size), F32),
            pltpu.VMEM((2, size, 64), F32),
            pltpu.VMEM((2, size, 64), F32),
        ],
        compiler_params=pltpu.CompilerParams(vmem_limit_bytes=48 << 20),
        cost_estimate=pl.CostEstimate(flops=40_000_000_000, bytes_accessed=40_000_000, transcendentals=2_600_000),
        name="attend_back",
    )(packed, grads, full, lse)


def pack_rows(value, seqs):
    split = value.reshape(seqs, 2, BLK, HEADS, HEAD_DIM).transpose(0, 3, 2, 1, 4)
    return split.reshape(seqs * HEADS, BLK, 2 * HEAD_DIM)


def unpack_rows(tiles, seqs):
    split = tiles.reshape(seqs, HEADS, BLK, 2, HEAD_DIM).transpose(0, 3, 2, 1, 4)
    return split.reshape(seqs * 2 * BLK, HEADS * HEAD_DIM)


def pad_pairs(tiles):
    missing = lax.axis_size("ctx") - tiles.shape[0]
    return jnp.pad(tiles, ((0, missing), (0, 0), (0, 0)))


def pack_mixed(query, key, value, seqs):
    pair = jnp.concatenate(
        [query.reshape(seqs, 2 * BLK, HEADS, HEAD_DIM), key.reshape(seqs, 2 * BLK, HEADS, HEAD_DIM)], axis=-1
    )
    pair = pair.transpose(0, 2, 1, 3).reshape(seqs * HEADS, 2 * BLK, 2 * HEAD_DIM)
    return pad_pairs(jnp.concatenate([pair, pack_rows(value, seqs)], axis=1))


def unpack_mixed(tiles, seqs):
    pair = tiles[: seqs * HEADS, : 2 * BLK].reshape(seqs, HEADS, 2 * BLK, 2, HEAD_DIM)
    pair = pair.transpose(3, 0, 2, 1, 4).reshape(2, seqs * 2 * BLK, HEADS * HEAD_DIM)
    return pair[0], pair[1], unpack_rows(tiles[: seqs * HEADS, 2 * BLK :], seqs)


def rotary_tables(seqs):
    device = lax.axis_index("ctx")
    devices = lax.axis_size("ctx")
    offsets = jnp.arange(BLK, dtype=jnp.int32)
    early = device * BLK + offsets
    late = 2 * BLK * devices - (device + 1) * BLK + offsets
    positions = jnp.tile(jnp.concatenate([early, late]), seqs).astype(F32)
    half = ROT // 2
    frequency = 10000.0 ** (-jnp.arange(half, dtype=F32) * 2.0 / ROT)
    angles = positions[:, None] * frequency[None, :]
    cosine, sine = lax.optimization_barrier((jnp.cos(angles), jnp.sin(angles)))
    rows = positions.shape[0]
    zero = jnp.zeros((rows, half), F32)
    rest = HEAD_DIM - ROT

    def whole(first, second, fill):
        return jnp.tile(jnp.concatenate([first, second, jnp.full((rows, rest), fill, F32)], axis=1), (1, HEADS))

    tables = (whole(cosine, cosine, 1.0), whole(zero, sine, 0.0), whole(sine, zero, 0.0))
    return lax.optimization_barrier(tables)


def turn(value, tables, sign):
    cosine, up, down = tables
    half = ROT // 2
    return value * cosine + sign * (jnp.roll(value, half, 1) * up - jnp.roll(value, -half, 1) * down)


def standardize(values):
    centred = values - jnp.mean(values, axis=-1, keepdims=True)
    scale = lax.rsqrt(jnp.mean(centred * centred, axis=-1, keepdims=True) + EPS)
    return centred * scale, scale


def cdf(value):
    return 0.5 * (1.0 + lax.erf(value * (0.5 ** 0.5)))


def layer_forward(x, w, tables, seqs):
    xhat, scale = standardize(x)
    xhat_low = xhat.astype(BF16)
    xhat_all = spread(xhat_low, "wt").reshape(-1, x.shape[1])
    n_attn = (xhat * w["g_attn"] + w["s_attn"]).astype(BF16)
    mixed = dot(n_attn, w["qkv"])
    width = x.shape[1]
    query = turn(mixed[:, :width] + w["b_q"], tables, 1.0).astype(BF16)
    key = turn(mixed[:, width : 2 * width], tables, 1.0).astype(BF16)
    value = (mixed[:, 2 * width :] + w["b_v"]).astype(BF16)
    packed = exchange(pack_mixed(query, key, value, seqs), "ctx")
    out, full, lse = attend(packed)
    context = unpack_rows(exchange(out, "ctx")[: seqs * HEADS], seqs)
    n_mlp_all = (xhat_all.astype(F32) * w["g_mlp"] + w["s_mlp"]).astype(BF16)
    hidden = dot(n_mlp_all, w["up"]) + w["b_up"]
    active = (hidden * cdf(hidden)).astype(BF16)
    partial = dot(active, w["down"]).astype(BF16)
    mlp = exchange(partial.reshape(-1, *x.shape), "wt").astype(F32).sum(0)
    branch = dot(context, w["out"]) + w["b_out"]
    group = lax.axis_size("wt")
    context_all = exchange(context.reshape(x.shape[0], group, -1).transpose(1, 0, 2), "wt")
    stored = (xhat, scale, xhat_all, n_mlp_all, packed, full, lse, context_all, hidden, active)
    return x + branch + (mlp + w["b_down"]), stored


def layer_backward(g, w, stored, tables, seqs):
    xhat, scale, xhat_all, n_mlp_all, packed, full, lse, context_all, hidden, active = stored
    rows, width = g.shape
    group = lax.axis_size("wt")
    g_low = g.astype(BF16)
    g_all = spread(g_low, "wt").reshape(-1, width)
    grad_context = dot(g_low, w["out"], NT).astype(BF16)
    grads = exchange(pad_pairs(pack_rows(grad_context, seqs)), "ctx")
    grad_active = dot(g_all, w["down"], NT)
    density = jnp.exp(-0.5 * hidden * hidden) * 0.3989422804014327
    grad_hidden = (grad_active * (cdf(hidden) + hidden * density)).astype(BF16)
    partial = dot(grad_hidden, w["up"], NT).astype(BF16)
    grad_n_mlp = exchange(partial.reshape(-1, rows, width), "wt").astype(F32).sum(0)
    tn = (((0,), (0,)), ((), ()))
    grad_down = dot(active, g_all, tn).astype(BF16)
    grad_out = dot(context_all.transpose(2, 0, 1).reshape(width // group, -1), g_all).astype(BF16)
    grad_up = dot(n_mlp_all, grad_hidden, tn).astype(BF16)
    grad_b_up = jnp.sum(grad_hidden.astype(F32), axis=0)
    grad_up = exchange(grad_up.reshape(group, width // group, -1), "wt").reshape(width, -1)
    sums = jnp.concatenate([grad_down, grad_up, grad_out], axis=0)
    pieces = exchange(sums.reshape(lax.axis_size("ctx"), -1, width), "ctx")
    wide = spread(pieces.astype(F32).sum(0).astype(BF16), "ctx").reshape(-1, width)
    back = exchange(attend_back(packed, grads, full, lse), "ctx")
    grad_q, grad_k, grad_v = unpack_mixed(back, seqs)
    grad_q = turn(grad_q.astype(F32), tables, -1.0).astype(BF16)
    grad_k = turn(grad_k.astype(F32), tables, -1.0).astype(BF16)
    grad_mixed = jnp.concatenate([grad_q, grad_k, grad_v], axis=1)
    grad_n_attn = dot(grad_mixed, w["qkv"], NT)
    mixed_all = exchange(grad_mixed.reshape(rows, group, -1).transpose(1, 0, 2), "wt").reshape(group * rows, -1)
    n_attn_all = (xhat_all.astype(F32) * w["g_attn"] + w["s_attn"]).astype(BF16)
    grad_qkv = dot(n_attn_all, mixed_all, tn).astype(BF16).reshape(group, width // group, -1)
    pull = grad_n_attn * w["g_attn"] + grad_n_mlp * w["g_mlp"]
    inner = pull - jnp.mean(pull, axis=-1, keepdims=True) - xhat * jnp.mean(pull * xhat, axis=-1, keepdims=True)
    small = jnp.stack(
        [
            jnp.sum(grad_n_attn * xhat, axis=0),
            jnp.sum(grad_n_attn, axis=0),
            jnp.sum(grad_n_mlp * xhat, axis=0),
            jnp.sum(grad_n_mlp, axis=0),
            jnp.sum(g_low.astype(F32), axis=0),
        ]
    )
    bias = jnp.concatenate([jnp.sum(grad_q.astype(F32), axis=0), jnp.sum(grad_v.astype(F32), axis=0)])
    small = small.reshape(5, group, -1).transpose(1, 0, 2).reshape(group, -1)
    small = jnp.concatenate([small, bias.reshape(group, -1)], axis=1)
    return g + scale * inner, wide, grad_qkv, small, grad_b_up


def gather_small(stacked):
    names = ("g_attn", "s_attn", "g_mlp", "s_mlp", "b_qv", "b_out", "b_down")
    flat = jnp.concatenate([stacked[name] for name in names], axis=1)
    every = lax.all_gather(flat, "wt", axis=0).astype(F32)
    found, at = {}, 0
    for name in names:
        size = stacked[name].shape[1]
        found[name] = every[:, :, at : at + size].transpose(1, 0, 2).reshape(LAYERS, -1)
        at += size
    return found


def local(tokens_in, cotangent, ln_gain_attn, ln_shift_attn, ln_gain_mlp, ln_shift_mlp, w_qkv, b_qv, w_out, b_out, w_up, b_up, w_down, b_down):
    seqs = tokens_in.shape[0]
    width = tokens_in.shape[3]
    rows = seqs * 2 * BLK
    group = lax.axis_size("wt")
    devices = lax.axis_size("ctx")
    tables = rotary_tables(seqs)
    small = gather_small(
        {"g_attn": ln_gain_attn, "s_attn": ln_shift_attn, "g_mlp": ln_gain_mlp, "s_mlp": ln_shift_mlp, "b_qv": b_qv, "b_out": b_out, "b_down": b_down}
    )
    layers = []
    for layer in range(LAYERS):
        up = w_up[layer].reshape(width // group, group, -1).transpose(1, 0, 2)
        w = {name: small[name][layer][None] for name in small}
        w["b_q"] = w["b_qv"][:, :width]
        w["b_v"] = w["b_qv"][:, width:]
        w["qkv"] = lax.all_gather(w_qkv[layer], "wt", axis=0, tiled=True)
        w["out"] = lax.all_gather(w_out[layer], "wt", axis=0, tiled=True)
        w["up"] = exchange(up, "wt").reshape(width, -1)
        w["down"] = w_down[layer]
        w["b_up"] = b_up[layer].astype(F32)[None]
        layers.append(w)
    x = tokens_in.reshape(rows, width).astype(F32)
    kept = []
    for w in layers:
        x, stored = layer_forward(x, w, tables, seqs)
        kept.append(stored)
    out_tokens = x.astype(BF16).reshape(tokens_in.shape)
    g = cotangent.reshape(rows, width).astype(F32)
    wides, qkvs, smalls, ups = ([None] * LAYERS for _ in range(4))
    for layer in reversed(range(LAYERS)):
        g, wides[layer], qkvs[layer], smalls[layer], ups[layer] = layer_backward(g, layers[layer], kept[layer], tables, seqs)
    columns = qkvs[0].shape[2]
    depth = width // group
    piece = width // devices

    def to_rows(value):
        size = value.shape[-1]
        lines = -(-size // columns)
        lines = -(-lines // 8) * 8
        padded = jnp.pad(value, ((0, 0), (0, lines * columns - size)))
        return padded.reshape(value.shape[0], lines, columns)

    totals = [None] * LAYERS
    for layer in reversed(range(1, LAYERS)):
        moved = exchange(qkvs[layer], "wt")
        part = exchange(moved.reshape(devices, piece, columns), "ctx").astype(F32).sum(0).astype(BF16)
        totals[layer] = spread(part, "ctx").reshape(group, depth, columns)
    tiny = to_rows(jnp.concatenate(smalls, axis=1).astype(BF16))
    moved = exchange(jnp.concatenate([qkvs[0], tiny], axis=1), "wt")
    small_sum = moved[:, depth:].astype(F32).sum(0).reshape(1, -1)[:, : sum(s.shape[1] for s in smalls)]
    tail = to_rows(jnp.concatenate([small_sum, *(u[None] for u in ups)], axis=1).astype(BF16))
    sent = jnp.concatenate(
        [moved[:, :depth].reshape(devices, piece, columns), jnp.broadcast_to(tail, (devices,) + tail.shape[1:])], axis=1
    )
    landed = exchange(sent, "ctx").astype(F32).sum(0)
    totals[0] = spread(landed[:piece].astype(BF16), "ctx").reshape(group, depth, columns)
    flat = landed[piece:].reshape(-1)
    tiny_size = smalls[0].shape[1]
    per_layer = [flat[layer * tiny_size : (layer + 1) * tiny_size] for layer in range(LAYERS)]
    at = LAYERS * tiny_size
    unit = ups[0].shape[0]
    grad_b_up = flat[at : at + LAYERS * unit].reshape(LAYERS, unit)

    def vector(index):
        return jnp.stack([v[index * depth : (index + 1) * depth] for v in per_layer])

    grad_bias = vector(4)
    grad_b_qv = jnp.stack([v[5 * depth :] for v in per_layer])
    grad_qkv = jnp.stack([t.astype(F32).transpose(1, 0, 2).reshape(depth, -1) for t in totals])
    grad_down = jnp.stack([v[:unit].astype(F32) for v in wides])
    grad_up = jnp.stack(
        [v[unit : unit + width].astype(F32).reshape(group, depth, unit).transpose(1, 0, 2).reshape(depth, -1) for v in wides]
    )
    grad_out = jnp.stack([v[unit + width :].astype(F32) for v in wides])
    return (
        out_tokens,
        g.reshape(tokens_in.shape),
        vector(0),
        vector(1),
        vector(2),
        vector(3),
        grad_qkv,
        grad_b_qv,
        grad_out,
        grad_bias,
        grad_up,
        grad_b_up,
        grad_down,
        grad_bias,
    )


def solution(mesh):
    tokens = P("wt", None, "ctx", None)
    vec, mat = P(None, "wt"), P(None, "wt", None)
    params = (vec, vec, vec, vec, mat, vec, mat, vec, mat, vec, mat, vec)
    return jax.shard_map(
        local,
        mesh=mesh,
        in_specs=(tokens, tokens) + params,
        out_specs=(tokens, tokens) + params,
        check_vma=False,
    )
```

time: 1630 us -> 832 us (0.51)
  waiting for transfers between devices: 894 us -> 329 us
  local copies, waits for them, and re-layouts: 347 us -> 140 us
  blocking collectives: 192 us -> 11.1 us
  starting transfers between devices: 1.2 us -> 168 us
  matrix products: 126 us -> 61.2 us
  other arithmetic: 28.4 us -> 65.1 us
  Pallas kernels: 0 us -> 29.5 us
    reduce_scatter x10 -> x0, waiting for transfers between devices: 510 us -> none  [the longest x2 173 us: layer_backward(): lax.psum_scatter(from_heads(grad_key).reshape(seq_count, 2, -1, model_wid...]
    all_to_all x0 -> x34, waiting for transfers between devices: none -> 298 us  [exchange(): return lax.all_to_all(chunks, axis, 0, 0, tiled=True)]
    all_gather x12 -> x4, waiting for transfers between devices: 266 us -> 29.4 us  [the longest x2 29.4 us: local(): w['qkv'] = lax.all_gather(w_qkv[layer], 'wt', axis=0, tiled=True)]
    all_to_all x0 -> x34, starting transfers between devices: none -> 168 us  [exchange(): return lax.all_to_all(chunks, axis, 0, 0, tiled=True)]
    psum x1 -> x0, blocking collectives: 124 us -> none  [local(): lax.psum(shard_sums[0].astype(jnp.bfloat16), 'ctx').astype(jnp.float32)]
    convert_element_type x19 -> x11, local copies, waits for them, and re-layouts: 125 us -> 8.5 us  [the longest x2 3.75 us: layer_backward(): dot(n_attn_all, mixed_all, tn).astype(BF16)]
    unnamed x27 -> x4, waiting for transfers between devices: 118 us -> 1.27 us
    all_gather x4 -> x0, local copies, waits for them, and re-layouts: 65.6 us -> none  [the longest x2 32.9 us: layer_forward(): lax.all_gather(value_low.reshape(seq_count, 2, block_rows, model_width),...]
  transfers between devices with their start and end apart: 25 -> 38, of which waited for: 20 -> 32; matrix products, arithmetic and copies ran while one was open for 24% -> 29% of each run, Pallas kernels for 0% -> 4%
where the time goes in v1:
time: 832 us; the launch traced here: 820 us
  waiting for transfers between devices  329 us (40%)
  starting transfers between devices  168 us (20%)
  local copies, waits for them, and re-layouts  140 us (17%)
  other arithmetic  65.1 us (8%)
  matrix products  61.2 us (7%)
  Pallas kernels  29.5 us (4%)
  between operations  16.1 us (2%)
  blocking collectives  11.1 us (1%)
    all_to_all x34, waiting for transfers between devices, exchange(): return lax.all_to_all(chunks, axis, 0, 0, tiled=True)  298 us
    all_to_all x34, starting transfers between devices, exchange(): return lax.all_to_all(chunks, axis, 0, 0, tiled=True)  168 us
    dot_general x24, matrix products, dot(): return lax.dot_general(left, right, dims, preferred_element_type=F32)  61.2 us
    all_gather x2, waiting for transfers between devices, local(): w['qkv'] = lax.all_gather(w_qkv[layer], 'wt', axis=0, tiled=True)  29.4 us
    pallas_call x2, Pallas kernels, attend_back(): pl.pallas_call(backward_kernel, out_shape=jax.ShapeDtypeStruct((count, 3...  18.2 us
  transfers between devices with their start and end apart: 38, of which 32 were waited for; matrix products, arithmetic and copies ran while one was open for 29% of the time, Pallas kernels for 4%

profile of v1, /device:TPU:1, one launch (start us, length us, event | category | flops | bytes accessed | tf_op | source)
XLA Modules:
  0.0 820.0 jit_solution(10862403481354040203)
XLA Ops:
  12.0 11.1 %all-gather.5 = bf16[4,2,1536]{2,1,0:T(2,128)(2,1)S(1)} all-gather(bf16[1,2,1536]{2,1,0:T(2,128)(2,1)S(1)} %bitcast.305), channel_id=2, replica_groups=mesh['ctx'=32,'wt'=4] {'wt'}, dimensions={0}, use_global_device_ids=true | all-gather | bytes 30720 | tf_op jit(solution)/shard_map/all_gather | solution.py:325
  40.6 9.4 %all-to-all-done.2 = bf16[4,128,768]{2,1,0:T(8,128)(2,1)S(1)} async-done(((bf16[4,128,768]{2,1,0:T(8,128)(2,1)}), bf16[4,128,768]{2,1,0:T(8,128)(2,1)S(1)}, u32[]{:S(2)}, u32[]{:S(2)}) %all-to-all-start.2) | async-done | bytes 786464 | tf_op jit(solution)/shard_map/all_to_all | solution.py:27
  57.1 19.0 %all-to-all-done.3 = bf16[4,192,768]{2,1,0:T(8,128)(2,1)} async-done(((bf16[4,192,768]{2,1,0:T(8,128)(2,1)}), bf16[4,192,768]{2,1,0:T(8,128)(2,1)}, u32[]{:S(2)}, u32[]{:S(2)}) %all-to-all-start.3) | async-done | bytes 1179680 | tf_op jit(solution)/shard_map/all_to_all | solution.py:27
  95.4 8.0 all-to-all-done.4
  104.2 8.4 %all-to-all-start = ((bf16[32,96,128]{2,1,0:T(8,128)(2,1)}), bf16[32,96,128]{2,1,0:T(8,128)(2,1)S(1)}, u32[]{:S(2)}, u32[]{:S(2)}) async-start(bf16[32,96,128]{2,1,0:T(8,128)(2,1)} %fusion.57), calls=%async_computation | async-start | bytes 1572864 | tf_op jit(solution)/shard_map/all_to_all | solution.py:27
  153.2 29.4 %all-gather.15.cloned.1.call-done = bf16[1,768,2304]{2,1,0:T(8,128)(2,1)} async-done(((bf16[1,192,2304]{2,1,0:T(8,128)(2,1)}), bf16[1,768,2304]{2,1,0:T(8,128)(2,1)}) %all-gather.15.cloned.1.call-update) | async-done | bytes 3538960 | tf_op jit(solution)/shard_map/all_gather | solution.py:350
  193.1 12.4 %all-to-all-done.8 = bf16[4,192,768]{2,1,0:T(8,128)(2,1)} async-done(((bf16[4,192,768]{2,1,0:T(8,128)(2,1)}), bf16[4,192,768]{2,1,0:T(8,128)(2,1)}, u32[]{:S(2)}, u32[]{:S(2)}) %all-to-all-start.8) | async-done | bytes 1179680 | tf_op jit(solution)/shard_map/all_to_all | solution.py:27
  225.6 8.5 %all-to-all-start.5 = ((bf16[32,96,128]{2,1,0:T(8,128)(2,1)}), bf16[32,96,128]{2,1,0:T(8,128)(2,1)S(1)}, u32[]{:S(2)}, u32[]{:S(2)}) async-start(bf16[32,96,128]{2,1,0:T(8,128)(2,1)} %fusion.58), calls=%async_computation.5 | async-start | bytes 1572864 | tf_op jit(solution)/shard_map/all_to_all | solution.py:27
  279.4 9.2 %attend_back.2 = bf16[32,96,128]{2,1,0:T(8,128)(2,1)} custom-call(bf16[32,96,128]{2,1,0:T(8,128)(2,1)S(1)} %all-to-all-done.5.in_ref, bf16[32,32,128]{2,1,0:T(8,128)(2,1)S(1)} %all-to-all-done.10.grad_ref, f32[128,1024]{1,0:T(8,128)S(1)} %get-tuple-element.32.full_ref, f32[8,1024]{1,0:T(8,128)S(1)} %get-tuple-element.33.lse_ref), custom_call_target="tpu_custom_call" | custom-call | flops 40000000000 | bytes 40000000 | tf_op jit(solution)/shard_map/attend_back/pallas_call | solution.py:160
  366.5 10.3 %all-to-all-start.14 = ((bf16[32,32,128]{2,1,0:T(8,128)(2,1)}), bf16[32,32,128]{2,1,0:T(8,128)(2,1)S(1)}, u32[]{:S(2)}, u32[]{:S(2)}) async-start(bf16[32,32,128]{2,1,0:T(8,128)(2,1)} %pad.25), calls=%async_computation.14 | async-start | bytes 524288 | tf_op jit(solution)/shard_map/all_to_all | solution.py:27
  378.8 7.0 all-to-all-done.14.grad_ref
  391.3 8.9 %all-to-all-done.22 = bf16[4,128,576]{1,2,0:T(8,128)(2,1)} async-done(((bf16[4,128,576]{1,2,0:T(8,128)(2,1)}), bf16[4,128,576]{1,2,0:T(8,128)(2,1)}, u32[]{:S(2)}, u32[]{:S(2)}) %all-to-all-start.22) | async-done | bytes 589856 | tf_op jit(solution)/shard_map/all_to_all | solution.py:27
  406.6 9.1 %attend_back.3 = bf16[32,96,128]{2,1,0:T(8,128)(2,1)} custom-call(bf16[32,96,128]{2,1,0:T(8,128)(2,1)S(1)} %all-to-all-done.in_ref, bf16[32,32,128]{2,1,0:T(8,128)(2,1)S(1)} %all-to-all-done.14.grad_ref, f32[128,1024]{1,0:T(8,128)S(1)} %get-tuple-element.34.full_ref, f32[8,1024]{1,0:T(8,128)S(1)} %get-tuple-element.35.lse_ref), custom_call_target="tpu_custom_call" | custom-call | flops 40000000000 | bytes 40000000 | tf_op jit(solution)/shard_map/attend_back/pallas_call | solution.py:160
  465.1 12.1 %all-to-all-done.23 = bf16[4,192,576]{2,1,0:T(8,128)(2,1)} async-done(((bf16[4,192,576]{2,1,0:T(8,128)(2,1)}), bf16[4,192,576]{2,1,0:T(8,128)(2,1)}, u32[]{:S(2)}, u32[]{:S(2)}) %all-to-all-start.23) | async-done | bytes 884768 | tf_op jit(solution)/shard_map/all_to_all | solution.py:27
  484.1 7.3 all-to-all-done.17
  519.2 9.2 %all-to-all-start.24 = ((bf16[32,24,576]{2,1,0:T(8,128)(2,1)}), bf16[32,24,576]{2,1,0:T(8,128)(2,1)}, u32[]{:S(2)}, u32[]{:S(2)}) async-start(bf16[32,24,576]{2,1,0:T(8,128)(2,1)} %bitcast.71), calls=%async_computation.24 | async-start | bytes 1966080 | tf_op jit(solution)/shard_map/all_to_all | solution.py:27
  532.9 11.7 %all-to-all-done.24 = bf16[32,24,576]{2,1,0:T(8,128)(2,1)} async-done(((bf16[32,24,576]{2,1,0:T(8,128)(2,1)}), bf16[32,24,576]{2,1,0:T(8,128)(2,1)}, u32[]{:S(2)}, u32[]{:S(2)}) %all-to-all-start.24) | async-done | bytes 884768 | tf_op jit(solution)/shard_map/all_to_all | solution.py:27
  556.1 7.7 all-to-all-done.19
  569.9 34.0 %all-to-all-done.32 = bf16[32,54,768]{2,1,0:T(8,128)(2,1)S(1)} async-done(((bf16[32,54,768]{2,1,0:T(8,128)(2,1)}), bf16[32,54,768]{2,1,0:T(8,128)(2,1)S(1)}, u32[]{:S(2)}, u32[]{:S(2)}) %all-to-all-start.32) | async-done | bytes 2654240 | tf_op jit(solution)/shard_map/all_to_all | solution.py:27
  613.8 12.7 %all-to-all-done.25 = bf16[32,24,576]{2,1,0:T(8,128)(2,1)} async-done(((bf16[32,24,576]{2,1,0:T(8,128)(2,1)}), bf16[32,24,576]{2,1,0:T(8,128)(2,1)}, u32[]{:S(2)}, u32[]{:S(2)}) %all-to-all-start.25) | async-done | bytes 884768 | tf_op jit(solution)/shard_map/all_to_all | solution.py:27
  641.0 10.1 %all-to-all-done.20 = bf16[32,32,576]{2,1,0:T(8,128)(2,1)} async-done(((bf16[32,32,576]{2,1,0:T(8,128)(2,1)}), bf16[32,32,576]{2,1,0:T(8,128)(2,1)}, u32[]{:S(2)}, u32[]{:S(2)}) %all-to-all-start.20) | async-done | bytes 1179680 | tf_op jit(solution)/shard_map/all_to_all | solution.py:27
  657.4 33.9 %all-to-all-done.28 = bf16[32,54,768]{2,1,0:T(8,128)(2,1)} async-done(((bf16[32,54,768]{2,1,0:T(8,128)(2,1)}), bf16[32,54,768]{2,1,0:T(8,128)(2,1)}, u32[]{:S(2)}, u32[]{:S(2)}) %all-to-all-start.28) | async-done | bytes 2654240 | tf_op jit(solution)/shard_map/all_to_all | solution.py:27
  698.0 15.9 %all-to-all-done.21 = bf16[32,24,576]{2,1,0:T(8,128)(2,1)} async-done(((bf16[32,24,576]{2,1,0:T(8,128)(2,1)}), bf16[32,24,576]{2,1,0:T(8,128)(2,1)}, u32[]{:S(2)}, u32[]{:S(2)}) %all-to-all-start.21) | async-done | bytes 884768 | tf_op jit(solution)/shard_map/all_to_all | solution.py:27
  726.0 29.0 %all-to-all-done.33 = bf16[32,54,768]{2,1,0:T(8,128)(2,1)S(1)} async-done(((bf16[32,54,768]{2,1,0:T(8,128)(2,1)}), bf16[32,54,768]{2,1,0:T(8,128)(2,1)S(1)}, u32[]{:S(2)}, u32[]{:S(2)}) %all-to-all-start.33) | async-done | bytes 2654240 | tf_op jit(solution)/shard_map/all_to_all | solution.py:27
  (584 shorter events, 469.9 us)
Async XLA Ops:
  7.2 77.6 %all-gather.11.cloned.1.call-start = ((), (), s32[]{:S(2)}) async-start(), calls=%async_computation.34 | async-start | bytes 4423680 | tf_op jit(solution)/shard_map/all_gather | solution.py:350
  10.1 126.1 %all-gather.17.cloned.1.call-start = ((), (), s32[]{:S(2)}) async-start(), calls=%async_computation.37 | async-start | bytes 1474560 | tf_op jit(solution)/shard_map/all_gather | solution.py:351
  11.1 140.1 %all-gather.13.cloned.1.call-start = ((), (), s32[]{:S(2)}) async-start(), calls=%async_computation.35 | async-start | bytes 1474560 | tf_op jit(solution)/shard_map/all_gather | solution.py:351
  26.3 23.6 %all-to-all-start.2 = ((bf16[4,128,768]{2,1,0:T(8,128)(2,1)}), bf16[4,128,768]{2,1,0:T(8,128)(2,1)S(1)}, u32[]{:S(2)}, u32[]{:S(2)}) async-start(bf16[4,128,768]{2,1,0:T(8,128)(2,1)} %broadcast_in_dim.26), calls=%async_computation.2 | async-start | bytes 1572864 | tf_op jit(solution)/shard_map/all_to_all | solution.py:27
  30.1 152.4 %all-gather.15.cloned.1.call-start = ((), (), s32[]{:S(2)}) async-start(), calls=%async_computation.36 | async-start | bytes 4423680 | tf_op jit(solution)/shard_map/all_gather | solution.py:350
  49.9 26.2 %all-to-all-start.3 = ((bf16[4,192,768]{2,1,0:T(8,128)(2,1)}), bf16[4,192,768]{2,1,0:T(8,128)(2,1)}, u32[]{:S(2)}, u32[]{:S(2)}) async-start(bf16[4,192,768]{2,1,0:T(8,128)(2,1)} %copy.138), calls=%async_computation.3 | async-start | bytes 2359296 | tf_op jit(solution)/shard_map/all_to_all | solution.py:27
  81.2 22.1 %all-to-all-start.4 = ((bf16[4,128,768]{2,1,0:T(8,128)(2,1)}), bf16[4,128,768]{2,1,0:T(8,128)(2,1)S(1)}, u32[]{:S(2)}, u32[]{:S(2)}) async-start(bf16[4,128,768]{2,1,0:T(8,128)(2,1)} %bitcast.297), calls=%async_computation.4 | async-start | bytes 1572864 | tf_op jit(solution)/shard_map/all_to_all | solution.py:27
  104.2 22.6 %all-to-all-start = ((bf16[32,96,128]{2,1,0:T(8,128)(2,1)}), bf16[32,96,128]{2,1,0:T(8,128)(2,1)S(1)}, u32[]{:S(2)}, u32[]{:S(2)}) async-start(bf16[32,96,128]{2,1,0:T(8,128)(2,1)} %fusion.57), calls=%async_computation | async-start | bytes 1572864 | tf_op jit(solution)/shard_map/all_to_all | solution.py:27
  146.1 39.2 %all-to-all-start.12 = ((bf16[4,128,768]{2,1,0:T(8,128)(2,1)}), bf16[4,128,768]{2,1,0:T(8,128)(2,1)}, u32[]{:S(2)}, u32[]{:S(2)}) async-start(bf16[4,128,768]{2,1,0:T(8,128)(2,1)} %broadcast_in_dim.28), calls=%async_computation.12 | async-start | bytes 1572864 | tf_op jit(solution)/shard_map/all_to_all | solution.py:27
  185.3 20.2 %all-to-all-start.8 = ((bf16[4,192,768]{2,1,0:T(8,128)(2,1)}), bf16[4,192,768]{2,1,0:T(8,128)(2,1)}, u32[]{:S(2)}, u32[]{:S(2)}) async-start(bf16[4,192,768]{2,1,0:T(8,128)(2,1)} %copy.150), calls=%async_computation.8 | async-start | bytes 2359296 | tf_op jit(solution)/shard_map/all_to_all | solution.py:27
  225.6 22.7 %all-to-all-start.5 = ((bf16[32,96,128]{2,1,0:T(8,128)(2,1)}), bf16[32,96,128]{2,1,0:T(8,128)(2,1)S(1)}, u32[]{:S(2)}, u32[]{:S(2)}) async-start(bf16[32,96,128]{2,1,0:T(8,128)(2,1)} %fusion.58), calls=%async_computation.5 | async-start | bytes 1572864 | tf_op jit(solution)/shard_map/all_to_all | solution.py:27
  291.4 19.2 %all-to-all-start.11 = ((bf16[32,96,128]{2,1,0:T(8,128)(2,1)}), bf16[32,96,128]{2,1,0:T(8,128)(2,1)S(1)}, u32[]{:S(2)}, u32[]{:S(2)}) async-start(bf16[32,96,128]{2,1,0:T(8,128)(2,1)} %attend_back.2), calls=%async_computation.11 | async-start | bytes 1572864 | tf_op jit(solution)/shard_map/all_to_all | solution.py:27
  310.6 32.1 %all-to-all-start.27 = ((bf16[4,128,192]{1,2,0:T(8,128)(2,1)}), bf16[4,128,192]{1,2,0:T(8,128)(2,1)}, u32[]{:S(2)}, u32[]{:S(2)}) async-start(bf16[4,128,192]{1,2,0:T(8,128)(2,1)} %bitcast.77), calls=%async_computation.27 | async-start | bytes 393216 | tf_op jit(solution)/shard_map/all_to_all | solution.py:27
  366.5 19.3 %all-to-all-start.14 = ((bf16[32,32,128]{2,1,0:T(8,128)(2,1)}), bf16[32,32,128]{2,1,0:T(8,128)(2,1)S(1)}, u32[]{:S(2)}, u32[]{:S(2)}) async-start(bf16[32,32,128]{2,1,0:T(8,128)(2,1)} %pad.25), calls=%async_computation.14 | async-start | bytes 524288 | tf_op jit(solution)/shard_map/all_to_all | solution.py:27
  418.0 19.8 %all-to-all-start.15 = ((bf16[32,96,128]{2,1,0:T(8,128)(2,1)}), bf16[32,96,128]{2,1,0:T(8,128)(2,1)S(1)}, u32[]{:S(2)}, u32[]{:S(2)}) async-start(bf16[32,96,128]{2,1,0:T(8,128)(2,1)} %attend_back.3), calls=%async_computation.15 | async-start | bytes 1572864 | tf_op jit(solution)/shard_map/all_to_all | solution.py:27
  437.8 21.3 %all-to-all-start.30 = ((bf16[4,192,768]{2,1,0:T(8,128)(2,1)}), bf16[4,192,768]{2,1,0:T(8,128)(2,1)}, u32[]{:S(2)}, u32[]{:S(2)}) async-start(bf16[4,192,768]{2,1,0:T(8,128)(2,1)} %bitcast.292), calls=%async_computation.30 | async-start | bytes 2359296 | tf_op jit(solution)/shard_map/all_to_all | solution.py:27
  519.2 25.5 %all-to-all-start.24 = ((bf16[32,24,576]{2,1,0:T(8,128)(2,1)}), bf16[32,24,576]{2,1,0:T(8,128)(2,1)}, u32[]{:S(2)}, u32[]{:S(2)}) async-start(bf16[32,24,576]{2,1,0:T(8,128)(2,1)} %bitcast.71), calls=%async_computation.24 | async-start | bytes 1966080 | tf_op jit(solution)/shard_map/all_to_all | solution.py:27
  563.8 40.1 %all-to-all-start.32 = ((bf16[32,54,768]{2,1,0:T(8,128)(2,1)}), bf16[32,54,768]{2,1,0:T(8,128)(2,1)S(1)}, u32[]{:S(2)}, u32[]{:S(2)}) async-start(bf16[32,54,768]{2,1,0:T(8,128)(2,1)} %reshape.604), calls=%async_computation.32 | async-start | bytes 5505024 | tf_op jit(solution)/shard_map/all_to_all | solution.py:27
  604.9 21.6 %all-to-all-start.25 = ((bf16[32,24,576]{2,1,0:T(8,128)(2,1)}), bf16[32,24,576]{2,1,0:T(8,128)(2,1)}, u32[]{:S(2)}, u32[]{:S(2)}) async-start(bf16[32,24,576]{2,1,0:T(8,128)(2,1)} %broadcast_in_dim.33), calls=%async_computation.25 | async-start | bytes 1966080 | tf_op jit(solution)/shard_map/all_to_all | solution.py:27
  626.5 24.6 %all-to-all-start.20 = ((bf16[32,32,576]{2,1,0:T(8,128)(2,1)}), bf16[32,32,576]{2,1,0:T(8,128)(2,1)}, u32[]{:S(2)}, u32[]{:S(2)}) async-start(bf16[32,32,576]{2,1,0:T(8,128)(2,1)} %pad_maximum_fusion.2), calls=%async_computation.20 | async-start | bytes 2621440 | tf_op jit(solution)/shard_map/all_to_all | solution.py:27
  651.0 40.2 %all-to-all-start.28 = ((bf16[32,54,768]{2,1,0:T(8,128)(2,1)}), bf16[32,54,768]{2,1,0:T(8,128)(2,1)}, u32[]{:S(2)}, u32[]{:S(2)}) async-start(bf16[32,54,768]{2,1,0:T(8,128)(2,1)} %reshape.600), calls=%async_computation.28 | async-start | bytes 5505024 | tf_op jit(solution)/shard_map/all_to_all | solution.py:27
  692.3 21.6 %all-to-all-start.21 = ((bf16[32,24,576]{2,1,0:T(8,128)(2,1)}), bf16[32,24,576]{2,1,0:T(8,128)(2,1)}, u32[]{:S(2)}, u32[]{:S(2)}) async-start(bf16[32,24,576]{2,1,0:T(8,128)(2,1)} %broadcast_in_dim.32), calls=%async_computation.21 | async-start | bytes 1966080 | tf_op jit(solution)/shard_map/all_to_all | solution.py:27
  715.6 39.4 %all-to-all-start.33 = ((bf16[32,54,768]{2,1,0:T(8,128)(2,1)}), bf16[32,54,768]{2,1,0:T(8,128)(2,1)S(1)}, u32[]{:S(2)}, u32[]{:S(2)}) async-start(bf16[32,54,768]{2,1,0:T(8,128)(2,1)} %broadcast_in_dim.35), calls=%async_computation.33 | async-start | bytes 5505024 | tf_op jit(solution)/shard_map/all_to_all | solution.py:27
  756.7 41.0 %all-to-all-start.29 = ((bf16[32,54,768]{2,1,0:T(8,128)(2,1)}), bf16[32,54,768]{2,1,0:T(8,128)(2,1)}, u32[]{:S(2)}, u32[]{:S(2)}) async-start(bf16[32,54,768]{2,1,0:T(8,128)(2,1)} %broadcast_in_dim.34), calls=%async_computation.29 | async-start | bytes 5505024 | tf_op jit(solution)/shard_map/all_to_all | solution.py:27
  (132 other events, 1414.0 us)
Sparse Core Ops, SparseCore 0:
  10.3 59.3 all-gather.10
  71.3 29.6 all-gather.16
  102.7 24.7 all-gather.12
  129.6 52.8 all-gather.14

commit v2 on v1

--- a/solution.py
+++ b/solution.py
@@ -25,6 +25,75 @@
 
 def exchange(chunks, axis):
     return lax.all_to_all(chunks, axis, 0, 0, tiled=True)
+
+
+def pass_on(value, shift):
+    count = lax.axis_size("wt")
+    return lax.ppermute(value, "wt", [(i, (i + shift) % count) for i in range(count)])
+
+
+def shifts():
+    return (1, 3, 2)
+
+
+def group_spread(value):
+    landed = {0: value}
+    for shift in shifts():
+        landed[shift] = pass_on(value, shift)
+    return [landed[shift] for shift in range(4)]
+
+
+def group_sum(blocks):
+    total = blocks[0]
+    for shift in shifts():
+        total = total + pass_on(blocks[shift].astype(BF16), (4 - shift) % 4).astype(F32)
+    return total
+
+
+def group_trade(chunks):
+    here = lax.axis_index("wt")
+
+    def chunk(shift):
+        return lax.dynamic_index_in_dim(chunks, (here + shift) % 4, 0, keepdims=False)
+
+    landed = {0: chunk(0)}
+    for shift in shifts():
+        landed[shift] = pass_on(chunk(shift), shift)
+    return [landed[shift] for shift in range(4)]
+
+
+def place(blocks, axis):
+    here = lax.axis_index("wt")
+    shape = list(blocks[0].shape)
+    size = shape[axis]
+    shape[axis] = 4 * size
+    whole = jnp.zeros(shape, blocks[0].dtype)
+    for shift in range(4):
+        whole = lax.dynamic_update_slice_in_dim(whole, blocks[shift], ((here - shift) % 4) * size, axis)
+    return whole
+
+
+def swap(value):
+    return lax.ppermute(value, "ctx", [(i, i ^ 1) for i in range(lax.axis_size("ctx"))])
+
+
+def gather_half(shard):
+    core = lax.axis_index("ctx") % 2
+    half = shard.shape[0] // 2
+    mine = lax.dynamic_slice_in_dim(shard, core * half, half, 0)
+    return place([b[None] for b in group_spread(mine)], 0)
+
+
+def gather_rest(here):
+    core = lax.axis_index("ctx") % 2
+    other = swap(here)
+    first = jnp.where(core == 0, here, other)
+    second = jnp.where(core == 0, other, here)
+    return jnp.stack([first, second], axis=1).reshape(-1, here.shape[2])
+
+
+def after(values, first):
+    return lax.optimization_barrier((values, first))[0]
 
 
 def spread(value, axis):
@@ -179,33 +248,166 @@
     )(packed, grads, full, lse)
 
 
-def pack_rows(value, seqs):
-    split = value.reshape(seqs, 2, BLK, HEADS, HEAD_DIM).transpose(0, 3, 2, 1, 4)
-    return split.reshape(seqs * HEADS, BLK, 2 * HEAD_DIM)
-
-
-def unpack_rows(tiles, seqs):
-    split = tiles.reshape(seqs, HEADS, BLK, 2, HEAD_DIM).transpose(0, 3, 2, 1, 4)
-    return split.reshape(seqs * 2 * BLK, HEADS * HEAD_DIM)
-
-
-def pad_pairs(tiles):
-    missing = lax.axis_size("ctx") - tiles.shape[0]
-    return jnp.pad(tiles, ((0, missing), (0, 0), (0, 0)))
-
-
-def pack_mixed(query, key, value, seqs):
-    pair = jnp.concatenate(
-        [query.reshape(seqs, 2 * BLK, HEADS, HEAD_DIM), key.reshape(seqs, 2 * BLK, HEADS, HEAD_DIM)], axis=-1
+def kernel_turn(value, tables, sign):
+    cosine, up, down = tables
+    half = ROT // 2
+    back = value.shape[1] - half
+    turned = pltpu.roll(value, half, 1) * up - pltpu.roll(value, back, 1) * down
+    return value * cosine + sign * turned
+
+
+def head(value, rows, index):
+    return value[rows, index * HEAD_DIM : (index + 1) * HEAD_DIM]
+
+
+def mix_kernel(x_ref, gain_ref, shift_ref, w_ref, bq_ref, bv_ref, cos_ref, up_ref, down_ref, xhat_ref, low_ref, scale_ref, out_ref):
+    x = x_ref[...]
+    rows, width = x.shape
+    centred = x - jnp.mean(x, axis=-1, keepdims=True)
+    scale = lax.rsqrt(jnp.mean(centred * centred, axis=-1, keepdims=True) + EPS)
+    xhat = centred * scale
+    xhat_ref[...] = xhat
+    low_ref[...] = xhat.astype(BF16)
+    scale_ref[...] = jnp.broadcast_to(scale, scale_ref.shape)
+    normed = (xhat * gain_ref[...] + shift_ref[...]).astype(BF16)
+    tables = (cos_ref[...], up_ref[...], down_ref[...])
+    query = kernel_turn(dot(normed, w_ref[:, :width]) + bq_ref[...], tables, 1.0)
+    key = kernel_turn(dot(normed, w_ref[:, width : 2 * width]), tables, 1.0)
+    value = dot(normed, w_ref[:, 2 * width :]) + bv_ref[...]
+    seqs = rows // (2 * BLK)
+    for s in range(seqs):
+        at = s * 2 * BLK
+        whole, early, late = slice(at, at + 2 * BLK), slice(at, at + BLK), slice(at + BLK, at + 2 * BLK)
+        for h in range(HEADS):
+            pair = jnp.concatenate([head(query, whole, h), head(key, whole, h)], axis=1)
+            out_ref[s * HEADS + h, : 2 * BLK, :] = pair.astype(BF16)
+            pair = jnp.concatenate([head(value, early, h), head(value, late, h)], axis=1)
+            out_ref[s * HEADS + h, 2 * BLK :, :] = pair.astype(BF16)
+    spare = out_ref.shape[0] - seqs * HEADS
+    out_ref[seqs * HEADS :, :, :] = jnp.zeros((spare,) + out_ref.shape[1:], BF16)
+
+
+def on_chip(kernel, out_shape, name, flops, *operands, scratch=()):
+    many = isinstance(out_shape, tuple)
+    spec = pl.BlockSpec(memory_space=pltpu.VMEM)
+    return pl.pallas_call(
+        kernel,
+        out_shape=out_shape,
+        in_specs=[spec] * len(operands),
+        out_specs=[spec] * len(out_shape) if many else spec,
+        scratch_shapes=list(scratch),
+        compiler_params=pltpu.CompilerParams(vmem_limit_bytes=48 << 20),
+        cost_estimate=pl.CostEstimate(flops=flops, bytes_accessed=8_000_000, transcendentals=0),
+        name=name,
+    )(*operands)
+
+
+def shaped(shape, dtype):
+    return jax.ShapeDtypeStruct(shape, dtype)
+
+
+def mix(x, w, tables):
+    rows, width = x.shape
+    count = lax.axis_size("ctx")
+    shapes = (
+        shaped((rows, width), F32),
+        shaped((rows, width), BF16),
+        shaped((rows, 128), F32),
+        shaped((count, 3 * BLK, 128), BF16),
     )
-    pair = pair.transpose(0, 2, 1, 3).reshape(seqs * HEADS, 2 * BLK, 2 * HEAD_DIM)
-    return pad_pairs(jnp.concatenate([pair, pack_rows(value, seqs)], axis=1))
-
-
-def unpack_mixed(tiles, seqs):
-    pair = tiles[: seqs * HEADS, : 2 * BLK].reshape(seqs, HEADS, 2 * BLK, 2, HEAD_DIM)
-    pair = pair.transpose(3, 0, 2, 1, 4).reshape(2, seqs * 2 * BLK, HEADS * HEAD_DIM)
-    return pair[0], pair[1], unpack_rows(tiles[: seqs * HEADS, 2 * BLK :], seqs)
+    return on_chip(mix_kernel, shapes, "mix", 5_000_000_000, x, w["g_attn"], w["s_attn"], w["qkv"], w["b_q"], w["b_v"], *tables)
+
+
+def join_kernel(tile_ref, x_ref, mlp_ref, w_ref, bias_ref, split_ref, out_ref, context):
+    rows, width = context.shape
+    for s in range(rows // (2 * BLK)):
+        for half in range(2):
+            at = (2 * s + half) * BLK
+            lanes = slice(half * HEAD_DIM, (half + 1) * HEAD_DIM)
+            row = [tile_ref[s * HEADS + h, :, lanes] for h in range(HEADS)]
+            context[at : at + BLK, :] = jnp.concatenate(row, axis=1)
+    size = width // 4
+    for block in range(4):
+        split_ref[block] = context[:, block * size : (block + 1) * size]
+    out_ref[...] = x_ref[...] + dot(context[...], w_ref[...]) + (mlp_ref[...] + bias_ref[...])
+
+
+def join(tiles, x, mlp, w):
+    rows, width = x.shape
+    shapes = (shaped((4, rows, width // 4), BF16), shaped((rows, width), F32))
+    scratch = [pltpu.VMEM((rows, width), BF16)]
+    return on_chip(join_kernel, shapes, "join", 500_000_000, tiles, x, mlp, w["out"], w["b_out"] + w["b_down"], scratch=scratch)
+
+
+def pull_kernel(g_ref, w_ref, out_ref):
+    grad = dot(g_ref[...], w_ref[...], NT)
+    seqs = grad.shape[0] // (2 * BLK)
+    for s in range(seqs):
+        at = s * 2 * BLK
+        for h in range(HEADS):
+            early, late = head(grad, slice(at, at + BLK), h), head(grad, slice(at + BLK, at + 2 * BLK), h)
+            out_ref[s * HEADS + h] = jnp.concatenate([early, late], axis=1).astype(BF16)
+    spare = out_ref.shape[0] - seqs * HEADS
+    out_ref[seqs * HEADS :, :, :] = jnp.zeros((spare,) + out_ref.shape[1:], BF16)
+
+
+def pull(g_low, w):
+    count = lax.axis_size("ctx")
+    return on_chip(pull_kernel, shaped((count, BLK, 128), BF16), "pull", 500_000_000, g_low, w["out"])
+
+
+def unmix_kernel(tile_ref, cos_ref, up_ref, down_ref, mixed_ref, split_ref, sums_ref):
+    rows, width = cos_ref.shape
+    tables = (cos_ref[...], up_ref[...], down_ref[...])
+    parts = [[], [], []]
+    for s in range(rows // (2 * BLK)):
+        for part in range(2):
+            lanes = slice(part * HEAD_DIM, (part + 1) * HEAD_DIM)
+            row = [tile_ref[s * HEADS + h, : 2 * BLK, lanes] for h in range(HEADS)]
+            parts[part].append(jnp.concatenate(row, axis=1))
+        for half in range(2):
+            lanes = slice(half * HEAD_DIM, (half + 1) * HEAD_DIM)
+            row = [tile_ref[s * HEADS + h, 2 * BLK :, lanes] for h in range(HEADS)]
+            parts[2].append(jnp.concatenate(row, axis=1))
+    query, key, value = (jnp.concatenate(part, axis=0) for part in parts)
+    mixed_ref[:, :width] = kernel_turn(query.astype(F32), tables, -1.0).astype(BF16)
+    mixed_ref[:, width : 2 * width] = kernel_turn(key.astype(F32), tables, -1.0).astype(BF16)
+    mixed_ref[:, 2 * width :] = value
+    size = 3 * width // 4
+    for block in range(4):
+        split_ref[block] = mixed_ref[:, block * size : (block + 1) * size]
+    sums_ref[...] = jnp.sum(mixed_ref[...].astype(F32), axis=0, keepdims=True)
+
+
+def unmix(tiles, tables):
+    rows, width = tables[0].shape
+    shapes = (
+        shaped((rows, 3 * width), BF16),
+        shaped((4, rows, 3 * width // 4), BF16),
+        shaped((1, 3 * width), F32),
+    )
+    return on_chip(unmix_kernel, shapes, "unmix", 500_000_000, tiles, *tables)
+
+
+def norm_kernel(mixed_ref, w_ref, g_ref, mlp_ref, xhat_ref, scale_ref, ga_ref, gm_ref, out_ref, low_ref, sums_ref):
+    attn = dot(mixed_ref[...], w_ref[...], NT)
+    mlp, xhat, g = mlp_ref[...], xhat_ref[...], g_ref[...]
+    both = attn * ga_ref[...] + mlp * gm_ref[...]
+    inner = both - jnp.mean(both, axis=-1, keepdims=True) - xhat * jnp.mean(both * xhat, axis=-1, keepdims=True)
+    new = g + scale_ref[:, :1] * inner
+    out_ref[...] = new
+    low_ref[...] = new.astype(BF16)
+    sums_ref[...] = jnp.zeros_like(sums_ref)
+    for row, value in enumerate((attn * xhat, attn, mlp * xhat, mlp, g.astype(BF16).astype(F32))):
+        sums_ref[row : row + 1, :] = jnp.sum(value, axis=0, keepdims=True)
+
+
+def norm_backward(g, mixed, grad_n_mlp, xhat, scale, w):
+    rows, width = g.shape
+    shapes = (shaped((rows, width), F32), shaped((rows, width), BF16), shaped((8, width), F32))
+    return on_chip(
+        norm_kernel, shapes, "norm_back", 1_500_000_000, mixed, w["qkv"], g, grad_n_mlp, xhat, scale, w["g_attn"], w["g_mlp"]
+    )
 
 
 def rotary_tables(seqs):
@@ -230,99 +432,52 @@
     return lax.optimization_barrier(tables)
 
 
-def turn(value, tables, sign):
-    cosine, up, down = tables
-    half = ROT // 2
-    return value * cosine + sign * (jnp.roll(value, half, 1) * up - jnp.roll(value, -half, 1) * down)
-
-
-def standardize(values):
-    centred = values - jnp.mean(values, axis=-1, keepdims=True)
-    scale = lax.rsqrt(jnp.mean(centred * centred, axis=-1, keepdims=True) + EPS)
-    return centred * scale, scale
-
-
 def cdf(value):
     return 0.5 * (1.0 + lax.erf(value * (0.5 ** 0.5)))
 
 
-def layer_forward(x, w, tables, seqs):
-    xhat, scale = standardize(x)
-    xhat_low = xhat.astype(BF16)
-    xhat_all = spread(xhat_low, "wt").reshape(-1, x.shape[1])
-    n_attn = (xhat * w["g_attn"] + w["s_attn"]).astype(BF16)
-    mixed = dot(n_attn, w["qkv"])
-    width = x.shape[1]
-    query = turn(mixed[:, :width] + w["b_q"], tables, 1.0).astype(BF16)
-    key = turn(mixed[:, width : 2 * width], tables, 1.0).astype(BF16)
-    value = (mixed[:, 2 * width :] + w["b_v"]).astype(BF16)
-    packed = exchange(pack_mixed(query, key, value, seqs), "ctx")
-    out, full, lse = attend(packed)
-    context = unpack_rows(exchange(out, "ctx")[: seqs * HEADS], seqs)
+TN = (((0,), (0,)), ((), ()))
+
+
+def split_columns(value):
+    return value.reshape(value.shape[0], 4, -1).transpose(1, 0, 2)
+
+
+def mlp_forward(xhat_all, w):
     n_mlp_all = (xhat_all.astype(F32) * w["g_mlp"] + w["s_mlp"]).astype(BF16)
     hidden = dot(n_mlp_all, w["up"]) + w["b_up"]
     active = (hidden * cdf(hidden)).astype(BF16)
-    partial = dot(active, w["down"]).astype(BF16)
-    mlp = exchange(partial.reshape(-1, *x.shape), "wt").astype(F32).sum(0)
-    branch = dot(context, w["out"]) + w["b_out"]
-    group = lax.axis_size("wt")
-    context_all = exchange(context.reshape(x.shape[0], group, -1).transpose(1, 0, 2), "wt")
-    stored = (xhat, scale, xhat_all, n_mlp_all, packed, full, lse, context_all, hidden, active)
-    return x + branch + (mlp + w["b_down"]), stored
-
-
-def layer_backward(g, w, stored, tables, seqs):
-    xhat, scale, xhat_all, n_mlp_all, packed, full, lse, context_all, hidden, active = stored
-    rows, width = g.shape
-    group = lax.axis_size("wt")
-    g_low = g.astype(BF16)
-    g_all = spread(g_low, "wt").reshape(-1, width)
-    grad_context = dot(g_low, w["out"], NT).astype(BF16)
-    grads = exchange(pad_pairs(pack_rows(grad_context, seqs)), "ctx")
+    partial = dot(active, w["down"])
+    rows = partial.shape[0] // 4
+    total = group_sum([partial[i * rows : (i + 1) * rows] for i in range(4)])
+    return n_mlp_all, hidden, active, total
+
+
+def mlp_backward(g_all, n_mlp_all, hidden, active, w):
     grad_active = dot(g_all, w["down"], NT)
     density = jnp.exp(-0.5 * hidden * hidden) * 0.3989422804014327
     grad_hidden = (grad_active * (cdf(hidden) + hidden * density)).astype(BF16)
-    partial = dot(grad_hidden, w["up"], NT).astype(BF16)
-    grad_n_mlp = exchange(partial.reshape(-1, rows, width), "wt").astype(F32).sum(0)
-    tn = (((0,), (0,)), ((), ()))
-    grad_down = dot(active, g_all, tn).astype(BF16)
-    grad_out = dot(context_all.transpose(2, 0, 1).reshape(width // group, -1), g_all).astype(BF16)
-    grad_up = dot(n_mlp_all, grad_hidden, tn).astype(BF16)
+    partial = dot(grad_hidden, w["up"], NT)
+    rows = partial.shape[0] // 4
+    grad_n_mlp = group_sum([partial[i * rows : (i + 1) * rows] for i in range(4)])
+    grad_down = dot(active, g_all, TN).astype(BF16)
+    grad_up = dot(n_mlp_all, grad_hidden, TN).astype(BF16)
     grad_b_up = jnp.sum(grad_hidden.astype(F32), axis=0)
-    grad_up = exchange(grad_up.reshape(group, width // group, -1), "wt").reshape(width, -1)
-    sums = jnp.concatenate([grad_down, grad_up, grad_out], axis=0)
-    pieces = exchange(sums.reshape(lax.axis_size("ctx"), -1, width), "ctx")
-    wide = spread(pieces.astype(F32).sum(0).astype(BF16), "ctx").reshape(-1, width)
-    back = exchange(attend_back(packed, grads, full, lse), "ctx")
-    grad_q, grad_k, grad_v = unpack_mixed(back, seqs)
-    grad_q = turn(grad_q.astype(F32), tables, -1.0).astype(BF16)
-    grad_k = turn(grad_k.astype(F32), tables, -1.0).astype(BF16)
-    grad_mixed = jnp.concatenate([grad_q, grad_k, grad_v], axis=1)
-    grad_n_attn = dot(grad_mixed, w["qkv"], NT)
-    mixed_all = exchange(grad_mixed.reshape(rows, group, -1).transpose(1, 0, 2), "wt").reshape(group * rows, -1)
-    n_attn_all = (xhat_all.astype(F32) * w["g_attn"] + w["s_attn"]).astype(BF16)
-    grad_qkv = dot(n_attn_all, mixed_all, tn).astype(BF16).reshape(group, width // group, -1)
-    pull = grad_n_attn * w["g_attn"] + grad_n_mlp * w["g_mlp"]
-    inner = pull - jnp.mean(pull, axis=-1, keepdims=True) - xhat * jnp.mean(pull * xhat, axis=-1, keepdims=True)
-    small = jnp.stack(
-        [
-            jnp.sum(grad_n_attn * xhat, axis=0),
-            jnp.sum(grad_n_attn, axis=0),
-            jnp.sum(grad_n_mlp * xhat, axis=0),
-            jnp.sum(grad_n_mlp, axis=0),
-            jnp.sum(g_low.astype(F32), axis=0),
-        ]
-    )
-    bias = jnp.concatenate([jnp.sum(grad_q.astype(F32), axis=0), jnp.sum(grad_v.astype(F32), axis=0)])
-    small = small.reshape(5, group, -1).transpose(1, 0, 2).reshape(group, -1)
-    small = jnp.concatenate([small, bias.reshape(group, -1)], axis=1)
-    return g + scale * inner, wide, grad_qkv, small, grad_b_up
+    grad_up = place(group_trade(grad_up.reshape(4, -1, grad_up.shape[1])), 1)
+    return grad_n_mlp, grad_down, grad_up, grad_b_up
+
+
+def small_sums(sums, mixed_sums):
+    width = sums.shape[1]
+    bias = jnp.concatenate([mixed_sums[0, :width], mixed_sums[0, 2 * width :]])
+    rest = sums[:5].reshape(5, 4, -1).transpose(1, 0, 2).reshape(4, -1)
+    return jnp.concatenate([rest, bias.reshape(4, -1)], axis=1)
 
 
 def gather_small(stacked):
     names = ("g_attn", "s_attn", "g_mlp", "s_mlp", "b_qv", "b_out", "b_down")
     flat = jnp.concatenate([stacked[name] for name in names], axis=1)
-    every = lax.all_gather(flat, "wt", axis=0).astype(F32)
+    every = spread(flat, "wt").astype(F32)
     found, at = {}, 0
     for name in names:
         size = stacked[name].shape[1]
@@ -335,36 +490,75 @@
     seqs = tokens_in.shape[0]
     width = tokens_in.shape[3]
     rows = seqs * 2 * BLK
-    group = lax.axis_size("wt")
     devices = lax.axis_size("ctx")
+    depth = width // 4
+    unit = b_up.shape[1]
     tables = rotary_tables(seqs)
     small = gather_small(
         {"g_attn": ln_gain_attn, "s_attn": ln_shift_attn, "g_mlp": ln_gain_mlp, "s_mlp": ln_shift_mlp, "b_qv": b_qv, "b_out": b_out, "b_down": b_down}
     )
+    half1 = gather_half(w_qkv[0])
+    later_out, later_qkv = after((w_out, w_qkv[1]), half1)
+    qkv = [gather_rest(half1), lax.all_gather(later_qkv, "wt", axis=0, tiled=True)]
+    out_both = lax.all_gather(later_out, "wt", axis=1, tiled=True)
+    ups = w_up.reshape(LAYERS * depth, 4, unit).transpose(1, 0, 2)
+    ups = exchange(ups, "wt").reshape(4, LAYERS, depth, unit).transpose(1, 0, 2, 3).reshape(LAYERS, width, unit)
     layers = []
     for layer in range(LAYERS):
-        up = w_up[layer].reshape(width // group, group, -1).transpose(1, 0, 2)
         w = {name: small[name][layer][None] for name in small}
         w["b_q"] = w["b_qv"][:, :width]
         w["b_v"] = w["b_qv"][:, width:]
-        w["qkv"] = lax.all_gather(w_qkv[layer], "wt", axis=0, tiled=True)
-        w["out"] = lax.all_gather(w_out[layer], "wt", axis=0, tiled=True)
-        w["up"] = exchange(up, "wt").reshape(width, -1)
+        w["qkv"] = qkv[layer]
+        w["out"] = out_both[layer]
+        w["up"] = ups[layer]
         w["down"] = w_down[layer]
         w["b_up"] = b_up[layer].astype(F32)[None]
         layers.append(w)
-    x = tokens_in.reshape(rows, width).astype(F32)
-    kept = []
-    for w in layers:
-        x, stored = layer_forward(x, w, tables, seqs)
-        kept.append(stored)
-    out_tokens = x.astype(BF16).reshape(tokens_in.shape)
-    g = cotangent.reshape(rows, width).astype(F32)
-    wides, qkvs, smalls, ups = ([None] * LAYERS for _ in range(4))
-    for layer in reversed(range(LAYERS)):
-        g, wides[layer], qkvs[layer], smalls[layer], ups[layer] = layer_backward(g, layers[layer], kept[layer], tables, seqs)
-    columns = qkvs[0].shape[2]
-    depth = width // group
+    first, second = layers
+    g2 = cotangent.reshape(rows, width)
+    x1 = tokens_in.reshape(rows, width).astype(F32)
+    xhat1, low1, scale1, packed1 = mix(x1, first, tables)
+    packed1 = exchange(packed1, "ctx")
+    xhat1_all = jnp.concatenate(group_spread(low1), axis=0)
+    n_mlp1, hidden1, active1, mlp1 = mlp_forward(xhat1_all, first)
+    out1, full1, lse1 = attend(packed1)
+    out1 = exchange(out1, "ctx")
+    split1, x2 = join(out1, x1, mlp1, first)
+    xhat2, low2, scale2, packed2 = mix(x2, second, tables)
+    packed2 = exchange(packed2, "ctx")
+    grads2 = exchange(pull(g2, second), "ctx")
+    xhat2_all = jnp.concatenate(group_spread(low2), axis=0)
+    n_mlp2, hidden2, active2, mlp2 = mlp_forward(xhat2_all, second)
+    out2, full2, lse2 = attend(packed2)
+    back2 = exchange(attend_back(packed2, grads2, full2, lse2), "ctx")
+    g2_all = jnp.concatenate(group_spread(g2), axis=0)
+    grad_n_mlp2, grad_down2, grad_up2, grad_b_up2 = mlp_backward(g2_all, n_mlp2, hidden2, active2, second)
+    mixed2, mixed2_split, mixed_sums2 = unmix(back2, tables)
+    g1, g1_low, sums2 = norm_backward(g2.astype(F32), mixed2, grad_n_mlp2, xhat2, scale2, second)
+    grads1 = exchange(pull(g1_low, first), "ctx")
+    g1_all = jnp.concatenate(group_spread(g1_low), axis=0)
+    grad_n_mlp1, grad_down1, grad_up1, grad_b_up1 = mlp_backward(g1_all, n_mlp1, hidden1, active1, first)
+    back1 = exchange(attend_back(packed1, grads1, full1, lse1), "ctx")
+    out2 = exchange(out2, "ctx")
+    split2, x3 = join(out2, x2, mlp2, second)
+    out_tokens = x3.astype(BF16).reshape(tokens_in.shape)
+    context1_all = jnp.concatenate(group_trade(split1), axis=0)
+    context2_all = jnp.concatenate(group_trade(split2), axis=0)
+    grad_out2 = dot(context2_all, g2_all, TN).astype(BF16)
+    mixed2_all = jnp.concatenate(group_trade(mixed2_split), axis=0)
+    grad_out1 = dot(context1_all, g1_all, TN).astype(BF16)
+    n_attn2_all = (xhat2_all.astype(F32) * second["g_attn"] + second["s_attn"]).astype(BF16)
+    grad_qkv2 = dot(n_attn2_all, mixed2_all, TN).astype(BF16)
+    mixed1, mixed1_split, mixed_sums1 = unmix(back1, tables)
+    mixed1_all = jnp.concatenate(group_trade(mixed1_split), axis=0)
+    n_attn1_all = (xhat1_all.astype(F32) * first["g_attn"] + first["s_attn"]).astype(BF16)
+    grad_qkv1 = dot(n_attn1_all, mixed1_all, TN).astype(BF16)
+    g0, _, sums1 = norm_backward(g1, mixed1, grad_n_mlp1, xhat1, scale1, first)
+    small1, small2 = small_sums(sums1, mixed_sums1), small_sums(sums2, mixed_sums2)
+    columns = grad_qkv2.shape[1]
+    moved2 = exchange(grad_qkv2.reshape(4, depth, columns), "wt")
+    wide = lax.psum((grad_down1, grad_up1, grad_out1, grad_down2, grad_up2, grad_out2, moved2), "ctx")
+    smalls, hidden_sums = (small1, small2), (grad_b_up1, grad_b_up2)
     piece = width // devices
 
     def to_rows(value):
@@ -374,52 +568,44 @@
         padded = jnp.pad(value, ((0, 0), (0, lines * columns - size)))
         return padded.reshape(value.shape[0], lines, columns)
 
-    totals = [None] * LAYERS
-    for layer in reversed(range(1, LAYERS)):
-        moved = exchange(qkvs[layer], "wt")
-        part = exchange(moved.reshape(devices, piece, columns), "ctx").astype(F32).sum(0).astype(BF16)
-        totals[layer] = spread(part, "ctx").reshape(group, depth, columns)
     tiny = to_rows(jnp.concatenate(smalls, axis=1).astype(BF16))
-    moved = exchange(jnp.concatenate([qkvs[0], tiny], axis=1), "wt")
-    small_sum = moved[:, depth:].astype(F32).sum(0).reshape(1, -1)[:, : sum(s.shape[1] for s in smalls)]
-    tail = to_rows(jnp.concatenate([small_sum, *(u[None] for u in ups)], axis=1).astype(BF16))
+    moved = exchange(jnp.concatenate([grad_qkv1.reshape(4, depth, columns), tiny], axis=1), "wt")
+    tiny_size = small1.shape[1]
+    small_sum = moved[:, depth:].astype(F32).sum(0).reshape(1, -1)[:, : LAYERS * tiny_size]
+    tail = to_rows(jnp.concatenate([small_sum, *(u[None] for u in hidden_sums)], axis=1).astype(BF16))
     sent = jnp.concatenate(
         [moved[:, :depth].reshape(devices, piece, columns), jnp.broadcast_to(tail, (devices,) + tail.shape[1:])], axis=1
     )
     landed = exchange(sent, "ctx").astype(F32).sum(0)
-    totals[0] = spread(landed[:piece].astype(BF16), "ctx").reshape(group, depth, columns)
+    moved1 = spread(landed[:piece].astype(BF16), "ctx").reshape(4, depth, columns)
     flat = landed[piece:].reshape(-1)
-    tiny_size = smalls[0].shape[1]
     per_layer = [flat[layer * tiny_size : (layer + 1) * tiny_size] for layer in range(LAYERS)]
     at = LAYERS * tiny_size
-    unit = ups[0].shape[0]
     grad_b_up = flat[at : at + LAYERS * unit].reshape(LAYERS, unit)
 
     def vector(index):
         return jnp.stack([v[index * depth : (index + 1) * depth] for v in per_layer])
 
+    def both(one, two):
+        return jnp.stack([one.astype(F32), two.astype(F32)])
+
     grad_bias = vector(4)
     grad_b_qv = jnp.stack([v[5 * depth :] for v in per_layer])
-    grad_qkv = jnp.stack([t.astype(F32).transpose(1, 0, 2).reshape(depth, -1) for t in totals])
-    grad_down = jnp.stack([v[:unit].astype(F32) for v in wides])
-    grad_up = jnp.stack(
-        [v[unit : unit + width].astype(F32).reshape(group, depth, unit).transpose(1, 0, 2).reshape(depth, -1) for v in wides]
-    )
-    grad_out = jnp.stack([v[unit + width :].astype(F32) for v in wides])
+    grad_qkv = both(*(m.transpose(1, 0, 2).reshape(depth, -1) for m in (moved1, wide[6])))
     return (
         out_tokens,
-        g.reshape(tokens_in.shape),
+        g0.reshape(tokens_in.shape),
         vector(0),
         vector(1),
         vector(2),
         vector(3),
         grad_qkv,
         grad_b_qv,
-        grad_out,
+        both(wide[2], wide[5]),
         grad_bias,
-        grad_up,
+        both(wide[1], wide[4]),
         grad_b_up,
-        grad_down,
+        both(wide[0], wide[3]),
         grad_bias,
     )
 

time: 832 us -> 598 us (0.72)
  waiting for transfers between devices: 329 us -> 203 us
  local copies, waits for them, and re-layouts: 140 us -> 86.1 us
  other arithmetic: 65.1 us -> 29 us
  matrix products: 61.2 us -> 34 us
  Pallas kernels: 29.5 us -> 51.3 us
  blocking collectives: 11.1 us -> 0 us
    all_to_all x34 -> x14, waiting for transfers between devices: 298 us -> 68.2 us  [exchange(): return lax.all_to_all(chunks, axis, 0, 0, tiled=True)]
    psum x0 -> x1, waiting for transfers between devices: none -> 77.1 us  [local(): lax.psum((grad_down1, grad_up1, grad_out1, grad_down2, grad_up2, grad_out...]
    ppermute x0 -> x46, starting transfers between devices: none -> 61.3 us  [the longest x45 60.3 us: pass_on(): lax.ppermute(value, 'wt', [(i, (i + shift) % count) for i in range(count)])]
    all_to_all x34 -> x14, starting transfers between devices: 168 us -> 106 us  [exchange(): return lax.all_to_all(chunks, axis, 0, 0, tiled=True)]
    ppermute x0 -> x46, waiting for transfers between devices: none -> 57.8 us  [the longest x45 57.8 us: pass_on(): lax.ppermute(value, 'wt', [(i, (i + shift) % count) for i in range(count)])]
    reshape x37 -> x8, local copies, waits for them, and re-layouts: 41.5 us -> 6.17 us  [the longest x1 5.69 us: local(): ups = w_up.reshape(LAYERS * depth, 4, unit).transpose(1, 0, 2)]
    all_gather x4 -> x2, waiting for transfers between devices: 29.4 us -> 0.02 us  [the longest x1 0.02 us: local(): out_both = lax.all_gather(later_out, 'wt', axis=1, tiled=True)]
    dot_general x24 -> x16, matrix products: 61.2 us -> 34 us  [dot(): return lax.dot_general(left, right, dims, preferred_element_type=F32)]
  transfers between devices with their start and end apart: 38 -> 63, of which waited for: 32 -> 25; matrix products, arithmetic and copies ran while one was open for 29% -> 19% of each run, Pallas kernels for 4% -> 9%
where the time goes in v2:
time: 598 us; the launch traced here: 587 us
  waiting for transfers between devices  203 us (34%)
  starting transfers between devices  168 us (28%)
  local copies, waits for them, and re-layouts  86.1 us (14%)
  Pallas kernels  51.3 us (9%)
  matrix products  34 us (6%)
  other arithmetic  29 us (5%)
  between operations  15.5 us (3%)
    all_to_all x14, starting transfers between devices, exchange(): return lax.all_to_all(chunks, axis, 0, 0, tiled=True)  106 us
    psum x1, waiting for transfers between devices, local(): lax.psum((grad_down1, grad_up1, grad_out1, grad_down2, grad_up2, grad_out...  77.1 us
    all_to_all x14, waiting for transfers between devices, exchange(): return lax.all_to_all(chunks, axis, 0, 0, tiled=True)  68.2 us
    ppermute x45, starting transfers between devices, pass_on(): lax.ppermute(value, 'wt', [(i, (i + shift) % count) for i in range(count)])  60.3 us
    ppermute x45, waiting for transfers between devices, pass_on(): lax.ppermute(value, 'wt', [(i, (i + shift) % count) for i in range(count)])  57.8 us
    dot_general x16, matrix products, dot(): return lax.dot_general(left, right, dims, preferred_element_type=F32)  34 us
    unnamed x202, local copies, waits for them, and re-layouts  25.4 us
    pallas_call x10, Pallas kernels, on_chip(): pl.pallas_call(kernel, out_shape=out_shape, in_specs=[spec] * len(operand...  21 us
  transfers between devices with their start and end apart: 63, of which 25 were waited for; matrix products, arithmetic and copies ran while one was open for 19% of the time, Pallas kernels for 9%

profile of v2, /device:TPU:1, one launch (start us, length us, event | category | flops | bytes accessed | tf_op | source)
XLA Modules:
  0.0 586.9 jit_solution(9706082055058643571)
XLA Ops:
  16.5 8.1 %collective-permute-done = bf16[96,2304]{1,0:T(8,128)(2,1)} collective-permute-done((bf16[96,2304]{1,0:T(8,128)(2,1)S(1)}, bf16[96,2304]{1,0:T(8,128)(2,1)}, u32[]{:S(2)}, u32[]{:S(2)}) %collective-permute-start) | collective-permute-done | bytes 442400 | tf_op jit(solution)/shard_map/ppermute | solution.py:32
  25.8 9.0 %collective-permute-done.1 = bf16[96,2304]{1,0:T(8,128)(2,1)S(1)} collective-permute-done((bf16[96,2304]{1,0:T(8,128)(2,1)S(1)}, bf16[96,2304]{1,0:T(8,128)(2,1)S(1)}, u32[]{:S(2)}, u32[]{:S(2)}) %collective-permute-start.1) | collective-permute-done | bytes 442400 | tf_op jit(solution)/shard_map/ppermute | solution.py:32
  48.7 5.7 reshape.294
  80.7 20.1 %all-to-all-done.3 = bf16[4,384,768]{2,1,0:T(8,128)(2,1)} async-done(((bf16[4,384,768]{2,1,0:T(8,128)(2,1)}), bf16[4,384,768]{2,1,0:T(8,128)(2,1)}, u32[]{:S(2)}, u32[]{:S(2)}) %all-to-all-start.3) | async-done | bytes 2359328 | tf_op jit(solution)/shard_map/all_to_all | solution.py:27
  103.5 7.9 %all-to-all-start.1 = ((bf16[32,96,128]{2,1,0:T(8,128)(2,1)}), bf16[32,96,128]{2,1,0:T(8,128)(2,1)S(1)}, u32[]{:S(2)}, u32[]{:S(2)}) async-start(bf16[32,96,128]{2,1,0:T(8,128)(2,1)} %get-tuple-element.55), calls=%async_computation.1 | async-start | bytes 1572864 | tf_op jit(solution)/shard_map/all_to_all | solution.py:27
  111.5 6.1 %collective-permute-done.5 = bf16[128,768]{1,0:T(8,128)(2,1)} collective-permute-done((bf16[128,768]{1,0:T(8,128)(2,1)S(1)}, bf16[128,768]{1,0:T(8,128)(2,1)}, u32[]{:S(2)}, u32[]{:S(2)}) %collective-permute-start.5) | collective-permute-done | bytes 196640 | tf_op jit(solution)/shard_map/ppermute | solution.py:32
  125.3 7.4 %collective-permute-done.7 = bf16[128,768]{1,0:T(8,128)(2,1)S(1)} collective-permute-done((bf16[128,768]{1,0:T(8,128)(2,1)S(1)}, bf16[128,768]{1,0:T(8,128)(2,1)S(1)}, u32[]{:S(2)}, u32[]{:S(2)}) %collective-permute-start.7) | collective-permute-done | bytes 196640 | tf_op jit(solution)/shard_map/ppermute | solution.py:32
  134.0 5.9 %collective-permute-done.9 = bf16[128,768]{1,0:T(8,128)(2,1)S(1)} collective-permute-done((bf16[128,768]{1,0:T(8,128)(2,1)S(1)}, bf16[128,768]{1,0:T(8,128)(2,1)S(1)}, u32[]{:S(2)}, u32[]{:S(2)}) %collective-permute-start.9) | collective-permute-done | bytes 196640 | tf_op jit(solution)/shard_map/ppermute | solution.py:32
  140.8 5.6 attend.2
  147.3 7.8 %all-to-all-start.2 = ((bf16[32,32,128]{2,1,0:T(8,128)(2,1)}), bf16[32,32,128]{2,1,0:T(8,128)(2,1)}, u32[]{:S(2)}, u32[]{:S(2)}) async-start(bf16[32,32,128]{2,1,0:T(8,128)(2,1)} %get-tuple-element.56), calls=%async_computation.2 | async-start | bytes 524288 | tf_op jit(solution)/shard_map/all_to_all | solution.py:27
  156.9 7.2 %all-to-all-done.2.tile_ref = bf16[32,32,128]{2,1,0:T(8,128)(2,1)} async-done(((bf16[32,32,128]{2,1,0:T(8,128)(2,1)}), bf16[32,32,128]{2,1,0:T(8,128)(2,1)}, u32[]{:S(2)}, u32[]{:S(2)}) %all-to-all-start.2) | async-done | bytes 262176 | tf_op jit(solution)/shard_map/all_to_all | solution.py:27
  234.2 16.6 %all-to-all-start.6 = ((bf16[32,32,128]{2,1,0:T(8,128)(2,1)}), bf16[32,32,128]{2,1,0:T(8,128)(2,1)}, u32[]{:S(2)}, u32[]{:S(2)}) async-start(bf16[32,32,128]{2,1,0:T(8,128)(2,1)} %copy-done.25), calls=%async_computation.6 | async-start | bytes 524288 | tf_op jit(solution)/shard_map/all_to_all | solution.py:27
  250.8 6.1 %attend.3 = (bf16[32,32,128]{2,1,0:T(8,128)(2,1)S(1)}, f32[128,1024]{1,0:T(8,128)S(1)}, f32[8,1024]{1,0:T(8,128)S(1)}) custom-call(bf16[32,96,128]{2,1,0:T(8,128)(2,1)} %all-to-all-done.4.in_ref), custom_call_target="tpu_custom_call" | custom-call | flops 20000000000 | bytes 20000000 | tf_op jit(solution)/shard_map/attend/pallas_call | solution.py:206
  259.8 7.2 %all-to-all-start.5 = ((bf16[32,32,128]{2,1,0:T(8,128)(2,1)}), bf16[32,32,128]{2,1,0:T(8,128)(2,1)}, u32[]{:S(2)}, u32[]{:S(2)}) async-start(bf16[32,32,128]{2,1,0:T(8,128)(2,1)} %copy-done.26), calls=%async_computation.5 | async-start | bytes 524288 | tf_op jit(solution)/shard_map/all_to_all | solution.py:27
  268.8 9.4 %attend_back.2 = bf16[32,96,128]{2,1,0:T(8,128)(2,1)S(1)} custom-call(bf16[32,96,128]{2,1,0:T(8,128)(2,1)} %all-to-all-done.4.in_ref, bf16[32,32,128]{2,1,0:T(8,128)(2,1)} %all-to-all-done.6.grad_ref, f32[128,1024]{1,0:T(8,128)S(1)} %copy-done.47, f32[8,1024]{1,0:T(8,128)S(1)} %copy-done.51), custom_call_target="tpu_custom_call" | custom-call | flops 40000000000 | bytes 40000000 | tf_op jit(solution)/shard_map/attend_back/pallas_call | solution.py:229
  279.1 7.4 %all-to-all-start.7 = ((bf16[32,96,128]{2,1,0:T(8,128)(2,1)}), bf16[32,96,128]{2,1,0:T(8,128)(2,1)}, u32[]{:S(2)}, u32[]{:S(2)}) async-start(bf16[32,96,128]{2,1,0:T(8,128)(2,1)} %copy-done.14), calls=%async_computation.7 | async-start | bytes 1572864 | tf_op jit(solution)/shard_map/all_to_all | solution.py:27
  313.7 9.2 %all-to-all-start.8 = ((bf16[32,32,128]{2,1,0:T(8,128)(2,1)}), bf16[32,32,128]{2,1,0:T(8,128)(2,1)S(1)}, u32[]{:S(2)}, u32[]{:S(2)}) async-start(bf16[32,32,128]{2,1,0:T(8,128)(2,1)} %pull.3), calls=%async_computation.8 | async-start | bytes 524288 | tf_op jit(solution)/shard_map/all_to_all | solution.py:27
  348.6 9.2 %attend_back.3 = bf16[32,96,128]{2,1,0:T(8,128)(2,1)} custom-call(bf16[32,96,128]{2,1,0:T(8,128)(2,1)S(1)} %copy-done.12, bf16[32,32,128]{2,1,0:T(8,128)(2,1)S(1)} %all-to-all-done.8.grad_ref, f32[128,1024]{1,0:T(8,128)S(1)} %copy-done.45, f32[8,1024]{1,0:T(8,128)S(1)} %copy-done.49), custom_call_target="tpu_custom_call" | custom-call | flops 40000000000 | bytes 40000000 | tf_op jit(solution)/shard_map/attend_back/pallas_call | solution.py:229
  357.8 13.7 %all-to-all-start.9 = ((bf16[32,96,128]{2,1,0:T(8,128)(2,1)}), bf16[32,96,128]{2,1,0:T(8,128)(2,1)}, u32[]{:S(2)}, u32[]{:S(2)}) async-start(bf16[32,96,128]{2,1,0:T(8,128)(2,1)} %attend_back.3), calls=%async_computation.9 | async-start | bytes 1572864 | tf_op jit(solution)/shard_map/all_to_all | solution.py:27
  434.9 9.6 %all-to-all-start.11 = ((bf16[32,32,576]{2,1,0:T(8,128)(2,1)}), bf16[32,32,576]{2,1,0:T(8,128)(2,1)S(1)}, u32[]{:S(2)}, u32[]{:S(2)}) async-start(bf16[32,32,576]{2,1,0:T(8,128)(2,1)} %pad_maximum_fusion.1), calls=%async_computation.11 | async-start | bytes 2621440 | tf_op jit(solution)/shard_map/all_to_all | solution.py:27
  445.3 22.2 %all-to-all-done.11 = bf16[32,32,576]{2,1,0:T(8,128)(2,1)S(1)} async-done(((bf16[32,32,576]{2,1,0:T(8,128)(2,1)}), bf16[32,32,576]{2,1,0:T(8,128)(2,1)S(1)}, u32[]{:S(2)}, u32[]{:S(2)}) %all-to-all-start.11) | async-done | bytes 1179680 | tf_op jit(solution)/shard_map/all_to_all | solution.py:27
  468.8 5.5 all-to-all-start.12
  478.0 12.5 %all-to-all-done.12 = bf16[32,24,576]{2,1,0:T(8,128)(2,1)S(1)} async-done(((bf16[32,24,576]{2,1,0:T(8,128)(2,1)}), bf16[32,24,576]{2,1,0:T(8,128)(2,1)S(1)}, u32[]{:S(2)}, u32[]{:S(2)}) %all-to-all-start.12) | async-done | bytes 884768 | tf_op jit(solution)/shard_map/all_to_all | solution.py:27
  491.9 77.1 %all-reduce.5.cloned.1.call-done = (bf16[1,192,2304]{2,1,0:T(8,128)(2,1)}, bf16[1,192,768]{2,1,0:T(8,128)(2,1)}, bf16[1,192,768]{2,1,0:T(8,128)(2,1)}, bf16[1,19...) async-done(((bf16[1,192,2304]{2,1,0:T(8,128)(2,1)}, bf16[1,192,768]{2,1,0:T(8,128)(2,1)}, ...) | async-done | bytes 6193168 | tf_op jit(solution)/shard_map/psum | solution.py:560
  (481 shorter events, 275.0 us)
Async XLA Ops:
  7.2 148.0 %all-gather.3.cloned.1.call-start = ((), (), s32[]{:S(2)}) async-start(), calls=%async_computation.14 | async-start | bytes 2949120 | tf_op jit(solution)/shard_map/all_gather | solution.py:503
  35.0 170.8 %collective-permute-start.16 = (bf16[128,768]{1,0:T(8,128)(2,1)}, bf16[128,768]{1,0:T(8,128)(2,1)}, u32[]{:S(2)}, u32[]{:S(2)}) collective-permute-start(bf16[128,768]{1,0:T(8,128)(2,1)} %bitcast.33.g_ref), channel_id=1, source_target_pairs={{0,1},{1,2},{2,3},{3,0},{4,5},{5,6},{6,7},{7,4},{8,9},{9,10},{10,1... | collective-permute-start | bytes 589832 | tf_op jit(solution)/shard_map/ppermute | solution.py:32
  36.6 169.2 %collective-permute-start.17 = (bf16[128,768]{1,0:T(8,128)(2,1)}, bf16[128,768]{1,0:T(8,128)(2,1)}, u32[]{:S(2)}, u32[]{:S(2)}) collective-permute-start(bf16[128,768]{1,0:T(8,128)(2,1)} %bitcast.33.g_ref), channel_id=1, source_target_pairs={{0,2},{1,3},{2,0},{3,1},{4,6},{5,7},{6,4},{7,5},{8,10},{9,11},{10,... | collective-permute-start | bytes 589832 | tf_op jit(solution)/shard_map/ppermute | solution.py:32
  57.8 42.9 %all-to-all-start.3 = ((bf16[4,384,768]{2,1,0:T(8,128)(2,1)}), bf16[4,384,768]{2,1,0:T(8,128)(2,1)}, u32[]{:S(2)}, u32[]{:S(2)}) async-start(bf16[4,384,768]{2,1,0:T(8,128)(2,1)} %copy.90), calls=%async_computation.3 | async-start | bytes 4718592 | tf_op jit(solution)/shard_map/all_to_all | solution.py:27
  62.4 106.5 %all-gather.5.cloned.1.call-start = ((), (), s32[]{:S(2)}) async-start(), calls=%async_computation.15 | async-start | bytes 4423680 | tf_op jit(solution)/shard_map/all_gather | solution.py:502
  75.4 36.0 %collective-permute-start.4 = (bf16[128,768]{1,0:T(8,128)(2,1)S(1)}, bf16[128,768]{1,0:T(8,128)(2,1)}, u32[]{:S(2)}, u32[]{:S(2)}) collective-permute-start(bf16[128,768]{1,0:T(8,128)(2,1)S(1)} %get-tuple-element.57), channel_id=1, source_target_pairs={{0,1},{1,2},{2,3},{3,0},{4,5},{5,6},{6,7},{7,4},{8,9},{9,10},{10,1... | collective-permute-start | bytes 589832 | tf_op jit(solution)/shard_map/ppermute | solution.py:32
  77.1 40.5 %collective-permute-start.5 = (bf16[128,768]{1,0:T(8,128)(2,1)S(1)}, bf16[128,768]{1,0:T(8,128)(2,1)}, u32[]{:S(2)}, u32[]{:S(2)}) collective-permute-start(bf16[128,768]{1,0:T(8,128)(2,1)S(1)} %get-tuple-element.57), channel_id=1, source_target_pairs={{0,2},{1,3},{2,0},{3,1},{4,6},{5,7},{6,4},{7,5},{8,10},{9,11},{10,... | collective-permute-start | bytes 589832 | tf_op jit(solution)/shard_map/ppermute | solution.py:32
  79.5 38.1 %collective-permute-start.6 = (bf16[128,768]{1,0:T(8,128)(2,1)S(1)}, bf16[128,768]{1,0:T(8,128)(2,1)}, u32[]{:S(2)}, u32[]{:S(2)}) collective-permute-start(bf16[128,768]{1,0:T(8,128)(2,1)S(1)} %get-tuple-element.57), channel_id=1, source_target_pairs={{0,3},{1,0},{2,1},{3,2},{4,7},{5,4},{6,5},{7,6},{8,11},{9,8},{10,9... | collective-permute-start | bytes 589832 | tf_op jit(solution)/shard_map/ppermute | solution.py:32
  103.5 37.3 %all-to-all-start.1 = ((bf16[32,96,128]{2,1,0:T(8,128)(2,1)}), bf16[32,96,128]{2,1,0:T(8,128)(2,1)S(1)}, u32[]{:S(2)}, u32[]{:S(2)}) async-start(bf16[32,96,128]{2,1,0:T(8,128)(2,1)} %get-tuple-element.55), calls=%async_computation.1 | async-start | bytes 1572864 | tf_op jit(solution)/shard_map/all_to_all | solution.py:27
  194.2 40.0 %all-to-all-start.4 = ((bf16[32,96,128]{2,1,0:T(8,128)(2,1)}), bf16[32,96,128]{2,1,0:T(8,128)(2,1)}, u32[]{:S(2)}, u32[]{:S(2)}) async-start(bf16[32,96,128]{2,1,0:T(8,128)(2,1)} %copy-done.13), calls=%async_computation.4 | async-start | bytes 1572864 | tf_op jit(solution)/shard_map/all_to_all | solution.py:27
  200.4 171.1 %collective-permute-start.34 = (bf16[128,192]{1,0:T(8,128)(2,1)}, bf16[128,192]{1,0:T(8,128)(2,1)}, u32[]{:S(2)}, u32[]{:S(2)}) collective-permute-start(bf16[128,192]{1,0:T(8,128)(2,1)} %get-tuple-element.150), channel_id=1, source_target_pairs={{0,1},{1,2},{2,3},{3,0},{4,5},{5,6},{6,7},{7,4},{8,9},{9,10},{10,1... | collective-permute-start | bytes 147464 | tf_op jit(solution)/shard_map/ppermute | solution.py:32
  200.8 174.2 %collective-permute-start.35 = (bf16[128,192]{1,0:T(8,128)(2,1)}, bf16[128,192]{1,0:T(8,128)(2,1)}, u32[]{:S(2)}, u32[]{:S(2)}) collective-permute-start(bf16[128,192]{1,0:T(8,128)(2,1)} %get-tuple-element.149), channel_id=1, source_target_pairs={{0,2},{1,3},{2,0},{3,1},{4,6},{5,7},{6,4},{7,5},{8,10},{9,11},{10,... | collective-permute-start | bytes 147464 | tf_op jit(solution)/shard_map/ppermute | solution.py:32
  226.3 60.2 %collective-permute-start.43 = (bf16[192,768]{1,0:T(8,128)(2,1)}, bf16[192,768]{1,0:T(8,128)(2,1)}, u32[]{:S(2)}, u32[]{:S(2)}) collective-permute-start(bf16[192,768]{1,0:T(8,128)(2,1)} %get-tuple-element.123), channel_id=1, source_target_pairs={{0,1},{1,2},{2,3},{3,0},{4,5},{5,6},{6,7},{7,4},{8,9},{9,10},{10,1... | collective-permute-start | bytes 884744 | tf_op jit(solution)/shard_map/ppermute | solution.py:32
  230.2 58.0 %collective-permute-start.44 = (bf16[192,768]{1,0:T(8,128)(2,1)}, bf16[192,768]{1,0:T(8,128)(2,1)}, u32[]{:S(2)}, u32[]{:S(2)}) collective-permute-start(bf16[192,768]{1,0:T(8,128)(2,1)} %get-tuple-element.122), channel_id=1, source_target_pairs={{0,2},{1,3},{2,0},{3,1},{4,6},{5,7},{6,4},{7,5},{8,10},{9,11},{10,... | collective-permute-start | bytes 884744 | tf_op jit(solution)/shard_map/ppermute | solution.py:32
  231.3 65.1 %collective-permute-start.45 = (bf16[192,768]{1,0:T(8,128)(2,1)}, bf16[192,768]{1,0:T(8,128)(2,1)}, u32[]{:S(2)}, u32[]{:S(2)}) collective-permute-start(bf16[192,768]{1,0:T(8,128)(2,1)} %get-tuple-element.121), channel_id=1, source_target_pairs={{0,3},{1,0},{2,1},{3,2},{4,7},{5,4},{6,5},{7,6},{8,11},{9,8},{10,9... | collective-permute-start | bytes 884744 | tf_op jit(solution)/shard_map/ppermute | solution.py:32
  313.7 34.9 %all-to-all-start.8 = ((bf16[32,32,128]{2,1,0:T(8,128)(2,1)}), bf16[32,32,128]{2,1,0:T(8,128)(2,1)S(1)}, u32[]{:S(2)}, u32[]{:S(2)}) async-start(bf16[32,32,128]{2,1,0:T(8,128)(2,1)} %pull.3), calls=%async_computation.8 | async-start | bytes 524288 | tf_op jit(solution)/shard_map/all_to_all | solution.py:27
  323.2 53.2 %collective-permute-start.36 = (bf16[128,192]{1,0:T(8,128)(2,1)}, bf16[128,192]{1,0:T(8,128)(2,1)}, u32[]{:S(2)}, u32[]{:S(2)}) collective-permute-start(bf16[128,192]{1,0:T(8,128)(2,1)} %get-tuple-element.148), channel_id=1, source_target_pairs={{0,3},{1,0},{2,1},{3,2},{4,7},{5,4},{6,5},{7,6},{8,11},{9,8},{10,9... | collective-permute-start | bytes 147464 | tf_op jit(solution)/shard_map/ppermute | solution.py:32
  341.7 37.4 %collective-permute-start.25 = (bf16[128,768]{1,0:T(8,128)(2,1)}, bf16[128,768]{1,0:T(8,128)(2,1)}, u32[]{:S(2)}, u32[]{:S(2)}) collective-permute-start(bf16[128,768]{1,0:T(8,128)(2,1)} %get-tuple-element.127), channel_id=1, source_target_pairs={{0,3},{1,0},{2,1},{3,2},{4,7},{5,4},{6,5},{7,6},{8,11},{9,8},{10,9... | collective-permute-start | bytes 589832 | tf_op jit(solution)/shard_map/ppermute | solution.py:32
  343.4 37.5 %collective-permute-start.26 = (bf16[128,768]{1,0:T(8,128)(2,1)}, bf16[128,768]{1,0:T(8,128)(2,1)}, u32[]{:S(2)}, u32[]{:S(2)}) collective-permute-start(bf16[128,768]{1,0:T(8,128)(2,1)} %get-tuple-element.129), channel_id=1, source_target_pairs={{0,1},{1,2},{2,3},{3,0},{4,5},{5,6},{6,7},{7,4},{8,9},{9,10},{10,1... | collective-permute-start | bytes 589832 | tf_op jit(solution)/shard_map/ppermute | solution.py:32
  357.8 29.8 %all-to-all-start.9 = ((bf16[32,96,128]{2,1,0:T(8,128)(2,1)}), bf16[32,96,128]{2,1,0:T(8,128)(2,1)}, u32[]{:S(2)}, u32[]{:S(2)}) async-start(bf16[32,96,128]{2,1,0:T(8,128)(2,1)} %attend_back.3), calls=%async_computation.9 | async-start | bytes 1572864 | tf_op jit(solution)/shard_map/all_to_all | solution.py:27
  376.4 43.9 %collective-permute-start.41 = (bf16[192,768]{1,0:T(8,128)(2,1)}, bf16[192,768]{1,0:T(8,128)(2,1)}, u32[]{:S(2)}, u32[]{:S(2)}) collective-permute-start(bf16[192,768]{1,0:T(8,128)(2,1)} %get-tuple-element.118), channel_id=1, source_target_pairs={{0,2},{1,3},{2,0},{3,1},{4,6},{5,7},{6,4},{7,5},{8,10},{9,11},{10,... | collective-permute-start | bytes 884744 | tf_op jit(solution)/shard_map/ppermute | solution.py:32
  379.1 42.9 %collective-permute-start.42 = (bf16[192,768]{1,0:T(8,128)(2,1)}, bf16[192,768]{1,0:T(8,128)(2,1)}, u32[]{:S(2)}, u32[]{:S(2)}) collective-permute-start(bf16[192,768]{1,0:T(8,128)(2,1)} %get-tuple-element.117), channel_id=1, source_target_pairs={{0,3},{1,0},{2,1},{3,2},{4,7},{5,4},{6,5},{7,6},{8,11},{9,8},{10,9... | collective-permute-start | bytes 884744 | tf_op jit(solution)/shard_map/ppermute | solution.py:32
  420.2 148.8 %all-reduce.5.cloned.1.call-start = ((), (), s32[]{:S(2)}) async-start(), calls=%async_computation.16 | async-start | bytes 12386304 | tf_op jit(solution)/shard_map/psum | solution.py:560
  434.9 32.5 %all-to-all-start.11 = ((bf16[32,32,576]{2,1,0:T(8,128)(2,1)}), bf16[32,32,576]{2,1,0:T(8,128)(2,1)S(1)}, u32[]{:S(2)}, u32[]{:S(2)}) async-start(bf16[32,32,576]{2,1,0:T(8,128)(2,1)} %pad_maximum_fusion.1), calls=%async_computation.11 | async-start | bytes 2621440 | tf_op jit(solution)/shard_map/all_to_all | solution.py:27
  (138 other events, 2088.2 us)
Sparse Core Ops, SparseCore 0:
  35.1 37.2 all-gather.2
  74.1 63.5 all-gather.4
  427.4 141.5 all-reduce.4

commit v3 on v2

--- a/solution.py
+++ b/solution.py
@@ -155,7 +155,7 @@
     out_ref[...] = full_ref[...].T.astype(BF16).reshape(count, BLK, 128)
 
 
-def backward_kernel(in_ref, grad_ref, full_ref, lse_ref, out_ref, q_scr, k_scr, kt_scr, v_scr, do_scr, delta_scr, dq_scr, dk_scr, dv_scr):
+def backward_kernel(in_ref, grad_ref, full_ref, lse_ref, carry_ref, out_ref, q_scr, k_scr, kt_scr, v_scr, do_scr, delta_scr, dq_scr, dk_scr, dv_scr):
     count = in_ref.shape[0]
     size = count * BLK
     grads = grad_ref[...].reshape(size, 128)
@@ -196,6 +196,8 @@
     for half in range(2):
         both = jnp.concatenate([queries[:, half * 64 : (half + 1) * 64], dk_scr[half]], axis=1)
         out_ref[:, half * BLK : (half + 1) * BLK, :] = both.astype(BF16).reshape(count, BLK, 128)
+    if carry_ref.shape[1] > 8:
+        out_ref[:, 3 * BLK :, :] = carry_ref[...]
     both = jnp.concatenate([dv_scr[0], dv_scr[1]], axis=1)
     out_ref[:, 2 * BLK : 3 * BLK, :] = both.astype(BF16).reshape(count, BLK, 128)
 
@@ -223,13 +225,14 @@
     )(packed)
 
 
-def attend_back(packed, grads, full, lse):
+def attend_back(packed, grads, full, lse, carry):
+    extra = carry.shape[1] if carry.shape[1] > 8 else 0
     count = packed.shape[0]
     size = count * BLK
     return pl.pallas_call(
         backward_kernel,
-        out_shape=jax.ShapeDtypeStruct((count, 3 * BLK, 128), BF16),
-        in_specs=[pl.BlockSpec(memory_space=pltpu.VMEM)] * 4,
+        out_shape=jax.ShapeDtypeStruct((count, 3 * BLK + extra, 128), BF16),
+        in_specs=[pl.BlockSpec(memory_space=pltpu.VMEM)] * 5,
         out_specs=pl.BlockSpec(memory_space=pltpu.VMEM),
         scratch_shapes=[
             pltpu.VMEM((2, size, 64), BF16),
@@ -245,7 +248,7 @@
         compiler_params=pltpu.CompilerParams(vmem_limit_bytes=48 << 20),
         cost_estimate=pl.CostEstimate(flops=40_000_000_000, bytes_accessed=40_000_000, transcendentals=2_600_000),
         name="attend_back",
-    )(packed, grads, full, lse)
+    )(packed, grads, full, lse, carry)
 
 
 def kernel_turn(value, tables, sign):
@@ -260,14 +263,16 @@
     return value[rows, index * HEAD_DIM : (index + 1) * HEAD_DIM]
 
 
-def mix_kernel(x_ref, gain_ref, shift_ref, w_ref, bq_ref, bv_ref, cos_ref, up_ref, down_ref, xhat_ref, low_ref, scale_ref, out_ref):
+def mix_kernel(x_ref, gain_ref, shift_ref, w_ref, bq_ref, bv_ref, cos_ref, up_ref, down_ref, extra_ref, xhat_ref, send_ref, scale_ref, out_ref):
     x = x_ref[...]
     rows, width = x.shape
     centred = x - jnp.mean(x, axis=-1, keepdims=True)
     scale = lax.rsqrt(jnp.mean(centred * centred, axis=-1, keepdims=True) + EPS)
     xhat = centred * scale
     xhat_ref[...] = xhat
-    low_ref[...] = xhat.astype(BF16)
+    for block in range(send_ref.shape[0]):
+        send_ref[block, :, :width] = xhat.astype(BF16)
+        send_ref[block, :, width:] = extra_ref[block]
     scale_ref[...] = jnp.broadcast_to(scale, scale_ref.shape)
     normed = (xhat * gain_ref[...] + shift_ref[...]).astype(BF16)
     tables = (cos_ref[...], up_ref[...], down_ref[...])
@@ -306,16 +311,16 @@
     return jax.ShapeDtypeStruct(shape, dtype)
 
 
-def mix(x, w, tables):
+def mix(x, w, tables, extra):
     rows, width = x.shape
     count = lax.axis_size("ctx")
     shapes = (
         shaped((rows, width), F32),
-        shaped((rows, width), BF16),
+        shaped((extra.shape[0], rows, width + extra.shape[2]), BF16),
         shaped((rows, 128), F32),
         shaped((count, 3 * BLK, 128), BF16),
     )
-    return on_chip(mix_kernel, shapes, "mix", 5_000_000_000, x, w["g_attn"], w["s_attn"], w["qkv"], w["b_q"], w["b_v"], *tables)
+    return on_chip(mix_kernel, shapes, "mix", 5_000_000_000, x, w["g_attn"], w["s_attn"], w["qkv"], w["b_q"], w["b_v"], *tables, extra)
 
 
 def join_kernel(tile_ref, x_ref, mlp_ref, w_ref, bias_ref, split_ref, out_ref, context):
@@ -367,7 +372,7 @@
             parts[part].append(jnp.concatenate(row, axis=1))
         for half in range(2):
             lanes = slice(half * HEAD_DIM, (half + 1) * HEAD_DIM)
-            row = [tile_ref[s * HEADS + h, 2 * BLK :, lanes] for h in range(HEADS)]
+            row = [tile_ref[s * HEADS + h, 2 * BLK : 3 * BLK, lanes] for h in range(HEADS)]
             parts[2].append(jnp.concatenate(row, axis=1))
     query, key, value = (jnp.concatenate(part, axis=0) for part in parts)
     mixed_ref[:, :width] = kernel_turn(query.astype(F32), tables, -1.0).astype(BF16)
@@ -389,7 +394,7 @@
     return on_chip(unmix_kernel, shapes, "unmix", 500_000_000, tiles, *tables)
 
 
-def norm_kernel(mixed_ref, w_ref, g_ref, mlp_ref, xhat_ref, scale_ref, ga_ref, gm_ref, out_ref, low_ref, sums_ref):
+def norm_kernel(mixed_ref, w_ref, g_ref, mlp_ref, xhat_ref, scale_ref, ga_ref, gm_ref, split_ref, context_ref, out_ref, low_ref, send_ref, sums_ref):
     attn = dot(mixed_ref[...], w_ref[...], NT)
     mlp, xhat, g = mlp_ref[...], xhat_ref[...], g_ref[...]
     both = attn * ga_ref[...] + mlp * gm_ref[...]
@@ -397,16 +402,26 @@
     new = g + scale_ref[:, :1] * inner
     out_ref[...] = new
     low_ref[...] = new.astype(BF16)
+    if send_ref.shape[0] == 4:
+        width = new.shape[1]
+        size, rest = split_ref.shape[2], context_ref.shape[2]
+        send_ref[...] = jnp.zeros_like(send_ref)
+        for block in range(4):
+            send_ref[block, :, :width] = new.astype(BF16)
+            send_ref[block, :, width : width + size] = split_ref[block]
+            send_ref[block, :, send_ref.shape[2] - rest :] = context_ref[block]
     sums_ref[...] = jnp.zeros_like(sums_ref)
     for row, value in enumerate((attn * xhat, attn, mlp * xhat, mlp, g.astype(BF16).astype(F32))):
         sums_ref[row : row + 1, :] = jnp.sum(value, axis=0, keepdims=True)
 
 
-def norm_backward(g, mixed, grad_n_mlp, xhat, scale, w):
+def norm_backward(g, mixed, grad_n_mlp, xhat, scale, w, split, context, send):
     rows, width = g.shape
-    shapes = (shaped((rows, width), F32), shaped((rows, width), BF16), shaped((8, width), F32))
+    size = -(-split.shape[2] // 128) * 128
+    sent = (4, rows, width + size + context.shape[2]) if send else (1, 8, 128)
+    shapes = (shaped((rows, width), F32), shaped((rows, width), BF16), shaped(sent, BF16), shaped((8, width), F32))
     return on_chip(
-        norm_kernel, shapes, "norm_back", 1_500_000_000, mixed, w["qkv"], g, grad_n_mlp, xhat, scale, w["g_attn"], w["g_mlp"]
+        norm_kernel, shapes, "norm_back", 1_500_000_000, mixed, w["qkv"], g, grad_n_mlp, xhat, scale, w["g_attn"], w["g_mlp"], split, context
     )
 
 
@@ -447,10 +462,12 @@
     n_mlp_all = (xhat_all.astype(F32) * w["g_mlp"] + w["s_mlp"]).astype(BF16)
     hidden = dot(n_mlp_all, w["up"]) + w["b_up"]
     active = (hidden * cdf(hidden)).astype(BF16)
-    partial = dot(active, w["down"])
+    return n_mlp_all, hidden, active, dot(active, w["down"])
+
+
+def own_sum(partial):
     rows = partial.shape[0] // 4
-    total = group_sum([partial[i * rows : (i + 1) * rows] for i in range(4)])
-    return n_mlp_all, hidden, active, total
+    return group_sum([partial[i * rows : (i + 1) * rows] for i in range(4)])
 
 
 def mlp_backward(g_all, n_mlp_all, hidden, active, w):
@@ -458,13 +475,10 @@
     density = jnp.exp(-0.5 * hidden * hidden) * 0.3989422804014327
     grad_hidden = (grad_active * (cdf(hidden) + hidden * density)).astype(BF16)
     partial = dot(grad_hidden, w["up"], NT)
-    rows = partial.shape[0] // 4
-    grad_n_mlp = group_sum([partial[i * rows : (i + 1) * rows] for i in range(4)])
     grad_down = dot(active, g_all, TN).astype(BF16)
     grad_up = dot(n_mlp_all, grad_hidden, TN).astype(BF16)
     grad_b_up = jnp.sum(grad_hidden.astype(F32), axis=0)
-    grad_up = place(group_trade(grad_up.reshape(4, -1, grad_up.shape[1])), 1)
-    return grad_n_mlp, grad_down, grad_up, grad_b_up
+    return partial, grad_down, grad_up.reshape(4, -1, grad_up.shape[1]), grad_b_up
 
 
 def small_sums(sums, mixed_sums):
@@ -498,11 +512,11 @@
         {"g_attn": ln_gain_attn, "s_attn": ln_shift_attn, "g_mlp": ln_gain_mlp, "s_mlp": ln_shift_mlp, "b_qv": b_qv, "b_out": b_out, "b_down": b_down}
     )
     half1 = gather_half(w_qkv[0])
-    later_out, later_qkv = after((w_out, w_qkv[1]), half1)
+    later_out, later_qkv, later_up = after((w_out, w_qkv[1], w_up), half1)
     qkv = [gather_rest(half1), lax.all_gather(later_qkv, "wt", axis=0, tiled=True)]
     out_both = lax.all_gather(later_out, "wt", axis=1, tiled=True)
-    ups = w_up.reshape(LAYERS * depth, 4, unit).transpose(1, 0, 2)
-    ups = exchange(ups, "wt").reshape(4, LAYERS, depth, unit).transpose(1, 0, 2, 3).reshape(LAYERS, width, unit)
+    ups = jnp.stack([later_up[:, :, i * unit : (i + 1) * unit] for i in range(4)])
+    ups = place([b[:, None] for b in group_trade(ups)], 1).reshape(LAYERS, width, unit)
     layers = []
     for layer in range(LAYERS):
         w = {name: small[name][layer][None] for name in small}
@@ -517,47 +531,56 @@
     first, second = layers
     g2 = cotangent.reshape(rows, width)
     x1 = tokens_in.reshape(rows, width).astype(F32)
-    xhat1, low1, scale1, packed1 = mix(x1, first, tables)
+    xhat1, send1, scale1, packed1 = mix(x1, first, tables, g2[None])
     packed1 = exchange(packed1, "ctx")
-    xhat1_all = jnp.concatenate(group_spread(low1), axis=0)
-    n_mlp1, hidden1, active1, mlp1 = mlp_forward(xhat1_all, first)
+    landed1 = jnp.concatenate(group_spread(send1[0]), axis=0)
+    xhat1_all, g2_all = landed1[:, :width], landed1[:, width:]
+    n_mlp1, hidden1, active1, partial1 = mlp_forward(xhat1_all, first)
+    mlp1 = own_sum(partial1)
     out1, full1, lse1 = attend(packed1)
-    out1 = exchange(out1, "ctx")
+    both1 = exchange(jnp.concatenate([out1, pull(g2, second)], axis=1), "ctx")
+    out1, grads2 = both1[:, :BLK], both1[:, BLK:]
     split1, x2 = join(out1, x1, mlp1, first)
-    xhat2, low2, scale2, packed2 = mix(x2, second, tables)
+    xhat2, send2, scale2, packed2 = mix(x2, second, tables, split1)
     packed2 = exchange(packed2, "ctx")
-    grads2 = exchange(pull(g2, second), "ctx")
-    xhat2_all = jnp.concatenate(group_spread(low2), axis=0)
-    n_mlp2, hidden2, active2, mlp2 = mlp_forward(xhat2_all, second)
+    landed2 = jnp.concatenate(group_trade(send2), axis=0)
+    xhat2_all, context1_all = landed2[:, :width], landed2[:, width:]
+    n_mlp2, hidden2, active2, partial2 = mlp_forward(xhat2_all, second)
     out2, full2, lse2 = attend(packed2)
-    back2 = exchange(attend_back(packed2, grads2, full2, lse2), "ctx")
-    g2_all = jnp.concatenate(group_spread(g2), axis=0)
-    grad_n_mlp2, grad_down2, grad_up2, grad_b_up2 = mlp_backward(g2_all, n_mlp2, hidden2, active2, second)
+    back2 = exchange(attend_back(packed2, grads2, full2, lse2, out2), "ctx")
+    back_partial2, grad_down2, grad_up2, grad_b_up2 = mlp_backward(g2_all, n_mlp2, hidden2, active2, second)
+    sums = own_sum(jnp.concatenate([partial2, back_partial2], axis=1))
+    mlp2, grad_n_mlp2 = sums[:, :width], sums[:, width:]
+    split2, x3 = join(back2[:, 3 * BLK :], x2, mlp2, second)
+    out_tokens = x3.astype(BF16).reshape(tokens_in.shape)
     mixed2, mixed2_split, mixed_sums2 = unmix(back2, tables)
-    g1, g1_low, sums2 = norm_backward(g2.astype(F32), mixed2, grad_n_mlp2, xhat2, scale2, second)
+    g1, g1_low, send3, sums2 = norm_backward(g2.astype(F32), mixed2, grad_n_mlp2, xhat2, scale2, second, mixed2_split, split2, True)
     grads1 = exchange(pull(g1_low, first), "ctx")
-    g1_all = jnp.concatenate(group_spread(g1_low), axis=0)
-    grad_n_mlp1, grad_down1, grad_up1, grad_b_up1 = mlp_backward(g1_all, n_mlp1, hidden1, active1, first)
-    back1 = exchange(attend_back(packed1, grads1, full1, lse1), "ctx")
-    out2 = exchange(out2, "ctx")
-    split2, x3 = join(out2, x2, mlp2, second)
-    out_tokens = x3.astype(BF16).reshape(tokens_in.shape)
-    context1_all = jnp.concatenate(group_trade(split1), axis=0)
-    context2_all = jnp.concatenate(group_trade(split2), axis=0)
+    landed3 = jnp.concatenate(group_trade(send3), axis=0)
+    columns = mixed2_split.shape[2]
+    g1_all, mixed2_all, context2_all = landed3[:, :width], landed3[:, width : width + columns], landed3[:, -depth:]
+    back_partial1, grad_down1, grad_up1, grad_b_up1 = mlp_backward(g1_all, n_mlp1, hidden1, active1, first)
+    grad_n_mlp1 = own_sum(back_partial1)
+    back1 = exchange(attend_back(packed1, grads1, full1, lse1, lse1[None].astype(BF16)), "ctx")
+    grad_up1 = place([b[None] for b in group_trade(grad_up1)], 0).reshape(width, unit)
+    grad_out1 = dot(context1_all, g1_all, TN).astype(BF16)
     grad_out2 = dot(context2_all, g2_all, TN).astype(BF16)
-    mixed2_all = jnp.concatenate(group_trade(mixed2_split), axis=0)
-    grad_out1 = dot(context1_all, g1_all, TN).astype(BF16)
     n_attn2_all = (xhat2_all.astype(F32) * second["g_attn"] + second["s_attn"]).astype(BF16)
     grad_qkv2 = dot(n_attn2_all, mixed2_all, TN).astype(BF16)
+    traded2 = group_trade(jnp.concatenate([grad_up2, grad_qkv2.reshape(4, depth, columns)], axis=2))
+    space = jnp.zeros((width, width - columns), BF16)
+    parts2 = [grad_down2, grad_out2] + [b[:, :unit] for b in traded2]
+    tall2 = jnp.concatenate(parts2 + [jnp.concatenate([jnp.concatenate([b[:, unit:] for b in traded2], axis=0), space], axis=1)], axis=0)
+    back1, tall2 = lax.optimization_barrier((back1, tall2))
+    tall2 = lax.psum_scatter(tall2.reshape(devices, -1, width), "ctx", scatter_dimension=0, tiled=False)
+    wide1 = jnp.concatenate([grad_down1, grad_up1, grad_out1], axis=0)
+    wide1 = exchange(wide1.reshape(devices, -1, width), "ctx").astype(F32).sum(0).astype(BF16)
     mixed1, mixed1_split, mixed_sums1 = unmix(back1, tables)
     mixed1_all = jnp.concatenate(group_trade(mixed1_split), axis=0)
     n_attn1_all = (xhat1_all.astype(F32) * first["g_attn"] + first["s_attn"]).astype(BF16)
     grad_qkv1 = dot(n_attn1_all, mixed1_all, TN).astype(BF16)
-    g0, _, sums1 = norm_backward(g1, mixed1, grad_n_mlp1, xhat1, scale1, first)
+    g0, _, _, sums1 = norm_backward(g1, mixed1, grad_n_mlp1, xhat1, scale1, first, mixed2_split, split2, False)
     small1, small2 = small_sums(sums1, mixed_sums1), small_sums(sums2, mixed_sums2)
-    columns = grad_qkv2.shape[1]
-    moved2 = exchange(grad_qkv2.reshape(4, depth, columns), "wt")
-    wide = lax.psum((grad_down1, grad_up1, grad_out1, grad_down2, grad_up2, grad_out2, moved2), "ctx")
     smalls, hidden_sums = (small1, small2), (grad_b_up1, grad_b_up2)
     piece = width // devices
 
@@ -569,15 +592,32 @@
         return padded.reshape(value.shape[0], lines, columns)
 
     tiny = to_rows(jnp.concatenate(smalls, axis=1).astype(BF16))
-    moved = exchange(jnp.concatenate([grad_qkv1.reshape(4, depth, columns), tiny], axis=1), "wt")
+    moved = group_trade(jnp.concatenate([grad_qkv1.reshape(4, depth, columns), tiny], axis=1))
+    moved = place([b[None] for b in moved], 0)
     tiny_size = small1.shape[1]
     small_sum = moved[:, depth:].astype(F32).sum(0).reshape(1, -1)[:, : LAYERS * tiny_size]
     tail = to_rows(jnp.concatenate([small_sum, *(u[None] for u in hidden_sums)], axis=1).astype(BF16))
     sent = jnp.concatenate(
         [moved[:, :depth].reshape(devices, piece, columns), jnp.broadcast_to(tail, (devices,) + tail.shape[1:])], axis=1
     )
-    landed = exchange(sent, "ctx").astype(F32).sum(0)
-    moved1 = spread(landed[:piece].astype(BF16), "ctx").reshape(4, depth, columns)
+    landed = exchange(after(sent, wide1), "ctx").astype(F32).sum(0)
+    lines = wide1.shape[0]
+    tall2 = after(tall2, landed)
+    tall2 = lax.all_gather(tall2, "ctx", axis=0).reshape(-1, width)
+    wide2 = (tall2[:unit], tall2[unit : unit + depth])
+    traded_up2 = tall2[unit + depth : unit + depth + width].reshape(4, depth, unit)
+    traded_qkv2 = tall2[unit + depth + width :, :columns].reshape(4, depth, columns)
+    last = jnp.pad(landed[:piece].astype(BF16), ((0, 0), (0, width - columns)))
+    last = spread(jnp.concatenate([wide1, last], axis=0), "ctx")
+    wide1 = last[:, :lines].reshape(-1, width)
+    moved1 = last[:, lines:, :columns].reshape(4, depth, columns)
+    up1 = wide1[unit : unit + width].reshape(4, depth, unit)
+    up2 = place([traded_up2[i : i + 1] for i in range(4)], 0)
+    qkv2 = place([traded_qkv2[i : i + 1] for i in range(4)], 0)
+
+    def side_by_side(blocks):
+        return blocks.transpose(1, 0, 2).reshape(depth, -1)
+
     flat = landed[piece:].reshape(-1)
     per_layer = [flat[layer * tiny_size : (layer + 1) * tiny_size] for layer in range(LAYERS)]
     at = LAYERS * tiny_size
@@ -591,7 +631,7 @@
 
     grad_bias = vector(4)
     grad_b_qv = jnp.stack([v[5 * depth :] for v in per_layer])
-    grad_qkv = both(*(m.transpose(1, 0, 2).reshape(depth, -1) for m in (moved1, wide[6])))
+    grad_qkv = both(side_by_side(moved1), side_by_side(qkv2))
     return (
         out_tokens,
         g0.reshape(tokens_in.shape),
@@ -601,11 +641,11 @@
         vector(3),
         grad_qkv,
         grad_b_qv,
-        both(wide[2], wide[5]),
+        both(wide1[unit + width :], wide2[1]),
         grad_bias,
-        both(wide[1], wide[4]),
+        both(side_by_side(up1), side_by_side(up2)),
         grad_b_up,
-        both(wide[0], wide[3]),
+        both(wide1[:unit], wide2[0]),
         grad_bias,
     )
 

time: 598 us -> 607 us (1.015)
  starting transfers between devices: 168 us -> 122 us
  local copies, waits for them, and re-layouts: 86.1 us -> 130 us
  blocking collectives: 0 us -> 27.2 us
  waiting for transfers between devices: 203 us -> 188 us
  other arithmetic: 29 us -> 36.7 us
    psum x1 -> x0, waiting for transfers between devices: 77.1 us -> none  [local(): lax.psum((grad_down1, grad_up1, grad_out1, grad_down2, grad_up2, grad_out...]
    ppermute x45 -> x36, waiting for transfers between devices: 57.8 us -> 119 us  [pass_on(): lax.ppermute(value, 'wt', [(i, (i + shift) % count) for i in range(count)])]
    all_to_all x14 -> x9, starting transfers between devices: 106 us -> 74 us  [exchange(): return lax.all_to_all(chunks, axis, 0, 0, tiled=True)]
    all_to_all x0 -> x1, blocking collectives: none -> 27.2 us  [exchange(): return lax.all_to_all(chunks, axis, 0, 0, tiled=True)]
    dynamic_update_slice x9 -> x22, local copies, waits for them, and re-layouts: 10.4 us -> 26.2 us  [place(): lax.dynamic_update_slice_in_dim(whole, blocks[shift], (here - shift) % 4...]
    ppermute x45 -> x36, starting transfers between devices: 60.3 us -> 45.7 us  [pass_on(): lax.ppermute(value, 'wt', [(i, (i + shift) % count) for i in range(count)])]
    slice x5 -> x16, local copies, waits for them, and re-layouts: 0.95 us -> 14.2 us  [the longest x3 3.04 us: own_sum(): return group_sum([partial[i * rows:(i + 1) * rows] for i in range(4)])]
    concatenate x1 -> x7, other arithmetic: 1.05 us -> 7.67 us  [the longest x1 1.68 us: local(): wide1 = jnp.concatenate([grad_down1, grad_up1, grad_out1], axis=0)]
  transfers between devices with their start and end apart: 63 -> 50, of which waited for: 25 -> 23; matrix products, arithmetic and copies ran while one was open for 19% -> 21% of each run, Pallas kernels for 9% -> 6%
where the time goes in v3:
time: 607 us; the launch traced here: 597 us
  waiting for transfers between devices  188 us (31%)
  local copies, waits for them, and re-layouts  130 us (21%)
  starting transfers between devices  122 us (20%)
  Pallas kernels  46.1 us (8%)
  other arithmetic  36.7 us (6%)
  matrix products  30.5 us (5%)
  blocking collectives  27.2 us (4%)
  between operations  15.7 us (3%)
    ppermute x36, waiting for transfers between devices, pass_on(): lax.ppermute(value, 'wt', [(i, (i + shift) % count) for i in range(count)])  119 us
    all_to_all x9, starting transfers between devices, exchange(): return lax.all_to_all(chunks, axis, 0, 0, tiled=True)  74 us
    all_to_all x9, waiting for transfers between devices, exchange(): return lax.all_to_all(chunks, axis, 0, 0, tiled=True)  68.6 us
    ppermute x36, starting transfers between devices, pass_on(): lax.ppermute(value, 'wt', [(i, (i + shift) % count) for i in range(count)])  45.7 us
    dot_general x16, matrix products, dot(): return lax.dot_general(left, right, dims, preferred_element_type=F32)  30.5 us
    unnamed x244, local copies, waits for them, and re-layouts  30.3 us
    all_to_all x1, blocking collectives, exchange(): return lax.all_to_all(chunks, axis, 0, 0, tiled=True)  27.2 us
    dynamic_update_slice x22, local copies, waits for them, and re-layouts, place(): lax.dynamic_update_slice_in_dim(whole, blocks[shift], (here - shift) % 4...  26.2 us
  transfers between devices with their start and end apart: 50, of which 23 were waited for; matrix products, arithmetic and copies ran while one was open for 21% of the time, Pallas kernels for 6%

profile of v3, /device:TPU:1, one launch (start us, length us, event | category | flops | bytes accessed | tf_op | source)
XLA Modules:
  0.0 596.9 jit_solution(13970818657609289484)
XLA Ops:
  18.4 8.0 %collective-permute-done = bf16[96,2304]{1,0:T(8,128)(2,1)S(1)} collective-permute-done((bf16[96,2304]{1,0:T(8,128)(2,1)S(1)}, bf16[96,2304]{1,0:T(8,128)(2,1)S(1)}, u32[]{:S(2)}, u32[]{:S(2)}) %collective-permute-start) | collective-permute-done | bytes 442400 | tf_op jit(solution)/shard_map/ppermute | solution.py:32
  27.2 9.5 %collective-permute-done.1 = bf16[96,2304]{1,0:T(8,128)(2,1)S(1)} collective-permute-done((bf16[96,2304]{1,0:T(8,128)(2,1)S(1)}, bf16[96,2304]{1,0:T(8,128)(2,1)S(1)}, u32[]{:S(2)}, u32[]{:S(2)}) %collective-permute-start.1) | collective-permute-done | bytes 442400 | tf_op jit(solution)/shard_map/ppermute | solution.py:32
  59.9 24.4 %collective-permute-done.7 = bf16[2,192,768]{2,1,0:T(8,128)(2,1)S(1)} collective-permute-done((bf16[2,192,768]{2,1,0:T(8,128)(2,1)}, bf16[2,192,768]{2,1,0:T(8,128)(2,1)S(1)}, u32[]{:S(2)}, u32[]{:S(2)}) %collective-permute-start.7) | collective-permute-done | bytes 589856 | tf_op jit(solution)/shard_map/ppermute | solution.py:32
  84.3 13.3 %collective-permute-done.8 = bf16[2,192,768]{2,1,0:T(8,128)(2,1)} collective-permute-done((bf16[2,192,768]{2,1,0:T(8,128)(2,1)}, bf16[2,192,768]{2,1,0:T(8,128)(2,1)}, u32[]{:S(2)}, u32[]{:S(2)}) %collective-permute-start.8) | collective-permute-done | bytes 589856 | tf_op jit(solution)/shard_map/ppermute | solution.py:32
  111.1 19.2 %all-to-all-start.1 = ((bf16[32,96,128]{2,1,0:T(8,128)(2,1)}), bf16[32,96,128]{2,1,0:T(8,128)(2,1)S(1)}, u32[]{:S(2)}, u32[]{:S(2)}) async-start(bf16[32,96,128]{2,1,0:T(8,128)(2,1)} %get-tuple-element.61), calls=%async_computation.1 | async-start | bytes 1572864 | tf_op jit(solution)/shard_map/all_to_all | solution.py:27
  131.6 8.8 %collective-permute-done.5 = bf16[128,1536]{1,0:T(8,128)(2,1)} collective-permute-done((bf16[128,1536]{1,0:T(8,128)(2,1)S(1)}, bf16[128,1536]{1,0:T(8,128)(2,1)}, u32[]{:S(2)}, u32[]{:S(2)}) %collective-permute-start.5) | collective-permute-done | bytes 393248 | tf_op jit(solution)/shard_map/ppermute | solution.py:32
  151.2 4.9 attend.2
  162.0 8.9 %all-to-all-start.2 = ((bf16[32,64,128]{2,1,0:T(8,128)(2,1)}), bf16[32,64,128]{2,1,0:T(8,128)(2,1)}, u32[]{:S(2)}, u32[]{:S(2)}) async-start(bf16[32,64,128]{2,1,0:T(8,128)(2,1)} %pad_maximum_fusion.10), calls=%async_computation.2 | async-start | bytes 1048576 | tf_op jit(solution)/shard_map/all_to_all | solution.py:27
  178.4 5.4 collective-permute-done.11
  208.3 9.3 %all-to-all-start.3 = ((bf16[32,96,128]{2,1,0:T(8,128)(2,1)}), bf16[32,96,128]{2,1,0:T(8,128)(2,1)S(1)}, u32[]{:S(2)}, u32[]{:S(2)}) async-start(bf16[32,96,128]{2,1,0:T(8,128)(2,1)} %copy-done.23), calls=%async_computation.3 | async-start | bytes 1572864 | tf_op jit(solution)/shard_map/all_to_all | solution.py:27
  232.7 4.9 attend.3
  237.7 8.4 %attend_back.2 = bf16[32,128,128]{2,1,0:T(8,128)(2,1)S(1)} custom-call(bf16[32,96,128]{2,1,0:T(8,128)(2,1)S(1)} %all-to-all-done.3.in_ref, bf16[32,32,128]{2,1,0:T(8,128)(2,1)S(1)} %get-tuple-element.168.grad_ref, f32[128,1024]{1,0:T(8,128)S(1)} %get-tuple-element.70.full_ref, f32[8,1024]{1,0:T(8,128)S(1)} %get-tuple-element.71.lse_ref, ...), custom_call_target="tpu_custom_call" | custom-call | flops 40000000000 | bytes 40000000 | tf_op jit(solution)/shard_map/attend_back/pallas_call | solution.py:232
  247.1 8.2 %all-to-all-start.4 = ((bf16[32,128,128]{2,1,0:T(8,128)(2,1)}), bf16[32,128,128]{2,1,0:T(8,128)(2,1)S(1)}, u32[]{:S(2)}, u32[]{:S(2)}) async-start(bf16[32,128,128]{2,1,0:T(8,128)(2,1)} %copy-done.19), calls=%async_computation.4 | async-start | bytes 2097152 | tf_op jit(solution)/shard_map/all_to_all | solution.py:27
  261.0 11.2 %all-to-all-done.4.tile_ref = bf16[32,128,128]{2,1,0:T(8,128)(2,1)S(1)} async-done(((bf16[32,128,128]{2,1,0:T(8,128)(2,1)}), bf16[32,128,128]{2,1,0:T(8,128)(2,1)S(1)}, u32[]{:S(2)}, u32[]{:S(2)}) %all-to-all-start.4) | async-done | bytes 1048608 | tf_op jit(solution)/shard_map/all_to_all | solution.py:27
  296.6 8.2 %attend_back.3 = bf16[32,96,128]{2,1,0:T(8,128)(2,1)S(1)} custom-call(bf16[32,96,128]{2,1,0:T(8,128)(2,1)S(1)} %copy-done.21, bf16[32,32,128]{2,1,0:T(8,128)(2,1)S(1)} %all-to-all-done.5.grad_ref, f32[128,1024]{1,0:T(8,128)S(1)} %copy-done.51, f32[8,1024]{1,0:T(8,128)S(1)} %copy-done.40, bf16[1,8,1024]{2,1,0:T(8,128)(2,1)S(1)} %convert_bitcast_fusion.carry_ref), custom_call_target="tpu_custom_call" | custom-call | flops 40000000000 | bytes 40000000 | tf_op jit(solution)/shard_map/attend_back/pallas_call | solution.py:232
  305.7 5.9 all-to-all-start.6
  344.2 23.1 %collective-permute-done.23 = bf16[192,1344]{1,0:T(8,128)(2,1)S(1)} collective-permute-done((bf16[192,1344]{1,0:T(8,128)(2,1)S(1)}, bf16[192,1344]{1,0:T(8,128)(2,1)S(1)}, u32[]{:S(2)}, u32[]{:S(2)}) %collective-permute-start.23) | collective-permute-done | bytes 516128 | tf_op jit(solution)/shard_map/ppermute | solution.py:32
  390.4 9.2 %all-to-all-start.7 = ((bf16[32,54,768]{2,1,0:T(8,128)(2,1)}), bf16[32,54,768]{2,1,0:T(8,128)(2,1)}, u32[]{:S(2)}, u32[]{:S(2)}) async-start(bf16[32,54,768]{2,1,0:T(8,128)(2,1)} %reshape.359), calls=%async_computation.7 | async-start | bytes 5505024 | tf_op jit(solution)/shard_map/all_to_all | solution.py:27
  424.8 7.0 %collective-permute-done.32 = bf16[200,576]{1,0:T(8,128)(2,1)S(1)} collective-permute-done((bf16[200,576]{1,0:T(8,128)(2,1)S(1)}, bf16[200,576]{1,0:T(8,128)(2,1)S(1)}, u32[]{:S(2)}, u32[]{:S(2)}) %collective-permute-start.32) | collective-permute-done | bytes 230432 | tf_op jit(solution)/shard_map/ppermute | solution.py:32
  432.4 6.2 %all-to-all-done.7 = bf16[32,54,768]{2,1,0:T(8,128)(2,1)} async-done(((bf16[32,54,768]{2,1,0:T(8,128)(2,1)}), bf16[32,54,768]{2,1,0:T(8,128)(2,1)}, u32[]{:S(2)}, u32[]{:S(2)}) %all-to-all-start.7) | async-done | bytes 2654240 | tf_op jit(solution)/shard_map/all_to_all | solution.py:27
  440.8 27.2 %all_to_all.50 = bf16[32,32,576]{2,1,0:T(8,128)(2,1)S(1)} all-to-all(bf16[32,32,576]{2,1,0:T(8,128)(2,1)S(1)} %pad_maximum_fusion.5), channel_id=1, replica_groups=mesh['ctx'=32,'wt'=4] {'ctx'}, dimensions={0} | all-to-all | bytes 2359296 | tf_op jit(solution)/shard_map/all_to_all | solution.py:27
  471.0 6.0 %all-to-all-start.9 = ((bf16[32,78,768]{2,1,0:T(8,128)(2,1)}), bf16[32,78,768]{2,1,0:T(8,128)(2,1)}, u32[]{:S(2)}, u32[]{:S(2)}) async-start(bf16[32,78,768]{2,1,0:T(8,128)(2,1)} %broadcast_in_dim.108), calls=%async_computation.9 | async-start | bytes 7864320 | tf_op jit(solution)/shard_map/all_to_all | solution.py:27
  481.5 46.5 %all-to-all-done.9 = bf16[32,78,768]{2,1,0:T(8,128)(2,1)} async-done(((bf16[32,78,768]{2,1,0:T(8,128)(2,1)}), bf16[32,78,768]{2,1,0:T(8,128)(2,1)}, u32[]{:S(2)}, u32[]{:S(2)}) %all-to-all-start.9) | async-done | bytes 3833888 | tf_op jit(solution)/shard_map/all_to_all | solution.py:27
  566.9 9.8 %dynamic_update_slice.91 = bf16[4,192,576]{2,0,1:T(4,128)(2,1)} dynamic-update-slice(bf16[4,192,576]{2,0,1:T(4,128)(2,1)} %copy.78, bf16[1,192,576]{2,0,1:T(2,128)(2,1)} %copy.79, s32[]{:T(128)S(6)} %select_n.225, s32[]{:T(128)} %constant.245.clone.1, s32[]{:T(128)} %constant.245.clone.1) | dynamic-update-slice | bytes 442372 | tf_op jit(solution)/shard_map/dynamic_update_slice | solution.py:72
  (543 shorter events, 287.7 us)
Async XLA Ops:
  7.2 151.1 %all-gather.6.cloned.1.call-start = ((), (), s32[]{:S(2)}) async-start(), calls=%async_computation.11 | async-start | bytes 2949120 | tf_op jit(solution)/shard_map/all_gather | solution.py:517
  42.4 148.1 %all-gather.8.cloned.1.call-start = ((), (), s32[]{:S(2)}) async-start(), calls=%async_computation.12 | async-start | bytes 4423680 | tf_op jit(solution)/shard_map/all_gather | solution.py:516
  48.1 50.7 %collective-permute-start.3 = (bf16[4,96,2304]{2,1,0:T(8,128)(2,1)}, bf16[4,96,2304]{2,1,0:T(8,128)(2,1)}, u32[]{:S(2)}, u32[]{:S(2)}) collective-permute-start(bf16[4,96,2304]{2,1,0:T(8,128)(2,1)} %bitcast_dynamic-update-slice_fusion.4), channel_id=1, source_target_pairs={{0,4},{4,0},{8,12},{12,8},{16,20},{20,16},{24,28},{28,24},{32,36},... | collective-permute-start | bytes 5308424 | tf_op jit(solution)/shard_map/ppermute | solution.py:77
  54.7 29.5 %collective-permute-start.7 = (bf16[2,192,768]{2,1,0:T(8,128)(2,1)}, bf16[2,192,768]{2,1,0:T(8,128)(2,1)S(1)}, u32[]{:S(2)}, u32[]{:S(2)}) collective-permute-start(bf16[2,192,768]{2,1,0:T(8,128)(2,1)} %get-tuple-element.124), channel_id=1, source_target_pairs={{0,1},{1,2},{2,3},{3,0},{4,5},{5,6},{6,7},{7,4},{8,9},{9,10},{10,1... | collective-permute-start | bytes 1769480 | tf_op jit(solution)/shard_map/ppermute | solution.py:32
  55.9 41.8 %collective-permute-start.8 = (bf16[2,192,768]{2,1,0:T(8,128)(2,1)}, bf16[2,192,768]{2,1,0:T(8,128)(2,1)}, u32[]{:S(2)}, u32[]{:S(2)}) collective-permute-start(bf16[2,192,768]{2,1,0:T(8,128)(2,1)} %get-tuple-element.123), channel_id=1, source_target_pairs={{0,2},{1,3},{2,0},{3,1},{4,6},{5,7},{6,4},{7,5},{8,10},{9,11},{10,... | collective-permute-start | bytes 1769480 | tf_op jit(solution)/shard_map/ppermute | solution.py:32
  57.6 52.3 %collective-permute-start.9 = (bf16[2,192,768]{2,1,0:T(8,128)(2,1)}, bf16[2,192,768]{2,1,0:T(8,128)(2,1)S(1)}, u32[]{:S(2)}, u32[]{:S(2)}) collective-permute-start(bf16[2,192,768]{2,1,0:T(8,128)(2,1)} %get-tuple-element.122), channel_id=1, source_target_pairs={{0,3},{1,0},{2,1},{3,2},{4,7},{5,4},{6,5},{7,6},{8,11},{9,8},{10,9... | collective-permute-start | bytes 1769480 | tf_op jit(solution)/shard_map/ppermute | solution.py:32
  107.2 33.2 %collective-permute-start.5 = (bf16[128,1536]{1,0:T(8,128)(2,1)S(1)}, bf16[128,1536]{1,0:T(8,128)(2,1)}, u32[]{:S(2)}, u32[]{:S(2)}) collective-permute-start(bf16[128,1536]{1,0:T(8,128)(2,1)S(1)} %bitcast.234), channel_id=1, source_target_pairs={{0,2},{1,3},{2,0},{3,1},{4,6},{5,7},{6,4},{7,5},{8,10},{9,11},{10,... | collective-permute-start | bytes 1179656 | tf_op jit(solution)/shard_map/ppermute | solution.py:32
  107.2 37.4 %collective-permute-start.6 = (bf16[128,1536]{1,0:T(8,128)(2,1)S(1)}, bf16[128,1536]{1,0:T(8,128)(2,1)}, u32[]{:S(2)}, u32[]{:S(2)}) collective-permute-start(bf16[128,1536]{1,0:T(8,128)(2,1)S(1)} %bitcast.235), channel_id=1, source_target_pairs={{0,3},{1,0},{2,1},{3,2},{4,7},{5,4},{6,5},{7,6},{8,11},{9,8},{10,9... | collective-permute-start | bytes 1179656 | tf_op jit(solution)/shard_map/ppermute | solution.py:32
  111.1 40.1 %all-to-all-start.1 = ((bf16[32,96,128]{2,1,0:T(8,128)(2,1)}), bf16[32,96,128]{2,1,0:T(8,128)(2,1)S(1)}, u32[]{:S(2)}, u32[]{:S(2)}) async-start(bf16[32,96,128]{2,1,0:T(8,128)(2,1)} %get-tuple-element.61), calls=%async_computation.1 | async-start | bytes 1572864 | tf_op jit(solution)/shard_map/all_to_all | solution.py:27
  208.3 24.4 %all-to-all-start.3 = ((bf16[32,96,128]{2,1,0:T(8,128)(2,1)}), bf16[32,96,128]{2,1,0:T(8,128)(2,1)S(1)}, u32[]{:S(2)}, u32[]{:S(2)}) async-start(bf16[32,96,128]{2,1,0:T(8,128)(2,1)} %copy-done.23), calls=%async_computation.3 | async-start | bytes 1572864 | tf_op jit(solution)/shard_map/all_to_all | solution.py:27
  227.7 30.9 %collective-permute-start.16 = (bf16[128,1536]{1,0:T(8,128)(2,1)}, bf16[128,1536]{1,0:T(8,128)(2,1)}, u32[]{:S(2)}, u32[]{:S(2)}) collective-permute-start(bf16[128,1536]{1,0:T(8,128)(2,1)} %get-tuple-element.139), channel_id=1, source_target_pairs={{0,3},{1,0},{2,1},{3,2},{4,7},{5,4},{6,5},{7,6},{8,11},{9,8},{10,9... | collective-permute-start | bytes 1179656 | tf_op jit(solution)/shard_map/ppermute | solution.py:32
  227.7 30.9 %collective-permute-start.17 = (bf16[128,1536]{1,0:T(8,128)(2,1)}, bf16[128,1536]{1,0:T(8,128)(2,1)}, u32[]{:S(2)}, u32[]{:S(2)}) collective-permute-start(bf16[128,1536]{1,0:T(8,128)(2,1)} %get-tuple-element.141), channel_id=1, source_target_pairs={{0,1},{1,2},{2,3},{3,0},{4,5},{5,6},{6,7},{7,4},{8,9},{9,10},{10,1... | collective-permute-start | bytes 1179656 | tf_op jit(solution)/shard_map/ppermute | solution.py:32
  229.2 29.5 %collective-permute-start.18 = (bf16[128,1536]{1,0:T(8,128)(2,1)}, bf16[128,1536]{1,0:T(8,128)(2,1)}, u32[]{:S(2)}, u32[]{:S(2)}) collective-permute-start(bf16[128,1536]{1,0:T(8,128)(2,1)} %get-tuple-element.140), channel_id=1, source_target_pairs={{0,2},{1,3},{2,0},{3,1},{4,6},{5,7},{6,4},{7,5},{8,10},{9,11},{10,... | collective-permute-start | bytes 1179656 | tf_op jit(solution)/shard_map/ppermute | solution.py:32
  247.1 25.1 %all-to-all-start.4 = ((bf16[32,128,128]{2,1,0:T(8,128)(2,1)}), bf16[32,128,128]{2,1,0:T(8,128)(2,1)S(1)}, u32[]{:S(2)}, u32[]{:S(2)}) async-start(bf16[32,128,128]{2,1,0:T(8,128)(2,1)} %copy-done.19), calls=%async_computation.4 | async-start | bytes 2097152 | tf_op jit(solution)/shard_map/all_to_all | solution.py:27
  305.7 64.3 %all-to-all-start.6 = ((bf16[32,96,128]{2,1,0:T(8,128)(2,1)}), bf16[32,96,128]{2,1,0:T(8,128)(2,1)S(1)}, u32[]{:S(2)}, u32[]{:S(2)}) async-start(bf16[32,96,128]{2,1,0:T(8,128)(2,1)} %copy-done.22), calls=%async_computation.6 | async-start | bytes 1572864 | tf_op jit(solution)/shard_map/all_to_all | solution.py:27
  311.6 157.2 %reduce-scatter.2.cloned.1.call-start = ((), (), s32[]{:S(2)}) async-start(), calls=%async_computation.13 | async-start | bytes 4055040 | tf_op jit(solution)/shard_map/reduce_scatter | solution.py:575
  329.7 51.1 %collective-permute-start.34 = (bf16[192,768]{1,0:T(8,128)(2,1)}, bf16[192,768]{1,0:T(8,128)(2,1)}, u32[]{:S(2)}, u32[]{:S(2)}) collective-permute-start(bf16[192,768]{1,0:T(8,128)(2,1)} %get-tuple-element.144), channel_id=1, source_target_pairs={{0,1},{1,2},{2,3},{3,0},{4,5},{5,6},{6,7},{7,4},{8,9},{9,10},{10,1... | collective-permute-start | bytes 884744 | tf_op jit(solution)/shard_map/ppermute | solution.py:32
  330.4 52.0 %collective-permute-start.35 = (bf16[192,768]{1,0:T(8,128)(2,1)}, bf16[192,768]{1,0:T(8,128)(2,1)}, u32[]{:S(2)}, u32[]{:S(2)}) collective-permute-start(bf16[192,768]{1,0:T(8,128)(2,1)} %get-tuple-element.143), channel_id=1, source_target_pairs={{0,2},{1,3},{2,0},{3,1},{4,6},{5,7},{6,4},{7,5},{8,10},{9,11},{10,... | collective-permute-start | bytes 884744 | tf_op jit(solution)/shard_map/ppermute | solution.py:32
  332.9 34.4 %collective-permute-start.23 = (bf16[192,1344]{1,0:T(8,128)(2,1)S(1)}, bf16[192,1344]{1,0:T(8,128)(2,1)S(1)}, u32[]{:S(2)}, u32[]{:S(2)}) collective-permute-start(bf16[192,1344]{1,0:T(8,128)(2,1)S(1)} %get-tuple-element.132), channel_id=1, source_target_pairs={{0,2},{1,3},{2,0},{3,1},{4,6},{5,7},{6,4},{7,5},{8,10},{9,11},{10,... | collective-permute-start | bytes 1548296 | tf_op jit(solution)/shard_map/ppermute | solution.py:32
  333.4 34.0 %collective-permute-start.24 = (bf16[192,1344]{1,0:T(8,128)(2,1)S(1)}, bf16[192,1344]{1,0:T(8,128)(2,1)S(1)}, u32[]{:S(2)}, u32[]{:S(2)}) collective-permute-start(bf16[192,1344]{1,0:T(8,128)(2,1)S(1)} %get-tuple-element.129), channel_id=1, source_target_pairs={{0,3},{1,0},{2,1},{3,2},{4,7},{5,4},{6,5},{7,6},{8,11},{9,8},{10,9... | collective-permute-start | bytes 1548296 | tf_op jit(solution)/shard_map/ppermute | solution.py:32
  341.5 41.9 %collective-permute-start.36 = (bf16[192,768]{1,0:T(8,128)(2,1)}, bf16[192,768]{1,0:T(8,128)(2,1)}, u32[]{:S(2)}, u32[]{:S(2)}) collective-permute-start(bf16[192,768]{1,0:T(8,128)(2,1)} %get-tuple-element.142), channel_id=1, source_target_pairs={{0,3},{1,0},{2,1},{3,2},{4,7},{5,4},{6,5},{7,6},{8,11},{9,8},{10,9... | collective-permute-start | bytes 884744 | tf_op jit(solution)/shard_map/ppermute | solution.py:32
  390.4 48.2 %all-to-all-start.7 = ((bf16[32,54,768]{2,1,0:T(8,128)(2,1)}), bf16[32,54,768]{2,1,0:T(8,128)(2,1)}, u32[]{:S(2)}, u32[]{:S(2)}) async-start(bf16[32,54,768]{2,1,0:T(8,128)(2,1)} %reshape.359), calls=%async_computation.7 | async-start | bytes 5505024 | tf_op jit(solution)/shard_map/all_to_all | solution.py:27
  399.6 143.2 %all-gather.10.cloned.1.call-start = ((), (), s32[]{:S(2)}) async-start(), calls=%async_computation.14 | async-start | bytes 4055040 | tf_op jit(solution)/shard_map/all_gather | solution.py:606
  471.0 57.0 %all-to-all-start.9 = ((bf16[32,78,768]{2,1,0:T(8,128)(2,1)}), bf16[32,78,768]{2,1,0:T(8,128)(2,1)}, u32[]{:S(2)}, u32[]{:S(2)}) async-start(bf16[32,78,768]{2,1,0:T(8,128)(2,1)} %broadcast_in_dim.108), calls=%async_computation.9 | async-start | bytes 7864320 | tf_op jit(solution)/shard_map/all_to_all | solution.py:27
  (145 other events, 1813.2 us)
Sparse Core Ops, SparseCore 0:
  38.4 51.9 all-gather.5
  92.7 63.9 all-gather.7
  375.0 93.6 reduce-scatter.1
  470.9 69.8 all-gather.9

commit v4 on v3

--- a/solution.py
+++ b/solution.py
@@ -512,11 +512,8 @@
         {"g_attn": ln_gain_attn, "s_attn": ln_shift_attn, "g_mlp": ln_gain_mlp, "s_mlp": ln_shift_mlp, "b_qv": b_qv, "b_out": b_out, "b_down": b_down}
     )
     half1 = gather_half(w_qkv[0])
-    later_out, later_qkv, later_up = after((w_out, w_qkv[1], w_up), half1)
-    qkv = [gather_rest(half1), lax.all_gather(later_qkv, "wt", axis=0, tiled=True)]
-    out_both = lax.all_gather(later_out, "wt", axis=1, tiled=True)
-    ups = jnp.stack([later_up[:, :, i * unit : (i + 1) * unit] for i in range(4)])
-    ups = place([b[:, None] for b in group_trade(ups)], 1).reshape(LAYERS, width, unit)
+    qkv = [gather_rest(half1), lax.all_gather(w_qkv[1], "wt", axis=0, tiled=True)]
+    out_both = lax.all_gather(w_out, "wt", axis=1, tiled=True)
     layers = []
     for layer in range(LAYERS):
         w = {name: small[name][layer][None] for name in small}
@@ -524,25 +521,32 @@
         w["b_v"] = w["b_qv"][:, width:]
         w["qkv"] = qkv[layer]
         w["out"] = out_both[layer]
-        w["up"] = ups[layer]
         w["down"] = w_down[layer]
         w["b_up"] = b_up[layer].astype(F32)[None]
         layers.append(w)
     first, second = layers
     g2 = cotangent.reshape(rows, width)
     x1 = tokens_in.reshape(rows, width).astype(F32)
-    xhat1, send1, scale1, packed1 = mix(x1, first, tables, g2[None])
+    xhat1, send1, scale1, packed1 = mix(x1, first, tables, jnp.zeros((1, rows, 128), BF16))
+    later_up, send1 = after((w_up, send1), packed1)
     packed1 = exchange(packed1, "ctx")
-    landed1 = jnp.concatenate(group_spread(send1[0]), axis=0)
-    xhat1_all, g2_all = landed1[:, :width], landed1[:, width:]
+    ups = jnp.stack([later_up[:, :, i * unit : (i + 1) * unit] for i in range(4)])
+    ups = group_trade(ups)
+    spread1 = group_spread(send1[0, :, :width])
+    out1, full1, lse1 = attend(packed1)
+    both1 = jnp.concatenate([out1, pull(g2, second)], axis=1)
+    ups, spread1, later_g2 = after((ups, spread1, g2), both1)
+    both1 = exchange(both1, "ctx")
+    ups = place([b[:, None] for b in ups], 1).reshape(LAYERS, width, unit)
+    first["up"], second["up"] = ups[0], ups[1]
+    xhat1_all = jnp.concatenate(spread1, axis=0)
     n_mlp1, hidden1, active1, partial1 = mlp_forward(xhat1_all, first)
     mlp1 = own_sum(partial1)
-    out1, full1, lse1 = attend(packed1)
-    both1 = exchange(jnp.concatenate([out1, pull(g2, second)], axis=1), "ctx")
     out1, grads2 = both1[:, :BLK], both1[:, BLK:]
     split1, x2 = join(out1, x1, mlp1, first)
     xhat2, send2, scale2, packed2 = mix(x2, second, tables, split1)
     packed2 = exchange(packed2, "ctx")
+    g2_all = jnp.concatenate(group_spread(after(later_g2, mlp1)), axis=0)
     landed2 = jnp.concatenate(group_trade(send2), axis=0)
     xhat2_all, context1_all = landed2[:, :width], landed2[:, width:]
     n_mlp2, hidden2, active2, partial2 = mlp_forward(xhat2_all, second)
@@ -560,23 +564,23 @@
     columns = mixed2_split.shape[2]
     g1_all, mixed2_all, context2_all = landed3[:, :width], landed3[:, width : width + columns], landed3[:, -depth:]
     back_partial1, grad_down1, grad_up1, grad_b_up1 = mlp_backward(g1_all, n_mlp1, hidden1, active1, first)
-    grad_n_mlp1 = own_sum(back_partial1)
     back1 = exchange(attend_back(packed1, grads1, full1, lse1, lse1[None].astype(BF16)), "ctx")
     grad_up1 = place([b[None] for b in group_trade(grad_up1)], 0).reshape(width, unit)
     grad_out1 = dot(context1_all, g1_all, TN).astype(BF16)
     grad_out2 = dot(context2_all, g2_all, TN).astype(BF16)
     n_attn2_all = (xhat2_all.astype(F32) * second["g_attn"] + second["s_attn"]).astype(BF16)
-    grad_qkv2 = dot(n_attn2_all, mixed2_all, TN).astype(BF16)
-    traded2 = group_trade(jnp.concatenate([grad_up2, grad_qkv2.reshape(4, depth, columns)], axis=2))
-    space = jnp.zeros((width, width - columns), BF16)
-    parts2 = [grad_down2, grad_out2] + [b[:, :unit] for b in traded2]
-    tall2 = jnp.concatenate(parts2 + [jnp.concatenate([jnp.concatenate([b[:, unit:] for b in traded2], axis=0), space], axis=1)], axis=0)
-    back1, tall2 = lax.optimization_barrier((back1, tall2))
-    tall2 = lax.psum_scatter(tall2.reshape(devices, -1, width), "ctx", scatter_dimension=0, tiled=False)
-    wide1 = jnp.concatenate([grad_down1, grad_up1, grad_out1], axis=0)
-    wide1 = exchange(wide1.reshape(devices, -1, width), "ctx").astype(F32).sum(0).astype(BF16)
+    grad_up2 = place([b[None] for b in group_trade(grad_up2)], 0).reshape(width, unit)
+    ready = [grad_down1, grad_up1, grad_down2, grad_up2, grad_out1, grad_out2]
+    lines = sum(v.shape[0] for v in ready)
+    lines = -(-lines // (16 * devices)) * 16 * devices - lines
+    ready = jnp.concatenate(ready + [jnp.zeros((lines, width), BF16)], axis=0)
+    back1, ready = lax.optimization_barrier((back1, ready))
+    wide = lax.psum_scatter(ready, "ctx", scatter_dimension=0, tiled=True)
     mixed1, mixed1_split, mixed_sums1 = unmix(back1, tables)
     mixed1_all = jnp.concatenate(group_trade(mixed1_split), axis=0)
+    back_partial1, mixed2_all = after((back_partial1, mixed2_all), mixed1_split)
+    grad_n_mlp1 = own_sum(back_partial1)
+    grad_qkv2 = dot(n_attn2_all, mixed2_all, TN).astype(BF16)
     n_attn1_all = (xhat1_all.astype(F32) * first["g_attn"] + first["s_attn"]).astype(BF16)
     grad_qkv1 = dot(n_attn1_all, mixed1_all, TN).astype(BF16)
     g0, _, _, sums1 = norm_backward(g1, mixed1, grad_n_mlp1, xhat1, scale1, first, mixed2_split, split2, False)
@@ -592,36 +596,29 @@
         return padded.reshape(value.shape[0], lines, columns)
 
     tiny = to_rows(jnp.concatenate(smalls, axis=1).astype(BF16))
-    moved = group_trade(jnp.concatenate([grad_qkv1.reshape(4, depth, columns), tiny], axis=1))
-    moved = place([b[None] for b in moved], 0)
+    both_qkv = [m.reshape(4, depth, columns) for m in (grad_qkv1, grad_qkv2)]
+    moved = exchange(jnp.concatenate(both_qkv + [tiny], axis=1), "wt")
     tiny_size = small1.shape[1]
-    small_sum = moved[:, depth:].astype(F32).sum(0).reshape(1, -1)[:, : LAYERS * tiny_size]
+    small_sum = moved[:, 2 * depth :].astype(F32).sum(0).reshape(1, -1)[:, : LAYERS * tiny_size]
     tail = to_rows(jnp.concatenate([small_sum, *(u[None] for u in hidden_sums)], axis=1).astype(BF16))
     sent = jnp.concatenate(
-        [moved[:, :depth].reshape(devices, piece, columns), jnp.broadcast_to(tail, (devices,) + tail.shape[1:])], axis=1
+        [moved[:, i * depth : (i + 1) * depth].reshape(devices, piece, columns) for i in range(LAYERS)]
+        + [jnp.broadcast_to(tail, (devices,) + tail.shape[1:])],
+        axis=1,
     )
-    landed = exchange(after(sent, wide1), "ctx").astype(F32).sum(0)
-    lines = wide1.shape[0]
-    tall2 = after(tall2, landed)
-    tall2 = lax.all_gather(tall2, "ctx", axis=0).reshape(-1, width)
-    wide2 = (tall2[:unit], tall2[unit : unit + depth])
-    traded_up2 = tall2[unit + depth : unit + depth + width].reshape(4, depth, unit)
-    traded_qkv2 = tall2[unit + depth + width :, :columns].reshape(4, depth, columns)
-    last = jnp.pad(landed[:piece].astype(BF16), ((0, 0), (0, width - columns)))
-    last = spread(jnp.concatenate([wide1, last], axis=0), "ctx")
-    wide1 = last[:, :lines].reshape(-1, width)
-    moved1 = last[:, lines:, :columns].reshape(4, depth, columns)
-    up1 = wide1[unit : unit + width].reshape(4, depth, unit)
-    up2 = place([traded_up2[i : i + 1] for i in range(4)], 0)
-    qkv2 = place([traded_qkv2[i : i + 1] for i in range(4)], 0)
-
+    landed = exchange(sent, "ctx").astype(F32).sum(0)
     def side_by_side(blocks):
         return blocks.transpose(1, 0, 2).reshape(depth, -1)
 
-    flat = landed[piece:].reshape(-1)
+    qkvs = spread(landed[: 2 * piece].astype(BF16), "ctx")
+    wide = lax.all_gather(after(wide, landed), "ctx", axis=0, tiled=True)
+    at = 2 * (unit + width)
+    down1, up1 = wide[:unit], wide[unit : unit + width].reshape(4, depth, unit)
+    down2, up2 = wide[unit + width : 2 * unit + width], wide[2 * unit + width : at].reshape(4, depth, unit)
+    qkvs = [side_by_side(qkvs[:, i * piece : (i + 1) * piece].reshape(4, depth, columns)) for i in range(LAYERS)]
+    flat = landed[2 * piece :].reshape(-1)
     per_layer = [flat[layer * tiny_size : (layer + 1) * tiny_size] for layer in range(LAYERS)]
-    at = LAYERS * tiny_size
-    grad_b_up = flat[at : at + LAYERS * unit].reshape(LAYERS, unit)
+    grad_b_up = flat[LAYERS * tiny_size :][: LAYERS * unit].reshape(LAYERS, unit)
 
     def vector(index):
         return jnp.stack([v[index * depth : (index + 1) * depth] for v in per_layer])
@@ -631,7 +628,7 @@
 
     grad_bias = vector(4)
     grad_b_qv = jnp.stack([v[5 * depth :] for v in per_layer])
-    grad_qkv = both(side_by_side(moved1), side_by_side(qkv2))
+    grad_qkv = both(*qkvs)
     return (
         out_tokens,
         g0.reshape(tokens_in.shape),
@@ -641,11 +638,11 @@
         vector(3),
         grad_qkv,
         grad_b_qv,
-        both(wide1[unit + width :], wide2[1]),
+        both(wide[at : at + depth], wide[at + depth : at + 2 * depth]),
         grad_bias,
         both(side_by_side(up1), side_by_side(up2)),
         grad_b_up,
-        both(wide1[:unit], wide2[0]),
+        both(down1, down2),
         grad_bias,
     )
 

time: 607 us -> 545 us (0.90)
  local copies, waits for them, and re-layouts: 130 us -> 92.7 us
  waiting for transfers between devices: 188 us -> 168 us
  blocking collectives: 27.2 us -> 40.6 us
  starting transfers between devices: 122 us -> 111 us
  other arithmetic: 36.7 us -> 30.5 us
    ppermute x36, waiting for transfers between devices: 119 us -> 82.7 us  [pass_on(): lax.ppermute(value, 'wt', [(i, (i + shift) % count) for i in range(count)])]
    all_gather x3, waiting for transfers between devices: 0.01 us -> 17 us  [the longest x1 17 us: local(): wide = lax.all_gather(after(wide, landed), 'ctx', axis=0, tiled=True)]
    dynamic_update_slice x22 -> x13, local copies, waits for them, and re-layouts: 26.2 us -> 9.95 us  [place(): lax.dynamic_update_slice_in_dim(whole, blocks[shift], (here - shift) % 4...]
    all_to_all x9, starting transfers between devices: 74 us -> 59.3 us  [exchange(): return lax.all_to_all(chunks, axis, 0, 0, tiled=True)]
    all_to_all x1, blocking collectives: 27.2 us -> 40.6 us  [exchange(): return lax.all_to_all(chunks, axis, 0, 0, tiled=True)]
    reshape x6 -> x3, local copies, waits for them, and re-layouts: 12.2 us -> 0.77 us  [the longest x1 0.6 us: local(): grad_b_up = flat[LAYERS * tiny_size:][:LAYERS * unit].reshape(LAYERS, unit)]
    slice x15 -> x8, local copies, waits for them, and re-layouts: 10.4 us -> 4.01 us  [the longest x1 2.46 us: local(): w_qkv[1]]
    unnamed x244 -> x204, local copies, waits for them, and re-layouts: 30.3 us -> 26.4 us
  transfers between devices with their start and end apart: 50 -> 50, of which waited for: 23 -> 18; matrix products, arithmetic and copies ran while one was open for 21% -> 22% of each run, Pallas kernels for 6% -> 8%
where the time goes in v4:
time: 545 us; the launch traced here: 536 us
  waiting for transfers between devices  168 us (31%)
  starting transfers between devices  111 us (20%)
  local copies, waits for them, and re-layouts  92.7 us (17%)
  Pallas kernels  46.8 us (9%)
  blocking collectives  40.6 us (7%)
  matrix products  30.7 us (6%)
  other arithmetic  30.5 us (6%)
  between operations  15.6 us (3%)
    ppermute x36, waiting for transfers between devices, pass_on(): lax.ppermute(value, 'wt', [(i, (i + shift) % count) for i in range(count)])  82.7 us
    all_to_all x9, waiting for transfers between devices, exchange(): return lax.all_to_all(chunks, axis, 0, 0, tiled=True)  67.1 us
    all_to_all x9, starting transfers between devices, exchange(): return lax.all_to_all(chunks, axis, 0, 0, tiled=True)  59.3 us
    ppermute x36, starting transfers between devices, pass_on(): lax.ppermute(value, 'wt', [(i, (i + shift) % count) for i in range(count)])  47.3 us
    all_to_all x1, blocking collectives, exchange(): return lax.all_to_all(chunks, axis, 0, 0, tiled=True)  40.6 us
    dot_general x16, matrix products, dot(): return lax.dot_general(left, right, dims, preferred_element_type=F32)  30.7 us
    unnamed x204, local copies, waits for them, and re-layouts  26.4 us
    pallas_call x10, Pallas kernels, on_chip(): pl.pallas_call(kernel, out_shape=out_shape, in_specs=[spec] * len(operand...  19.4 us
  transfers between devices with their start and end apart: 50, of which 18 were waited for; matrix products, arithmetic and copies ran while one was open for 22% of the time, Pallas kernels for 8%

profile of v4, /device:TPU:1, one launch (start us, length us, event | category | flops | bytes accessed | tf_op | source)
XLA Modules:
  0.0 535.8 jit_solution(16133006660280044011)
XLA Ops:
  27.9 19.6 %collective-permute-done.1 = bf16[96,2304]{1,0:T(8,128)(2,1)S(1)} collective-permute-done((bf16[96,2304]{1,0:T(8,128)(2,1)S(1)}, bf16[96,2304]{1,0:T(8,128)(2,1)S(1)}, u32[]{:S(2)}, u32[]{:S(2)}) %collective-permute-start.1) | collective-permute-done | bytes 442400 | tf_op jit(solution)/shard_map/ppermute | solution.py:32
  49.0 4.0 collective-permute-start.3
  64.1 4.0 mix.2
  68.9 7.4 %all-to-all-start.1 = ((bf16[32,96,128]{2,1,0:T(8,128)(2,1)}), bf16[32,96,128]{2,1,0:T(8,128)(2,1)S(1)}, u32[]{:S(2)}, u32[]{:S(2)}) async-start(bf16[32,96,128]{2,1,0:T(8,128)(2,1)} %get-tuple-element.71), calls=%async_computation.1 | async-start | bytes 1572864 | tf_op jit(solution)/shard_map/all_to_all | solution.py:27
  90.6 4.9 attend.2
  100.7 6.0 %all-to-all-start.2 = ((bf16[32,64,128]{2,1,0:T(8,128)(2,1)}), bf16[32,64,128]{2,1,0:T(8,128)(2,1)}, u32[]{:S(2)}, u32[]{:S(2)}) async-start(bf16[32,64,128]{2,1,0:T(8,128)(2,1)} %pad_maximum_fusion.9), calls=%async_computation.2 | async-start | bytes 1048576 | tf_op jit(solution)/shard_map/all_to_all | solution.py:27
  106.7 29.6 %collective-permute-done.9 = bf16[128,768]{1,0:T(8,128)(2,1)} collective-permute-done((bf16[128,768]{1,0:T(8,128)(2,1)}, bf16[128,768]{1,0:T(8,128)(2,1)}, u32[]{:S(2)}, u32[]{:S(2)}) %collective-permute-start.9) | collective-permute-done | bytes 196640 | tf_op jit(solution)/shard_map/ppermute | solution.py:32
  153.6 5.1 collective-permute-done.11
  184.1 9.0 %all-to-all-start.3 = ((bf16[32,96,128]{2,1,0:T(8,128)(2,1)}), bf16[32,96,128]{2,1,0:T(8,128)(2,1)S(1)}, u32[]{:S(2)}, u32[]{:S(2)}) async-start(bf16[32,96,128]{2,1,0:T(8,128)(2,1)} %copy-done.22), calls=%async_computation.3 | async-start | bytes 1572864 | tf_op jit(solution)/shard_map/all_to_all | solution.py:27
  216.1 5.0 attend.3
  221.1 8.4 %attend_back.2 = bf16[32,128,128]{2,1,0:T(8,128)(2,1)S(1)} custom-call(bf16[32,96,128]{2,1,0:T(8,128)(2,1)S(1)} %all-to-all-done.3.in_ref, bf16[32,32,128]{2,1,0:T(8,128)(2,1)S(1)} %copy-done.34, f32[128,1024]{1,0:T(8,128)S(1)} %get-tuple-element.87.full_ref, f32[8,1024]{1,0:T(8,128)S(1)} %get-tuple-element.88.lse_ref, ...), custom_call_target="tpu_custom_call" | custom-call | flops 40000000000 | bytes 40000000 | tf_op jit(solution)/shard_map/attend_back/pallas_call | solution.py:232
  230.4 16.6 %all-to-all-start.4 = ((bf16[32,128,128]{2,1,0:T(8,128)(2,1)}), bf16[32,128,128]{2,1,0:T(8,128)(2,1)S(1)}, u32[]{:S(2)}, u32[]{:S(2)}) async-start(bf16[32,128,128]{2,1,0:T(8,128)(2,1)} %copy-done.19), calls=%async_computation.4 | async-start | bytes 2097152 | tf_op jit(solution)/shard_map/all_to_all | solution.py:27
  253.0 10.9 %all-to-all-done.4.tile_ref = bf16[32,128,128]{2,1,0:T(8,128)(2,1)S(1)} async-done(((bf16[32,128,128]{2,1,0:T(8,128)(2,1)}), bf16[32,128,128]{2,1,0:T(8,128)(2,1)S(1)}, u32[]{:S(2)}, u32[]{:S(2)}) %all-to-all-start.4) | async-done | bytes 1048608 | tf_op jit(solution)/shard_map/all_to_all | solution.py:27
  275.3 4.0 all-to-all-start.5
  288.3 9.1 %attend_back.3 = bf16[32,96,128]{2,1,0:T(8,128)(2,1)} custom-call(bf16[32,96,128]{2,1,0:T(8,128)(2,1)S(1)} %copy-done.21, bf16[32,32,128]{2,1,0:T(8,128)(2,1)S(1)} %all-to-all-done.5.grad_ref, f32[128,1024]{1,0:T(8,128)S(1)} %copy-done.51, f32[8,1024]{1,0:T(8,128)S(1)} %copy-done.38, bf16[1,8,1024]{2,1,0:T(8,128)(2,1)S(1)} %convert_bitcast_fusion.carry_ref), custom_call_target="tpu_custom_call" | custom-call | flops 40000000000 | bytes 40000000 | tf_op jit(solution)/shard_map/attend_back/pallas_call | solution.py:232
  297.4 5.1 all-to-all-start.6
  302.6 4.0 collective-permute-done.22
  319.1 9.9 %collective-permute-done.25 = bf16[192,768]{1,0:T(8,128)(2,1)S(1)} collective-permute-done((bf16[192,768]{1,0:T(8,128)(2,1)S(1)}, bf16[192,768]{1,0:T(8,128)(2,1)S(1)}, u32[]{:S(2)}, u32[]{:S(2)}) %collective-permute-start.25) | collective-permute-done | bytes 294944 | tf_op jit(solution)/shard_map/ppermute | solution.py:32
  373.6 4.4 norm_back.3
  385.3 24.3 %all-to-all-done.7 = bf16[4,392,576]{2,1,0:T(8,128)(2,1)S(1)} async-done(((bf16[4,392,576]{2,1,0:T(8,128)(2,1)}), bf16[4,392,576]{2,1,0:T(8,128)(2,1)S(1)}, u32[]{:S(2)}, u32[]{:S(2)}) %all-to-all-start.7) | async-done | bytes 1806368 | tf_op jit(solution)/shard_map/all_to_all | solution.py:27
  410.3 40.6 %all_to_all.50 = bf16[32,56,576]{2,1,0:T(8,128)(2,1)S(1)} all-to-all(bf16[32,56,576]{2,1,0:T(8,128)(2,1)S(1)} %pad_maximum_fusion.3), channel_id=1, replica_groups=mesh['ctx'=32,'wt'=4] {'ctx'}, dimensions={0} | all-to-all | bytes 4128768 | tf_op jit(solution)/shard_map/all_to_all | solution.py:27
  452.8 4.3 all-to-all-start.9
  461.5 25.1 %all-to-all-done.9 = bf16[32,48,576]{2,1,0:T(8,128)(2,1)S(1)} async-done(((bf16[32,48,576]{2,1,0:T(8,128)(2,1)}), bf16[32,48,576]{2,1,0:T(8,128)(2,1)S(1)}, u32[]{:S(2)}, u32[]{:S(2)}) %all-to-all-start.9) | async-done | bytes 1769504 | tf_op jit(solution)/shard_map/all_to_all | solution.py:27
  491.8 17.0 %all-gather.7.cloned.1.call-done = bf16[3584,768]{1,0:T(8,128)(2,1)} async-done(((bf16[112,768]{1,0:T(8,128)(2,1)}), bf16[3584,768]{1,0:T(8,128)(2,1)}) %all-gather.7.cloned.1.call-update) | async-done | bytes 5505040 | tf_op jit(solution)/shard_map/all_gather | solution.py:614
  (482 shorter events, 242.2 us)
Async XLA Ops:
  7.2 90.0 %all-gather.5.cloned.1.call-start = ((), (), s32[]{:S(2)}) async-start(), calls=%async_computation.11 | async-start | bytes 2949120 | tf_op jit(solution)/shard_map/all_gather | solution.py:516
  15.1 32.4 %collective-permute-start.1 = (bf16[96,2304]{1,0:T(8,128)(2,1)S(1)}, bf16[96,2304]{1,0:T(8,128)(2,1)S(1)}, u32[]{:S(2)}, u32[]{:S(2)}) collective-permute-start(bf16[96,2304]{1,0:T(8,128)(2,1)S(1)} %get-tuple-element.179), channel_id=1, source_target_pairs={{0,2},{1,3},{2,0},{3,1},{4,6},{5,7},{6,4},{7,5},{8,10},{9,11},{10,... | collective-permute-start | bytes 1327112 | tf_op jit(solution)/shard_map/ppermute | solution.py:32
  18.4 29.9 %collective-permute-start.2 = (bf16[96,2304]{1,0:T(8,128)(2,1)S(1)}, bf16[96,2304]{1,0:T(8,128)(2,1)S(1)}, u32[]{:S(2)}, u32[]{:S(2)}) collective-permute-start(bf16[96,2304]{1,0:T(8,128)(2,1)S(1)} %get-tuple-element.179), channel_id=1, source_target_pairs={{0,3},{1,0},{2,1},{3,2},{4,7},{5,4},{6,5},{7,6},{8,11},{9,8},{10,9... | collective-permute-start | bytes 1327112 | tf_op jit(solution)/shard_map/ppermute | solution.py:32
  19.9 34.5 %all-to-all-start = ((bf16[4,2,1536]{2,1,0:T(2,128)(2,1)}), bf16[4,2,1536]{2,1,0:T(2,128)(2,1)S(1)}, u32[]{:S(2)}, u32[]{:S(2)}) async-start(bf16[4,2,1536]{2,1,0:T(2,128)(2,1)} %broadcast_in_dim.86), calls=%async_computation | async-start | bytes 49152 | tf_op jit(solution)/shard_map/all_to_all | solution.py:27
  23.1 146.0 %all-gather.9.cloned.1.call-start = ((), (), s32[]{:S(2)}) async-start(), calls=%async_computation.14 | async-start | bytes 4423680 | tf_op jit(solution)/shard_map/all_gather | solution.py:515
  77.0 29.7 %collective-permute-start.8 = (bf16[128,768]{1,0:T(8,128)(2,1)}, bf16[128,768]{1,0:T(8,128)(2,1)}, u32[]{:S(2)}, u32[]{:S(2)}) collective-permute-start(bf16[128,768]{1,0:T(8,128)(2,1)} %slice_bitcast_fusion.10), channel_id=1, source_target_pairs={{0,2},{1,3},{2,0},{3,1},{4,6},{5,7},{6,4},{7,5},{8,10},{9,11},{10,... | collective-permute-start | bytes 589832 | tf_op jit(solution)/shard_map/ppermute | solution.py:32
  82.6 53.7 %collective-permute-start.4 = (bf16[2,192,768]{2,1,0:T(8,128)(2,1)}, bf16[2,192,768]{2,1,0:T(8,128)(2,1)}, u32[]{:S(2)}, u32[]{:S(2)}) collective-permute-start(bf16[2,192,768]{2,1,0:T(8,128)(2,1)} %get-tuple-element.148), channel_id=1, source_target_pairs={{0,1},{1,2},{2,3},{3,0},{4,5},{5,6},{6,7},{7,4},{8,9},{9,10},{10,1... | collective-permute-start | bytes 1769480 | tf_op jit(solution)/shard_map/ppermute | solution.py:32
  83.8 53.7 %collective-permute-start.5 = (bf16[2,192,768]{2,1,0:T(8,128)(2,1)}, bf16[2,192,768]{2,1,0:T(8,128)(2,1)}, u32[]{:S(2)}, u32[]{:S(2)}) collective-permute-start(bf16[2,192,768]{2,1,0:T(8,128)(2,1)} %get-tuple-element.147), channel_id=1, source_target_pairs={{0,2},{1,3},{2,0},{3,1},{4,6},{5,7},{6,4},{7,5},{8,10},{9,11},{10,... | collective-permute-start | bytes 1769480 | tf_op jit(solution)/shard_map/ppermute | solution.py:32
  85.9 51.7 %collective-permute-start.6 = (bf16[2,192,768]{2,1,0:T(8,128)(2,1)}, bf16[2,192,768]{2,1,0:T(8,128)(2,1)}, u32[]{:S(2)}, u32[]{:S(2)}) collective-permute-start(bf16[2,192,768]{2,1,0:T(8,128)(2,1)} %get-tuple-element.146), channel_id=1, source_target_pairs={{0,3},{1,0},{2,1},{3,2},{4,7},{5,4},{6,5},{7,6},{8,11},{9,8},{10,9... | collective-permute-start | bytes 1769480 | tf_op jit(solution)/shard_map/ppermute | solution.py:32
  97.0 39.3 %collective-permute-start.9 = (bf16[128,768]{1,0:T(8,128)(2,1)}, bf16[128,768]{1,0:T(8,128)(2,1)}, u32[]{:S(2)}, u32[]{:S(2)}) collective-permute-start(bf16[128,768]{1,0:T(8,128)(2,1)} %slice_bitcast_fusion.10), channel_id=1, source_target_pairs={{0,3},{1,0},{2,1},{3,2},{4,7},{5,4},{6,5},{7,6},{8,11},{9,8},{10,9... | collective-permute-start | bytes 589832 | tf_op jit(solution)/shard_map/ppermute | solution.py:32
  100.7 62.8 %all-to-all-start.2 = ((bf16[32,64,128]{2,1,0:T(8,128)(2,1)}), bf16[32,64,128]{2,1,0:T(8,128)(2,1)}, u32[]{:S(2)}, u32[]{:S(2)}) async-start(bf16[32,64,128]{2,1,0:T(8,128)(2,1)} %pad_maximum_fusion.9), calls=%async_computation.2 | async-start | bytes 1048576 | tf_op jit(solution)/shard_map/all_to_all | solution.py:27
  184.1 32.0 %all-to-all-start.3 = ((bf16[32,96,128]{2,1,0:T(8,128)(2,1)}), bf16[32,96,128]{2,1,0:T(8,128)(2,1)S(1)}, u32[]{:S(2)}, u32[]{:S(2)}) async-start(bf16[32,96,128]{2,1,0:T(8,128)(2,1)} %copy-done.22), calls=%async_computation.3 | async-start | bytes 1572864 | tf_op jit(solution)/shard_map/all_to_all | solution.py:27
  206.1 44.4 %collective-permute-start.21 = (bf16[128,1536]{1,0:T(8,128)(2,1)}, bf16[128,1536]{1,0:T(8,128)(2,1)}, u32[]{:S(2)}, u32[]{:S(2)}) collective-permute-start(bf16[128,1536]{1,0:T(8,128)(2,1)} %get-tuple-element.165), channel_id=1, source_target_pairs={{0,2},{1,3},{2,0},{3,1},{4,6},{5,7},{6,4},{7,5},{8,10},{9,11},{10,... | collective-permute-start | bytes 1179656 | tf_op jit(solution)/shard_map/ppermute | solution.py:32
  208.9 41.5 %collective-permute-start.20 = (bf16[128,1536]{1,0:T(8,128)(2,1)}, bf16[128,1536]{1,0:T(8,128)(2,1)}, u32[]{:S(2)}, u32[]{:S(2)}) collective-permute-start(bf16[128,1536]{1,0:T(8,128)(2,1)} %get-tuple-element.166), channel_id=1, source_target_pairs={{0,1},{1,2},{2,3},{3,0},{4,5},{5,6},{6,7},{7,4},{8,9},{9,10},{10,1... | collective-permute-start | bytes 1179656 | tf_op jit(solution)/shard_map/ppermute | solution.py:32
  209.3 41.1 %collective-permute-start.19 = (bf16[128,1536]{1,0:T(8,128)(2,1)}, bf16[128,1536]{1,0:T(8,128)(2,1)}, u32[]{:S(2)}, u32[]{:S(2)}) collective-permute-start(bf16[128,1536]{1,0:T(8,128)(2,1)} %get-tuple-element.164), channel_id=1, source_target_pairs={{0,3},{1,0},{2,1},{3,2},{4,7},{5,4},{6,5},{7,6},{8,11},{9,8},{10,9... | collective-permute-start | bytes 1179656 | tf_op jit(solution)/shard_map/ppermute | solution.py:32
  211.6 35.5 %collective-permute-start.29 = (bf16[192,768]{1,0:T(8,128)(2,1)}, bf16[192,768]{1,0:T(8,128)(2,1)}, u32[]{:S(2)}, u32[]{:S(2)}) collective-permute-start(bf16[192,768]{1,0:T(8,128)(2,1)} %get-tuple-element.168), channel_id=1, source_target_pairs={{0,2},{1,3},{2,0},{3,1},{4,6},{5,7},{6,4},{7,5},{8,10},{9,11},{10,... | collective-permute-start | bytes 884744 | tf_op jit(solution)/shard_map/ppermute | solution.py:32
  214.4 34.3 %collective-permute-start.30 = (bf16[192,768]{1,0:T(8,128)(2,1)}, bf16[192,768]{1,0:T(8,128)(2,1)}, u32[]{:S(2)}, u32[]{:S(2)}) collective-permute-start(bf16[192,768]{1,0:T(8,128)(2,1)} %get-tuple-element.167), channel_id=1, source_target_pairs={{0,3},{1,0},{2,1},{3,2},{4,7},{5,4},{6,5},{7,6},{8,11},{9,8},{10,9... | collective-permute-start | bytes 884744 | tf_op jit(solution)/shard_map/ppermute | solution.py:32
  230.4 33.5 %all-to-all-start.4 = ((bf16[32,128,128]{2,1,0:T(8,128)(2,1)}), bf16[32,128,128]{2,1,0:T(8,128)(2,1)S(1)}, u32[]{:S(2)}, u32[]{:S(2)}) async-start(bf16[32,128,128]{2,1,0:T(8,128)(2,1)} %copy-done.19), calls=%async_computation.4 | async-start | bytes 2097152 | tf_op jit(solution)/shard_map/all_to_all | solution.py:27
  297.4 43.6 %all-to-all-start.6 = ((bf16[32,96,128]{2,1,0:T(8,128)(2,1)}), bf16[32,96,128]{2,1,0:T(8,128)(2,1)S(1)}, u32[]{:S(2)}, u32[]{:S(2)}) async-start(bf16[32,96,128]{2,1,0:T(8,128)(2,1)} %attend_back.3), calls=%async_computation.6 | async-start | bytes 1572864 | tf_op jit(solution)/shard_map/all_to_all | solution.py:27
  302.5 148.8 %reduce-scatter.2.cloned.1.call-start = ((), (), s32[]{:S(2)}) async-start(), calls=%async_computation.12 | async-start | bytes 5677056 | tf_op jit(solution)/shard_map/reduce_scatter | solution.py:578
  347.7 24.7 %collective-permute-start.33 = (bf16[128,768]{1,0:T(8,128)(2,1)}, bf16[128,768]{1,0:T(8,128)(2,1)S(1)}, u32[]{:S(2)}, u32[]{:S(2)}) collective-permute-start(bf16[128,768]{1,0:T(8,128)(2,1)} %get-tuple-element.182), channel_id=1, source_target_pairs={{0,2},{1,3},{2,0},{3,1},{4,6},{5,7},{6,4},{7,5},{8,10},{9,11},{10,... | collective-permute-start | bytes 589832 | tf_op jit(solution)/shard_map/ppermute | solution.py:32
  381.4 28.1 %all-to-all-start.7 = ((bf16[4,392,576]{2,1,0:T(8,128)(2,1)}), bf16[4,392,576]{2,1,0:T(8,128)(2,1)S(1)}, u32[]{:S(2)}, u32[]{:S(2)}) async-start(bf16[4,392,576]{2,1,0:T(8,128)(2,1)} %pad_maximum_fusion.4), calls=%async_computation.7 | async-start | bytes 4014080 | tf_op jit(solution)/shard_map/all_to_all | solution.py:27
  385.2 123.6 %all-gather.7.cloned.1.call-start = ((), (), s32[]{:S(2)}) async-start(), calls=%async_computation.13 | async-start | bytes 5677056 | tf_op jit(solution)/shard_map/all_gather | solution.py:614
  452.8 33.9 %all-to-all-start.9 = ((bf16[32,48,576]{2,1,0:T(8,128)(2,1)}), bf16[32,48,576]{2,1,0:T(8,128)(2,1)S(1)}, u32[]{:S(2)}, u32[]{:S(2)}) async-start(bf16[32,48,576]{2,1,0:T(8,128)(2,1)} %broadcast_in_dim.108), calls=%async_computation.9 | async-start | bytes 3932160 | tf_op jit(solution)/shard_map/all_to_all | solution.py:27
  (125 other events, 1377.9 us)
Sparse Core Ops, SparseCore 0:
  9.7 47.8 all-gather.4
  59.8 73.0 all-gather.8
  341.1 88.2 reduce-scatter.1
  451.4 57.3 all-gather.6

commit v5 on v4

--- a/solution.py
+++ b/solution.py
@@ -1,3 +1,5 @@
+from functools import partial
+
 import jax
 import jax.numpy as jnp
 from jax import lax
@@ -425,6 +427,28 @@
     )
 
 
+def finish_kernel(unit, depth, wide_ref, up_ref, down_ref, out_ref):
+    width = wide_ref.shape[1]
+    for layer in range(LAYERS):
+        at = layer * (unit + width)
+        down_ref[layer] = wide_ref[at : at + unit, :].astype(F32)
+        for block in range(4):
+            row = at + unit + block * depth
+            up_ref[layer, :, block * unit : (block + 1) * unit] = wide_ref[row : row + depth, :].astype(F32)
+        at = LAYERS * (unit + width) + layer * depth
+        out_ref[layer] = wide_ref[at : at + depth, :].astype(F32)
+
+
+def finish(wide, unit, depth):
+    width = wide.shape[1]
+    shapes = (
+        shaped((LAYERS, depth, 4 * unit), F32),
+        shaped((LAYERS, unit, width), F32),
+        shaped((LAYERS, depth, width), F32),
+    )
+    return on_chip(partial(finish_kernel, unit, depth), shapes, "finish", 5_000_000, wide)
+
+
 def rotary_tables(seqs):
     device = lax.axis_index("ctx")
     devices = lax.axis_size("ctx")
@@ -512,46 +536,51 @@
         {"g_attn": ln_gain_attn, "s_attn": ln_shift_attn, "g_mlp": ln_gain_mlp, "s_mlp": ln_shift_mlp, "b_qv": b_qv, "b_out": b_out, "b_down": b_down}
     )
     half1 = gather_half(w_qkv[0])
-    qkv = [gather_rest(half1), lax.all_gather(w_qkv[1], "wt", axis=0, tiled=True)]
-    out_both = lax.all_gather(w_out, "wt", axis=1, tiled=True)
+    out_both = lax.all_gather(after(w_out, half1), "wt", axis=1, tiled=True)
     layers = []
     for layer in range(LAYERS):
         w = {name: small[name][layer][None] for name in small}
         w["b_q"] = w["b_qv"][:, :width]
         w["b_v"] = w["b_qv"][:, width:]
-        w["qkv"] = qkv[layer]
         w["out"] = out_both[layer]
         w["down"] = w_down[layer]
         w["b_up"] = b_up[layer].astype(F32)[None]
         layers.append(w)
     first, second = layers
+    first["qkv"] = gather_rest(half1)
     g2 = cotangent.reshape(rows, width)
     x1 = tokens_in.reshape(rows, width).astype(F32)
     xhat1, send1, scale1, packed1 = mix(x1, first, tables, jnp.zeros((1, rows, 128), BF16))
-    later_up, send1 = after((w_up, send1), packed1)
+    later_up, later_qkv, send1 = after((w_up, w_qkv[1], send1), packed1)
     packed1 = exchange(packed1, "ctx")
-    ups = jnp.stack([later_up[:, :, i * unit : (i + 1) * unit] for i in range(4)])
-    ups = group_trade(ups)
     spread1 = group_spread(send1[0, :, :width])
+
+    def up_columns(value):
+        return group_trade(jnp.stack([value[:, i * unit : (i + 1) * unit] for i in range(4)]))
+
+    ups = up_columns(later_up[0])
+    half2 = gather_half(later_qkv)
     out1, full1, lse1 = attend(packed1)
-    both1 = jnp.concatenate([out1, pull(g2, second)], axis=1)
-    ups, spread1, later_g2 = after((ups, spread1, g2), both1)
-    both1 = exchange(both1, "ctx")
-    ups = place([b[:, None] for b in ups], 1).reshape(LAYERS, width, unit)
-    first["up"], second["up"] = ups[0], ups[1]
+    ups, spread1, later_g2, later_up, half2 = after((ups, spread1, g2, w_up[1], half2), out1)
+    out1 = exchange(out1, "ctx")
+    first["up"] = place([b[None] for b in ups], 0).reshape(width, unit)
+    second["up"] = place([b[None] for b in up_columns(later_up)], 0).reshape(width, unit)
+    second["qkv"] = gather_rest(half2)
     xhat1_all = jnp.concatenate(spread1, axis=0)
     n_mlp1, hidden1, active1, partial1 = mlp_forward(xhat1_all, first)
     mlp1 = own_sum(partial1)
-    out1, grads2 = both1[:, :BLK], both1[:, BLK:]
     split1, x2 = join(out1, x1, mlp1, first)
     xhat2, send2, scale2, packed2 = mix(x2, second, tables, split1)
-    packed2 = exchange(packed2, "ctx")
+    packed2 = exchange(jnp.concatenate([packed2, pull(g2, second)], axis=1), "ctx")
+    packed2, grads2 = packed2[:, : 3 * BLK], packed2[:, 3 * BLK :]
     g2_all = jnp.concatenate(group_spread(after(later_g2, mlp1)), axis=0)
     landed2 = jnp.concatenate(group_trade(send2), axis=0)
     xhat2_all, context1_all = landed2[:, :width], landed2[:, width:]
     n_mlp2, hidden2, active2, partial2 = mlp_forward(xhat2_all, second)
     out2, full2, lse2 = attend(packed2)
-    back2 = exchange(attend_back(packed2, grads2, full2, lse2, out2), "ctx")
+    back2 = attend_back(packed2, grads2, full2, lse2, out2)
+    done2 = back2
+    back2 = exchange(back2, "ctx")
     back_partial2, grad_down2, grad_up2, grad_b_up2 = mlp_backward(g2_all, n_mlp2, hidden2, active2, second)
     sums = own_sum(jnp.concatenate([partial2, back_partial2], axis=1))
     mlp2, grad_n_mlp2 = sums[:, :width], sums[:, width:]
@@ -569,7 +598,8 @@
     grad_out1 = dot(context1_all, g1_all, TN).astype(BF16)
     grad_out2 = dot(context2_all, g2_all, TN).astype(BF16)
     n_attn2_all = (xhat2_all.astype(F32) * second["g_attn"] + second["s_attn"]).astype(BF16)
-    grad_up2 = place([b[None] for b in group_trade(grad_up2)], 0).reshape(width, unit)
+    grad_up2 = group_trade(after(grad_up2, done2))
+    grad_up2 = place([b[None] for b in grad_up2], 0).reshape(width, unit)
     ready = [grad_down1, grad_up1, grad_down2, grad_up2, grad_out1, grad_out2]
     lines = sum(v.shape[0] for v in ready)
     lines = -(-lines // (16 * devices)) * 16 * devices - lines
@@ -612,9 +642,7 @@
 
     qkvs = spread(landed[: 2 * piece].astype(BF16), "ctx")
     wide = lax.all_gather(after(wide, landed), "ctx", axis=0, tiled=True)
-    at = 2 * (unit + width)
-    down1, up1 = wide[:unit], wide[unit : unit + width].reshape(4, depth, unit)
-    down2, up2 = wide[unit + width : 2 * unit + width], wide[2 * unit + width : at].reshape(4, depth, unit)
+    grad_up, grad_down, grad_out = finish(wide, unit, depth)
     qkvs = [side_by_side(qkvs[:, i * piece : (i + 1) * piece].reshape(4, depth, columns)) for i in range(LAYERS)]
     flat = landed[2 * piece :].reshape(-1)
     per_layer = [flat[layer * tiny_size : (layer + 1) * tiny_size] for layer in range(LAYERS)]
@@ -638,11 +666,11 @@
         vector(3),
         grad_qkv,
         grad_b_qv,
-        both(wide[at : at + depth], wide[at + depth : at + 2 * depth]),
+        grad_out,
         grad_bias,
-        both(side_by_side(up1), side_by_side(up2)),
+        grad_up,
         grad_b_up,
-        both(down1, down2),
+        grad_down,
         grad_bias,
     )
 

time: 545 us -> 534 us (0.980)
  local copies, waits for them, and re-layouts: 92.7 us -> 81.7 us
  Pallas kernels: 46.8 us -> 53 us
    ppermute x36 -> x42, waiting for transfers between devices: 82.7 us -> 95.7 us  [pass_on(): lax.ppermute(value, 'wt', [(i, (i + shift) % count) for i in range(count)])]
    all_to_all x9, waiting for transfers between devices: 67.1 us -> 54.4 us  [exchange(): return lax.all_to_all(chunks, axis, 0, 0, tiled=True)]
    convert_element_type x8 -> x4, local copies, waits for them, and re-layouts: 12.7 us -> 2.93 us  [both(): return jnp.stack([one.astype(F32), two.astype(F32)])]
    another operation x4 -> x1, other arithmetic: 8.1 us -> 2.03 us  [both(): return jnp.stack([one.astype(F32), two.astype(F32)])]
    pallas_call x10 -> x11, Pallas kernels: 19.4 us -> 24.9 us  [on_chip(): pl.pallas_call(kernel, out_shape=out_shape, in_specs=[spec] * len(operand...]
    dynamic_update_slice x13 -> x19, local copies, waits for them, and re-layouts: 9.95 us -> 13.1 us  [place(): lax.dynamic_update_slice_in_dim(whole, blocks[shift], (here - shift) % 4...]
    ppermute x36 -> x42, starting transfers between devices: 47.3 us -> 48.2 us  [pass_on(): lax.ppermute(value, 'wt', [(i, (i + shift) % count) for i in range(count)])]
  transfers between devices with their start and end apart: 50 -> 56, of which waited for: 18 -> 21; matrix products, arithmetic and copies ran while one was open for 22% -> 22% of each run, Pallas kernels for 8% -> 9%
where the time goes in v5:
time: 534 us; the launch traced here: 525 us
  waiting for transfers between devices  167 us (31%)
  starting transfers between devices  111 us (21%)
  local copies, waits for them, and re-layouts  81.7 us (15%)
  Pallas kernels  53 us (10%)
  blocking collectives  39.8 us (7%)
  other arithmetic  28.1 us (5%)
  matrix products  28 us (5%)
  between operations  15.9 us (3%)
    ppermute x42, waiting for transfers between devices, pass_on(): lax.ppermute(value, 'wt', [(i, (i + shift) % count) for i in range(count)])  95.7 us
    all_to_all x9, starting transfers between devices, exchange(): return lax.all_to_all(chunks, axis, 0, 0, tiled=True)  59.9 us
    all_to_all x9, waiting for transfers between devices, exchange(): return lax.all_to_all(chunks, axis, 0, 0, tiled=True)  54.4 us
    ppermute x42, starting transfers between devices, pass_on(): lax.ppermute(value, 'wt', [(i, (i + shift) % count) for i in range(count)])  48.2 us
    all_to_all x1, blocking collectives, exchange(): return lax.all_to_all(chunks, axis, 0, 0, tiled=True)  39.8 us
    dot_general x16, matrix products, dot(): return lax.dot_general(left, right, dims, preferred_element_type=F32)  28 us
    pallas_call x11, Pallas kernels, on_chip(): pl.pallas_call(kernel, out_shape=out_shape, in_specs=[spec] * len(operand...  24.9 us
    unnamed x204, local copies, waits for them, and re-layouts  24.4 us
  transfers between devices with their start and end apart: 56, of which 21 were waited for; matrix products, arithmetic and copies ran while one was open for 22% of the time, Pallas kernels for 9%

profile of v5, /device:TPU:1, one launch (start us, length us, event | category | flops | bytes accessed | tf_op | source)
XLA Modules:
  0.0 524.7 jit_solution(17457321834085224922)
XLA Ops:
  28.3 8.4 %collective-permute-done.1 = bf16[96,2304]{1,0:T(8,128)(2,1)S(1)} collective-permute-done((bf16[96,2304]{1,0:T(8,128)(2,1)S(1)}, bf16[96,2304]{1,0:T(8,128)(2,1)S(1)}, u32[]{:S(2)}, u32[]{:S(2)}) %collective-permute-start.1) | collective-permute-done | bytes 442400 | tf_op jit(solution)/shard_map/ppermute | solution.py:34
  56.3 7.2 %all-to-all-start.1 = ((bf16[32,96,128]{2,1,0:T(8,128)(2,1)}), bf16[32,96,128]{2,1,0:T(8,128)(2,1)S(1)}, u32[]{:S(2)}, u32[]{:S(2)}) async-start(bf16[32,96,128]{2,1,0:T(8,128)(2,1)} %get-tuple-element.79), calls=%async_computation.1 | async-start | bytes 1572864 | tf_op jit(solution)/shard_map/all_to_all | solution.py:29
  73.0 25.3 %collective-permute-done.10 = bf16[96,2304]{1,0:T(8,128)(2,1)S(1)} collective-permute-done((bf16[96,2304]{1,0:T(8,128)(2,1)S(1)}, bf16[96,2304]{1,0:T(8,128)(2,1)S(1)}, u32[]{:S(2)}, u32[]{:S(2)}) %collective-permute-start.10) | collective-permute-done | bytes 442400 | tf_op jit(solution)/shard_map/ppermute | solution.py:34
  99.6 8.4 %collective-permute-done.11 = bf16[96,2304]{1,0:T(8,128)(2,1)S(1)} collective-permute-done((bf16[96,2304]{1,0:T(8,128)(2,1)S(1)}, bf16[96,2304]{1,0:T(8,128)(2,1)S(1)}, u32[]{:S(2)}, u32[]{:S(2)}) %collective-permute-start.11) | collective-permute-done | bytes 442400 | tf_op jit(solution)/shard_map/ppermute | solution.py:34
  112.5 5.7 %attend.2 = (bf16[32,32,128]{2,1,0:T(8,128)(2,1)}, f32[128,1024]{1,0:T(8,128)S(1)}, f32[8,1024]{1,0:T(8,128)S(1)}) custom-call(bf16[32,96,128]{2,1,0:T(8,128)(2,1)S(1)} %all-to-all-done.1.in_ref), custom_call_target="tpu_custom_call" | custom-call | flops 20000000000 | bytes 20000000 | tf_op jit(solution)/shard_map/attend/pallas_call | solution.py:210
  119.0 12.0 %all-to-all-start.2 = ((bf16[32,32,128]{2,1,0:T(8,128)(2,1)}), bf16[32,32,128]{2,1,0:T(8,128)(2,1)S(1)}, u32[]{:S(2)}, u32[]{:S(2)}) async-start(bf16[32,32,128]{2,1,0:T(8,128)(2,1)} %get-tuple-element.80), calls=%async_computation.2 | async-start | bytes 524288 | tf_op jit(solution)/shard_map/all_to_all | solution.py:29
  158.8 4.4 collective-permute-done.21
  163.6 4.7 collective-permute-done.23
  191.7 9.2 %all-to-all-start.3 = ((bf16[32,128,128]{2,1,0:T(8,128)(2,1)}), bf16[32,128,128]{2,1,0:T(8,128)(2,1)S(1)}, u32[]{:S(2)}, u32[]{:S(2)}) async-start(bf16[32,128,128]{2,1,0:T(8,128)(2,1)} %pad_maximum_fusion.8), calls=%async_computation.3 | async-start | bytes 2097152 | tf_op jit(solution)/shard_map/all_to_all | solution.py:29
  218.9 4.9 attend.3
  223.9 8.4 %attend_back.2 = bf16[32,128,128]{2,1,0:T(8,128)(2,1)S(1)} custom-call(bf16[32,96,128]{2,1,0:T(8,128)(2,1)S(1)} %slice.474.in_ref, bf16[32,32,128]{2,1,0:T(8,128)(2,1)S(1)} %slice.475.grad_ref, f32[128,1024]{1,0:T(8,128)S(1)} %get-tuple-element.98.full_ref, f32[8,1024]{1,0:T(8,128)S(1)} %get-tuple-element.99.lse_ref, ...), custom_call_target="tpu_custom_call" | custom-call | flops 40000000000 | bytes 40000000 | tf_op jit(solution)/shard_map/attend_back/pallas_call | solution.py:234
  233.3 8.2 %all-to-all-start.4 = ((bf16[32,128,128]{2,1,0:T(8,128)(2,1)}), bf16[32,128,128]{2,1,0:T(8,128)(2,1)S(1)}, u32[]{:S(2)}, u32[]{:S(2)}) async-start(bf16[32,128,128]{2,1,0:T(8,128)(2,1)} %copy-done.20), calls=%async_computation.4 | async-start | bytes 2097152 | tf_op jit(solution)/shard_map/all_to_all | solution.py:29
  250.2 10.8 %collective-permute-done.35 = bf16[192,768]{1,0:T(8,128)(2,1)S(1)} collective-permute-done((bf16[192,768]{1,0:T(8,128)(2,1)S(1)}, bf16[192,768]{1,0:T(8,128)(2,1)S(1)}, u32[]{:S(2)}, u32[]{:S(2)}) %collective-permute-start.35) | collective-permute-done | bytes 294944 | tf_op jit(solution)/shard_map/ppermute | solution.py:34
  273.9 8.1 %all-to-all-start.5 = ((bf16[32,32,128]{2,1,0:T(8,128)(2,1)}), bf16[32,32,128]{2,1,0:T(8,128)(2,1)S(1)}, u32[]{:S(2)}, u32[]{:S(2)}) async-start(bf16[32,32,128]{2,1,0:T(8,128)(2,1)} %pull.3), calls=%async_computation.5 | async-start | bytes 524288 | tf_op jit(solution)/shard_map/all_to_all | solution.py:29
  286.4 4.5 all-to-all-done.5.grad_ref
  291.0 9.1 %attend_back.3 = bf16[32,96,128]{2,1,0:T(8,128)(2,1)} custom-call(bf16[32,96,128]{2,1,0:T(8,128)(2,1)S(1)} %copy-done.22, bf16[32,32,128]{2,1,0:T(8,128)(2,1)S(1)} %all-to-all-done.5.grad_ref, f32[128,1024]{1,0:T(8,128)S(1)} %copy-done.43, f32[8,1024]{1,0:T(8,128)S(1)} %copy-done.32, bf16[1,8,1024]{2,1,0:T(8,128)(2,1)S(1)} %convert_bitcast_fusion.carry_ref), custom_call_target="tpu_custom_call" | custom-call | flops 40000000000 | bytes 40000000 | tf_op jit(solution)/shard_map/attend_back/pallas_call | solution.py:234
  318.7 10.9 %collective-permute-done.32 = bf16[192,768]{1,0:T(8,128)(2,1)S(1)} collective-permute-done((bf16[192,768]{1,0:T(8,128)(2,1)S(1)}, bf16[192,768]{1,0:T(8,128)(2,1)S(1)}, u32[]{:S(2)}, u32[]{:S(2)}) %collective-permute-start.32) | collective-permute-done | bytes 294944 | tf_op jit(solution)/shard_map/ppermute | solution.py:34
  375.1 4.4 norm_back.3
  386.8 24.8 %all-to-all-done.7 = bf16[4,392,576]{2,1,0:T(8,128)(2,1)S(1)} async-done(((bf16[4,392,576]{2,1,0:T(8,128)(2,1)}), bf16[4,392,576]{2,1,0:T(8,128)(2,1)S(1)}, u32[]{:S(2)}, u32[]{:S(2)}) %all-to-all-start.7) | async-done | bytes 1806368 | tf_op jit(solution)/shard_map/all_to_all | solution.py:29
  412.3 39.8 %all_to_all.50 = bf16[32,56,576]{2,1,0:T(8,128)(2,1)S(1)} all-to-all(bf16[32,56,576]{2,1,0:T(8,128)(2,1)S(1)} %pad_maximum_fusion.3), channel_id=1, replica_groups=mesh['ctx'=32,'wt'=4] {'ctx'}, dimensions={0} | all-to-all | bytes 4128768 | tf_op jit(solution)/shard_map/all_to_all | solution.py:29
  453.9 4.5 all-to-all-start.9
  462.8 25.1 %all-to-all-done.9 = bf16[32,48,576]{2,1,0:T(8,128)(2,1)S(1)} async-done(((bf16[32,48,576]{2,1,0:T(8,128)(2,1)}), bf16[32,48,576]{2,1,0:T(8,128)(2,1)S(1)}, u32[]{:S(2)}, u32[]{:S(2)}) %all-to-all-start.9) | async-done | bytes 1769504 | tf_op jit(solution)/shard_map/all_to_all | solution.py:29
  493.1 17.1 %all-gather.5.cloned.1.call-done.wide_ref = bf16[3584,768]{1,0:T(8,128)(2,1)} async-done(((bf16[112,768]{1,0:T(8,128)(2,1)}), bf16[3584,768]{1,0:T(8,128)(2,1)}) %all-gather.5.cloned.1.call-update) | async-done | bytes 5505040 | tf_op jit(solution)/shard_map/all_gather | solution.py:644
  512.8 4.5 finish.1
  (504 shorter events, 238.4 us)
Async XLA Ops:
  22.4 150.0 %all-gather.3.cloned.1.call-start = ((), (), s32[]{:S(2)}) async-start(), calls=%async_computation.11 | async-start | bytes 2949120 | tf_op jit(solution)/shard_map/all_gather | solution.py:539
  56.3 56.1 %all-to-all-start.1 = ((bf16[32,96,128]{2,1,0:T(8,128)(2,1)}), bf16[32,96,128]{2,1,0:T(8,128)(2,1)S(1)}, u32[]{:S(2)}, u32[]{:S(2)}) async-start(bf16[32,96,128]{2,1,0:T(8,128)(2,1)} %get-tuple-element.79), calls=%async_computation.1 | async-start | bytes 1572864 | tf_op jit(solution)/shard_map/all_to_all | solution.py:29
  64.2 45.4 %collective-permute-start.7 = (bf16[128,768]{1,0:T(8,128)(2,1)}, bf16[128,768]{1,0:T(8,128)(2,1)S(1)}, u32[]{:S(2)}, u32[]{:S(2)}) collective-permute-start(bf16[128,768]{1,0:T(8,128)(2,1)} %slice_bitcast_fusion.13), channel_id=1, source_target_pairs={{0,1},{1,2},{2,3},{3,0},{4,5},{5,6},{6,7},{7,4},{8,9},{9,10},{10,1... | collective-permute-start | bytes 589832 | tf_op jit(solution)/shard_map/ppermute | solution.py:34
  64.3 66.7 %collective-permute-start.8 = (bf16[128,768]{1,0:T(8,128)(2,1)}, bf16[128,768]{1,0:T(8,128)(2,1)}, u32[]{:S(2)}, u32[]{:S(2)}) collective-permute-start(bf16[128,768]{1,0:T(8,128)(2,1)} %slice_bitcast_fusion.13), channel_id=1, source_target_pairs={{0,2},{1,3},{2,0},{3,1},{4,6},{5,7},{6,4},{7,5},{8,10},{9,11},{10,... | collective-permute-start | bytes 589832 | tf_op jit(solution)/shard_map/ppermute | solution.py:34
  66.4 64.6 %collective-permute-start.9 = (bf16[128,768]{1,0:T(8,128)(2,1)}, bf16[128,768]{1,0:T(8,128)(2,1)}, u32[]{:S(2)}, u32[]{:S(2)}) collective-permute-start(bf16[128,768]{1,0:T(8,128)(2,1)} %slice_bitcast_fusion.13), channel_id=1, source_target_pairs={{0,3},{1,0},{2,1},{3,2},{4,7},{5,4},{6,5},{7,6},{8,11},{9,8},{10,9... | collective-permute-start | bytes 589832 | tf_op jit(solution)/shard_map/ppermute | solution.py:34
  70.5 27.8 %collective-permute-start.10 = (bf16[96,2304]{1,0:T(8,128)(2,1)S(1)}, bf16[96,2304]{1,0:T(8,128)(2,1)S(1)}, u32[]{:S(2)}, u32[]{:S(2)}) collective-permute-start(bf16[96,2304]{1,0:T(8,128)(2,1)S(1)} %get-tuple-element.151), channel_id=1, source_target_pairs={{0,1},{1,2},{2,3},{3,0},{4,5},{5,6},{6,7},{7,4},{8,9},{9,10},{10,1... | collective-permute-start | bytes 1327112 | tf_op jit(solution)/shard_map/ppermute | solution.py:34
  70.5 37.4 %collective-permute-start.11 = (bf16[96,2304]{1,0:T(8,128)(2,1)S(1)}, bf16[96,2304]{1,0:T(8,128)(2,1)S(1)}, u32[]{:S(2)}, u32[]{:S(2)}) collective-permute-start(bf16[96,2304]{1,0:T(8,128)(2,1)S(1)} %get-tuple-element.151), channel_id=1, source_target_pairs={{0,2},{1,3},{2,0},{3,1},{4,6},{5,7},{6,4},{7,5},{8,10},{9,11},{10,... | collective-permute-start | bytes 1327112 | tf_op jit(solution)/shard_map/ppermute | solution.py:34
  108.0 23.0 %collective-permute-start.4 = (bf16[192,768]{1,0:T(8,128)(2,1)}, bf16[192,768]{1,0:T(8,128)(2,1)}, u32[]{:S(2)}, u32[]{:S(2)}) collective-permute-start(bf16[192,768]{1,0:T(8,128)(2,1)} %get-tuple-element.189), channel_id=1, source_target_pairs={{0,1},{1,2},{2,3},{3,0},{4,5},{5,6},{6,7},{7,4},{8,9},{9,10},{10,1... | collective-permute-start | bytes 884744 | tf_op jit(solution)/shard_map/ppermute | solution.py:34
  119.0 55.3 %all-to-all-start.2 = ((bf16[32,32,128]{2,1,0:T(8,128)(2,1)}), bf16[32,32,128]{2,1,0:T(8,128)(2,1)S(1)}, u32[]{:S(2)}, u32[]{:S(2)}) async-start(bf16[32,32,128]{2,1,0:T(8,128)(2,1)} %get-tuple-element.80), calls=%async_computation.2 | async-start | bytes 524288 | tf_op jit(solution)/shard_map/all_to_all | solution.py:29
  142.7 34.0 %collective-permute-start.16 = (bf16[4,96,2304]{2,1,0:T(8,128)(2,1)}, bf16[4,96,2304]{2,1,0:T(8,128)(2,1)}, u32[]{:S(2)}, u32[]{:S(2)}) collective-permute-start(bf16[4,96,2304]{2,1,0:T(8,128)(2,1)} %bitcast_dynamic-update-slice_fusion), channel_id=1, source_target_pairs={{0,4},{4,0},{8,12},{12,8},{16,20},{20,16},{24,28},{28,24},{32,36},... | collective-permute-start | bytes 5308424 | tf_op jit(solution)/shard_map/ppermute | solution.py:79
  163.1 24.3 %collective-permute-start.25 = (bf16[128,768]{1,0:T(8,128)(2,1)}, bf16[128,768]{1,0:T(8,128)(2,1)}, u32[]{:S(2)}, u32[]{:S(2)}) collective-permute-start(bf16[128,768]{1,0:T(8,128)(2,1)} %bitcast.27.g_ref), channel_id=1, source_target_pairs={{0,3},{1,0},{2,1},{3,2},{4,7},{5,4},{6,5},{7,6},{8,11},{9,8},{10,9... | collective-permute-start | bytes 589832 | tf_op jit(solution)/shard_map/ppermute | solution.py:34
  191.7 27.2 %all-to-all-start.3 = ((bf16[32,128,128]{2,1,0:T(8,128)(2,1)}), bf16[32,128,128]{2,1,0:T(8,128)(2,1)S(1)}, u32[]{:S(2)}, u32[]{:S(2)}) async-start(bf16[32,128,128]{2,1,0:T(8,128)(2,1)} %pad_maximum_fusion.8), calls=%async_computation.3 | async-start | bytes 2097152 | tf_op jit(solution)/shard_map/all_to_all | solution.py:29
  211.2 33.9 %collective-permute-start.28 = (bf16[128,1536]{1,0:T(8,128)(2,1)}, bf16[128,1536]{1,0:T(8,128)(2,1)}, u32[]{:S(2)}, u32[]{:S(2)}) collective-permute-start(bf16[128,1536]{1,0:T(8,128)(2,1)} %get-tuple-element.169), channel_id=1, source_target_pairs={{0,2},{1,3},{2,0},{3,1},{4,6},{5,7},{6,4},{7,5},{8,10},{9,11},{10,... | collective-permute-start | bytes 1179656 | tf_op jit(solution)/shard_map/ppermute | solution.py:34
  214.2 30.9 %collective-permute-start.27 = (bf16[128,1536]{1,0:T(8,128)(2,1)}, bf16[128,1536]{1,0:T(8,128)(2,1)}, u32[]{:S(2)}, u32[]{:S(2)}) collective-permute-start(bf16[128,1536]{1,0:T(8,128)(2,1)} %get-tuple-element.170), channel_id=1, source_target_pairs={{0,1},{1,2},{2,3},{3,0},{4,5},{5,6},{6,7},{7,4},{8,9},{9,10},{10,1... | collective-permute-start | bytes 1179656 | tf_op jit(solution)/shard_map/ppermute | solution.py:34
  214.2 30.9 %collective-permute-start.26 = (bf16[128,1536]{1,0:T(8,128)(2,1)}, bf16[128,1536]{1,0:T(8,128)(2,1)}, u32[]{:S(2)}, u32[]{:S(2)}) collective-permute-start(bf16[128,1536]{1,0:T(8,128)(2,1)} %get-tuple-element.168), channel_id=1, source_target_pairs={{0,3},{1,0},{2,1},{3,2},{4,7},{5,4},{6,5},{7,6},{8,11},{9,8},{10,9... | collective-permute-start | bytes 1179656 | tf_op jit(solution)/shard_map/ppermute | solution.py:34
  233.3 29.2 %all-to-all-start.4 = ((bf16[32,128,128]{2,1,0:T(8,128)(2,1)}), bf16[32,128,128]{2,1,0:T(8,128)(2,1)S(1)}, u32[]{:S(2)}, u32[]{:S(2)}) async-start(bf16[32,128,128]{2,1,0:T(8,128)(2,1)} %copy-done.20), calls=%async_computation.4 | async-start | bytes 2097152 | tf_op jit(solution)/shard_map/all_to_all | solution.py:29
  248.4 81.3 %collective-permute-start.37 = (bf16[192,768]{1,0:T(8,128)(2,1)}, bf16[192,768]{1,0:T(8,128)(2,1)}, u32[]{:S(2)}, u32[]{:S(2)}) collective-permute-start(bf16[192,768]{1,0:T(8,128)(2,1)} %get-tuple-element.171), channel_id=1, source_target_pairs={{0,3},{1,0},{2,1},{3,2},{4,7},{5,4},{6,5},{7,6},{8,11},{9,8},{10,9... | collective-permute-start | bytes 884744 | tf_op jit(solution)/shard_map/ppermute | solution.py:34
  300.0 42.1 %all-to-all-start.6 = ((bf16[32,96,128]{2,1,0:T(8,128)(2,1)}), bf16[32,96,128]{2,1,0:T(8,128)(2,1)S(1)}, u32[]{:S(2)}, u32[]{:S(2)}) async-start(bf16[32,96,128]{2,1,0:T(8,128)(2,1)} %attend_back.3), calls=%async_computation.6 | async-start | bytes 1572864 | tf_op jit(solution)/shard_map/all_to_all | solution.py:29
  303.8 148.6 %reduce-scatter.2.cloned.1.call-start = ((), (), s32[]{:S(2)}) async-start(), calls=%async_computation.12 | async-start | bytes 5677056 | tf_op jit(solution)/shard_map/reduce_scatter | solution.py:608
  348.8 25.1 %collective-permute-start.40 = (bf16[128,768]{1,0:T(8,128)(2,1)}, bf16[128,768]{1,0:T(8,128)(2,1)S(1)}, u32[]{:S(2)}, u32[]{:S(2)}) collective-permute-start(bf16[128,768]{1,0:T(8,128)(2,1)} %get-tuple-element.202), channel_id=1, source_target_pairs={{0,2},{1,3},{2,0},{3,1},{4,6},{5,7},{6,4},{7,5},{8,10},{9,11},{10,... | collective-permute-start | bytes 589832 | tf_op jit(solution)/shard_map/ppermute | solution.py:34
  349.6 24.3 %collective-permute-start.39 = (bf16[128,768]{1,0:T(8,128)(2,1)}, bf16[128,768]{1,0:T(8,128)(2,1)S(1)}, u32[]{:S(2)}, u32[]{:S(2)}) collective-permute-start(bf16[128,768]{1,0:T(8,128)(2,1)} %get-tuple-element.203), channel_id=1, source_target_pairs={{0,1},{1,2},{2,3},{3,0},{4,5},{5,6},{6,7},{7,4},{8,9},{9,10},{10,1... | collective-permute-start | bytes 589832 | tf_op jit(solution)/shard_map/ppermute | solution.py:34
  382.9 28.6 %all-to-all-start.7 = ((bf16[4,392,576]{2,1,0:T(8,128)(2,1)}), bf16[4,392,576]{2,1,0:T(8,128)(2,1)S(1)}, u32[]{:S(2)}, u32[]{:S(2)}) async-start(bf16[4,392,576]{2,1,0:T(8,128)(2,1)} %pad_maximum_fusion.4), calls=%async_computation.7 | async-start | bytes 4014080 | tf_op jit(solution)/shard_map/all_to_all | solution.py:29
  386.7 123.6 %all-gather.5.cloned.1.call-start = ((), (), s32[]{:S(2)}) async-start(), calls=%async_computation.13 | async-start | bytes 5677056 | tf_op jit(solution)/shard_map/all_gather | solution.py:644
  453.9 34.1 %all-to-all-start.9 = ((bf16[32,48,576]{2,1,0:T(8,128)(2,1)}), bf16[32,48,576]{2,1,0:T(8,128)(2,1)S(1)}, u32[]{:S(2)}, u32[]{:S(2)}) async-start(bf16[32,48,576]{2,1,0:T(8,128)(2,1)} %broadcast_in_dim.129), calls=%async_computation.9 | async-start | bytes 3932160 | tf_op jit(solution)/shard_map/all_to_all | solution.py:29
  (131 other events, 1432.9 us)
Sparse Core Ops, SparseCore 0:
  47.3 49.4 all-gather.2
  342.3 87.3 reduce-scatter.1
  452.5 57.6 all-gather.4

commit v6 on v5

--- a/solution.py
+++ b/solution.py
@@ -551,7 +551,7 @@
     g2 = cotangent.reshape(rows, width)
     x1 = tokens_in.reshape(rows, width).astype(F32)
     xhat1, send1, scale1, packed1 = mix(x1, first, tables, jnp.zeros((1, rows, 128), BF16))
-    later_up, later_qkv, send1 = after((w_up, w_qkv[1], send1), packed1)
+    later_up, send1 = after((w_up, send1), packed1)
     packed1 = exchange(packed1, "ctx")
     spread1 = group_spread(send1[0, :, :width])
 
@@ -559,9 +559,9 @@
         return group_trade(jnp.stack([value[:, i * unit : (i + 1) * unit] for i in range(4)]))
 
     ups = up_columns(later_up[0])
+    out1, full1, lse1 = attend(packed1)
+    ups, spread1, later_g2, later_up, later_qkv = after((ups, spread1, g2, w_up[1], w_qkv[1]), out1)
     half2 = gather_half(later_qkv)
-    out1, full1, lse1 = attend(packed1)
-    ups, spread1, later_g2, later_up, half2 = after((ups, spread1, g2, w_up[1], half2), out1)
     out1 = exchange(out1, "ctx")
     first["up"] = place([b[None] for b in ups], 0).reshape(width, unit)
     second["up"] = place([b[None] for b in up_columns(later_up)], 0).reshape(width, unit)

time: 534 us -> 519 us (0.972)
  waiting for transfers between devices: 167 us -> 151 us
    ppermute x42, waiting for transfers between devices: 95.7 us -> 78 us  [pass_on(): lax.ppermute(value, 'wt', [(i, (i + shift) % count) for i in range(count)])]
    unnamed x204 -> x200, local copies, waits for them, and re-layouts: 24.4 us -> 24.4 us
  transfers between devices with their start and end apart: 56 -> 56, of which waited for: 21 -> 22; matrix products, arithmetic and copies ran while one was open for 22% -> 23% of each run, Pallas kernels for 9% -> 10%
where the time goes in v6:
time: 519 us; the launch traced here: 510 us
  waiting for transfers between devices  151 us (29%)
  starting transfers between devices  111 us (21%)
  local copies, waits for them, and re-layouts  83.8 us (16%)
  Pallas kernels  53 us (10%)
  blocking collectives  39.7 us (8%)
  other arithmetic  28.1 us (5%)
  matrix products  28.1 us (5%)
  between operations  15.8 us (3%)
    ppermute x42, waiting for transfers between devices, pass_on(): lax.ppermute(value, 'wt', [(i, (i + shift) % count) for i in range(count)])  78 us
    all_to_all x9, starting transfers between devices, exchange(): return lax.all_to_all(chunks, axis, 0, 0, tiled=True)  57.1 us
    all_to_all x9, waiting for transfers between devices, exchange(): return lax.all_to_all(chunks, axis, 0, 0, tiled=True)  55.2 us
    ppermute x42, starting transfers between devices, pass_on(): lax.ppermute(value, 'wt', [(i, (i + shift) % count) for i in range(count)])  48.6 us
    all_to_all x1, blocking collectives, exchange(): return lax.all_to_all(chunks, axis, 0, 0, tiled=True)  39.7 us
    dot_general x16, matrix products, dot(): return lax.dot_general(left, right, dims, preferred_element_type=F32)  28.1 us
    pallas_call x11, Pallas kernels, on_chip(): pl.pallas_call(kernel, out_shape=out_shape, in_specs=[spec] * len(operand...  24.9 us
    unnamed x200, local copies, waits for them, and re-layouts  24.4 us
  transfers between devices with their start and end apart: 56, of which 22 were waited for; matrix products, arithmetic and copies ran while one was open for 23% of the time, Pallas kernels for 10%

profile of v6, /device:TPU:1, one launch (start us, length us, event | category | flops | bytes accessed | tf_op | source)
XLA Modules:
  0.0 510.4 jit_solution(6275293343590490055)
XLA Ops:
  28.3 8.4 %collective-permute-done.1 = bf16[96,2304]{1,0:T(8,128)(2,1)S(1)} collective-permute-done((bf16[96,2304]{1,0:T(8,128)(2,1)S(1)}, bf16[96,2304]{1,0:T(8,128)(2,1)S(1)}, u32[]{:S(2)}, u32[]{:S(2)}) %collective-permute-start.1) | collective-permute-done | bytes 442400 | tf_op jit(solution)/shard_map/ppermute | solution.py:34
  56.3 7.2 %all-to-all-start.1 = ((bf16[32,96,128]{2,1,0:T(8,128)(2,1)}), bf16[32,96,128]{2,1,0:T(8,128)(2,1)S(1)}, u32[]{:S(2)}, u32[]{:S(2)}) async-start(bf16[32,96,128]{2,1,0:T(8,128)(2,1)} %get-tuple-element.78), calls=%async_computation.1 | async-start | bytes 1572864 | tf_op jit(solution)/shard_map/all_to_all | solution.py:29
  72.0 4.7 collective-permute-done.7
  77.7 5.7 %attend.2 = (bf16[32,32,128]{2,1,0:T(8,128)(2,1)}, f32[128,1024]{1,0:T(8,128)S(1)}, f32[8,1024]{1,0:T(8,128)S(1)}) custom-call(bf16[32,96,128]{2,1,0:T(8,128)(2,1)S(1)} %all-to-all-done.1.in_ref), custom_call_target="tpu_custom_call" | custom-call | flops 20000000000 | bytes 20000000 | tf_op jit(solution)/shard_map/attend/pallas_call | solution.py:210
  84.2 8.5 %all-to-all-start.2 = ((bf16[32,32,128]{2,1,0:T(8,128)(2,1)}), bf16[32,32,128]{2,1,0:T(8,128)(2,1)S(1)}, u32[]{:S(2)}, u32[]{:S(2)}) async-start(bf16[32,32,128]{2,1,0:T(8,128)(2,1)} %get-tuple-element.79), calls=%async_computation.2 | async-start | bytes 524288 | tf_op jit(solution)/shard_map/all_to_all | solution.py:29
  93.4 8.3 %collective-permute-done.5 = bf16[192,768]{1,0:T(8,128)(2,1)} collective-permute-done((bf16[192,768]{1,0:T(8,128)(2,1)}, bf16[192,768]{1,0:T(8,128)(2,1)}, u32[]{:S(2)}, u32[]{:S(2)}) %collective-permute-start.5) | collective-permute-done | bytes 294944 | tf_op jit(solution)/shard_map/ppermute | solution.py:34
  117.8 12.4 %collective-permute-done.13 = bf16[96,2304]{1,0:T(8,128)(2,1)S(1)} collective-permute-done((bf16[96,2304]{1,0:T(8,128)(2,1)S(1)}, bf16[96,2304]{1,0:T(8,128)(2,1)S(1)}, u32[]{:S(2)}, u32[]{:S(2)}) %collective-permute-start.13) | collective-permute-done | bytes 442400 | tf_op jit(solution)/shard_map/ppermute | solution.py:34
  178.8 8.6 %all-to-all-start.3 = ((bf16[32,128,128]{2,1,0:T(8,128)(2,1)}), bf16[32,128,128]{2,1,0:T(8,128)(2,1)S(1)}, u32[]{:S(2)}, u32[]{:S(2)}) async-start(bf16[32,128,128]{2,1,0:T(8,128)(2,1)} %pad_maximum_fusion.8), calls=%async_computation.3 | async-start | bytes 2097152 | tf_op jit(solution)/shard_map/all_to_all | solution.py:29
  204.7 4.9 attend.3
  209.6 8.4 %attend_back.2 = bf16[32,128,128]{2,1,0:T(8,128)(2,1)S(1)} custom-call(bf16[32,96,128]{2,1,0:T(8,128)(2,1)S(1)} %slice.474.in_ref, bf16[32,32,128]{2,1,0:T(8,128)(2,1)S(1)} %slice.475.grad_ref, f32[128,1024]{1,0:T(8,128)S(1)} %get-tuple-element.96.full_ref, f32[8,1024]{1,0:T(8,128)S(1)} %get-tuple-element.97.lse_ref, ...), custom_call_target="tpu_custom_call" | custom-call | flops 40000000000 | bytes 40000000 | tf_op jit(solution)/shard_map/attend_back/pallas_call | solution.py:234
  219.0 8.2 %all-to-all-start.4 = ((bf16[32,128,128]{2,1,0:T(8,128)(2,1)}), bf16[32,128,128]{2,1,0:T(8,128)(2,1)S(1)}, u32[]{:S(2)}, u32[]{:S(2)}) async-start(bf16[32,128,128]{2,1,0:T(8,128)(2,1)} %copy-done.20), calls=%async_computation.4 | async-start | bytes 2097152 | tf_op jit(solution)/shard_map/all_to_all | solution.py:29
  236.4 4.5 collective-permute-done.35
  241.6 4.5 collective-permute-done.36
  258.3 9.3 %all-to-all-start.5 = ((bf16[32,32,128]{2,1,0:T(8,128)(2,1)}), bf16[32,32,128]{2,1,0:T(8,128)(2,1)S(1)}, u32[]{:S(2)}, u32[]{:S(2)}) async-start(bf16[32,32,128]{2,1,0:T(8,128)(2,1)} %pull.3), calls=%async_computation.5 | async-start | bytes 524288 | tf_op jit(solution)/shard_map/all_to_all | solution.py:29
  272.1 4.5 all-to-all-done.5.grad_ref
  276.6 9.1 %attend_back.3 = bf16[32,96,128]{2,1,0:T(8,128)(2,1)} custom-call(bf16[32,96,128]{2,1,0:T(8,128)(2,1)S(1)} %copy-done.22, bf16[32,32,128]{2,1,0:T(8,128)(2,1)S(1)} %all-to-all-done.5.grad_ref, f32[128,1024]{1,0:T(8,128)S(1)} %copy-done.43, f32[8,1024]{1,0:T(8,128)S(1)} %copy-done.32, bf16[1,8,1024]{2,1,0:T(8,128)(2,1)S(1)} %convert_bitcast_fusion.carry_ref), custom_call_target="tpu_custom_call" | custom-call | flops 40000000000 | bytes 40000000 | tf_op jit(solution)/shard_map/attend_back/pallas_call | solution.py:234
  304.4 10.9 %collective-permute-done.32 = bf16[192,768]{1,0:T(8,128)(2,1)S(1)} collective-permute-done((bf16[192,768]{1,0:T(8,128)(2,1)S(1)}, bf16[192,768]{1,0:T(8,128)(2,1)S(1)}, u32[]{:S(2)}, u32[]{:S(2)}) %collective-permute-start.32) | collective-permute-done | bytes 294944 | tf_op jit(solution)/shard_map/ppermute | solution.py:34
  360.7 4.4 norm_back.3
  372.4 24.8 %all-to-all-done.7 = bf16[4,392,576]{2,1,0:T(8,128)(2,1)S(1)} async-done(((bf16[4,392,576]{2,1,0:T(8,128)(2,1)}), bf16[4,392,576]{2,1,0:T(8,128)(2,1)S(1)}, u32[]{:S(2)}, u32[]{:S(2)}) %all-to-all-start.7) | async-done | bytes 1806368 | tf_op jit(solution)/shard_map/all_to_all | solution.py:29
  397.9 39.7 %all_to_all.50 = bf16[32,56,576]{2,1,0:T(8,128)(2,1)S(1)} all-to-all(bf16[32,56,576]{2,1,0:T(8,128)(2,1)S(1)} %pad_maximum_fusion.3), channel_id=1, replica_groups=mesh['ctx'=32,'wt'=4] {'ctx'}, dimensions={0} | all-to-all | bytes 4128768 | tf_op jit(solution)/shard_map/all_to_all | solution.py:29
  439.5 4.5 all-to-all-start.9
  448.5 25.1 %all-to-all-done.9 = bf16[32,48,576]{2,1,0:T(8,128)(2,1)S(1)} async-done(((bf16[32,48,576]{2,1,0:T(8,128)(2,1)}), bf16[32,48,576]{2,1,0:T(8,128)(2,1)S(1)}, u32[]{:S(2)}, u32[]{:S(2)}) %all-to-all-start.9) | async-done | bytes 1769504 | tf_op jit(solution)/shard_map/all_to_all | solution.py:29
  478.8 17.2 %all-gather.5.cloned.1.call-done.wide_ref = bf16[3584,768]{1,0:T(8,128)(2,1)} async-done(((bf16[112,768]{1,0:T(8,128)(2,1)}), bf16[3584,768]{1,0:T(8,128)(2,1)}) %all-gather.5.cloned.1.call-update) | async-done | bytes 5505040 | tf_op jit(solution)/shard_map/all_gather | solution.py:644
  498.5 4.5 finish.1
  (500 shorter events, 246.0 us)
Async XLA Ops:
  22.4 135.6 %all-gather.3.cloned.1.call-start = ((), (), s32[]{:S(2)}) async-start(), calls=%async_computation.11 | async-start | bytes 2949120 | tf_op jit(solution)/shard_map/all_gather | solution.py:539
  64.2 28.4 %collective-permute-start.8 = (bf16[128,768]{1,0:T(8,128)(2,1)}, bf16[128,768]{1,0:T(8,128)(2,1)}, u32[]{:S(2)}, u32[]{:S(2)}) collective-permute-start(bf16[128,768]{1,0:T(8,128)(2,1)} %slice_bitcast_fusion.13), channel_id=1, source_target_pairs={{0,2},{1,3},{2,0},{3,1},{4,6},{5,7},{6,4},{7,5},{8,10},{9,11},{10,... | collective-permute-start | bytes 589832 | tf_op jit(solution)/shard_map/ppermute | solution.py:34
  66.3 26.3 %collective-permute-start.9 = (bf16[128,768]{1,0:T(8,128)(2,1)}, bf16[128,768]{1,0:T(8,128)(2,1)}, u32[]{:S(2)}, u32[]{:S(2)}) collective-permute-start(bf16[128,768]{1,0:T(8,128)(2,1)} %slice_bitcast_fusion.13), channel_id=1, source_target_pairs={{0,3},{1,0},{2,1},{3,2},{4,7},{5,4},{6,5},{7,6},{8,11},{9,8},{10,9... | collective-permute-start | bytes 589832 | tf_op jit(solution)/shard_map/ppermute | solution.py:34
  70.9 30.8 %collective-permute-start.5 = (bf16[192,768]{1,0:T(8,128)(2,1)}, bf16[192,768]{1,0:T(8,128)(2,1)}, u32[]{:S(2)}, u32[]{:S(2)}) collective-permute-start(bf16[192,768]{1,0:T(8,128)(2,1)} %get-tuple-element.186), channel_id=1, source_target_pairs={{0,2},{1,3},{2,0},{3,1},{4,6},{5,7},{6,4},{7,5},{8,10},{9,11},{10,... | collective-permute-start | bytes 884744 | tf_op jit(solution)/shard_map/ppermute | solution.py:34
  76.7 25.0 %collective-permute-start.6 = (bf16[192,768]{1,0:T(8,128)(2,1)}, bf16[192,768]{1,0:T(8,128)(2,1)}, u32[]{:S(2)}, u32[]{:S(2)}) collective-permute-start(bf16[192,768]{1,0:T(8,128)(2,1)} %get-tuple-element.185), channel_id=1, source_target_pairs={{0,3},{1,0},{2,1},{3,2},{4,7},{5,4},{6,5},{7,6},{8,11},{9,8},{10,9... | collective-permute-start | bytes 884744 | tf_op jit(solution)/shard_map/ppermute | solution.py:34
  84.2 75.6 %all-to-all-start.2 = ((bf16[32,32,128]{2,1,0:T(8,128)(2,1)}), bf16[32,32,128]{2,1,0:T(8,128)(2,1)S(1)}, u32[]{:S(2)}, u32[]{:S(2)}) async-start(bf16[32,32,128]{2,1,0:T(8,128)(2,1)} %get-tuple-element.79), calls=%async_computation.2 | async-start | bytes 524288 | tf_op jit(solution)/shard_map/all_to_all | solution.py:29
  104.9 25.4 %collective-permute-start.13 = (bf16[96,2304]{1,0:T(8,128)(2,1)S(1)}, bf16[96,2304]{1,0:T(8,128)(2,1)S(1)}, u32[]{:S(2)}, u32[]{:S(2)}) collective-permute-start(bf16[96,2304]{1,0:T(8,128)(2,1)S(1)} %get-tuple-element.149), channel_id=1, source_target_pairs={{0,1},{1,2},{2,3},{3,0},{4,5},{5,6},{6,7},{7,4},{8,9},{9,10},{10,1... | collective-permute-start | bytes 1327112 | tf_op jit(solution)/shard_map/ppermute | solution.py:34
  104.9 26.1 %collective-permute-start.14 = (bf16[96,2304]{1,0:T(8,128)(2,1)S(1)}, bf16[96,2304]{1,0:T(8,128)(2,1)S(1)}, u32[]{:S(2)}, u32[]{:S(2)}) collective-permute-start(bf16[96,2304]{1,0:T(8,128)(2,1)S(1)} %get-tuple-element.149), channel_id=1, source_target_pairs={{0,2},{1,3},{2,0},{3,1},{4,6},{5,7},{6,4},{7,5},{8,10},{9,11},{10,... | collective-permute-start | bytes 1327112 | tf_op jit(solution)/shard_map/ppermute | solution.py:34
  106.1 27.2 %collective-permute-start.15 = (bf16[96,2304]{1,0:T(8,128)(2,1)S(1)}, bf16[96,2304]{1,0:T(8,128)(2,1)S(1)}, u32[]{:S(2)}, u32[]{:S(2)}) collective-permute-start(bf16[96,2304]{1,0:T(8,128)(2,1)S(1)} %get-tuple-element.149), channel_id=1, source_target_pairs={{0,3},{1,0},{2,1},{3,2},{4,7},{5,4},{6,5},{7,6},{8,11},{9,8},{10,9... | collective-permute-start | bytes 1327112 | tf_op jit(solution)/shard_map/ppermute | solution.py:34
  134.1 28.1 %collective-permute-start.16 = (bf16[4,96,2304]{2,1,0:T(8,128)(2,1)}, bf16[4,96,2304]{2,1,0:T(8,128)(2,1)}, u32[]{:S(2)}, u32[]{:S(2)}) collective-permute-start(bf16[4,96,2304]{2,1,0:T(8,128)(2,1)} %bitcast_dynamic-update-slice_fusion), channel_id=1, source_target_pairs={{0,4},{4,0},{8,12},{12,8},{16,20},{20,16},{24,28},{28,24},{32,36},... | collective-permute-start | bytes 5308424 | tf_op jit(solution)/shard_map/ppermute | solution.py:79
  148.1 26.4 %collective-permute-start.25 = (bf16[128,768]{1,0:T(8,128)(2,1)}, bf16[128,768]{1,0:T(8,128)(2,1)}, u32[]{:S(2)}, u32[]{:S(2)}) collective-permute-start(bf16[128,768]{1,0:T(8,128)(2,1)} %bitcast.26.g_ref), channel_id=1, source_target_pairs={{0,3},{1,0},{2,1},{3,2},{4,7},{5,4},{6,5},{7,6},{8,11},{9,8},{10,9... | collective-permute-start | bytes 589832 | tf_op jit(solution)/shard_map/ppermute | solution.py:34
  178.8 25.8 %all-to-all-start.3 = ((bf16[32,128,128]{2,1,0:T(8,128)(2,1)}), bf16[32,128,128]{2,1,0:T(8,128)(2,1)S(1)}, u32[]{:S(2)}, u32[]{:S(2)}) async-start(bf16[32,128,128]{2,1,0:T(8,128)(2,1)} %pad_maximum_fusion.8), calls=%async_computation.3 | async-start | bytes 2097152 | tf_op jit(solution)/shard_map/all_to_all | solution.py:29
  199.3 31.4 %collective-permute-start.28 = (bf16[128,1536]{1,0:T(8,128)(2,1)}, bf16[128,1536]{1,0:T(8,128)(2,1)}, u32[]{:S(2)}, u32[]{:S(2)}) collective-permute-start(bf16[128,1536]{1,0:T(8,128)(2,1)} %get-tuple-element.167), channel_id=1, source_target_pairs={{0,2},{1,3},{2,0},{3,1},{4,6},{5,7},{6,4},{7,5},{8,10},{9,11},{10,... | collective-permute-start | bytes 1179656 | tf_op jit(solution)/shard_map/ppermute | solution.py:34
  199.9 30.9 %collective-permute-start.27 = (bf16[128,1536]{1,0:T(8,128)(2,1)}, bf16[128,1536]{1,0:T(8,128)(2,1)}, u32[]{:S(2)}, u32[]{:S(2)}) collective-permute-start(bf16[128,1536]{1,0:T(8,128)(2,1)} %get-tuple-element.168), channel_id=1, source_target_pairs={{0,1},{1,2},{2,3},{3,0},{4,5},{5,6},{6,7},{7,4},{8,9},{9,10},{10,1... | collective-permute-start | bytes 1179656 | tf_op jit(solution)/shard_map/ppermute | solution.py:34
  200.8 30.0 %collective-permute-start.26 = (bf16[128,1536]{1,0:T(8,128)(2,1)}, bf16[128,1536]{1,0:T(8,128)(2,1)}, u32[]{:S(2)}, u32[]{:S(2)}) collective-permute-start(bf16[128,1536]{1,0:T(8,128)(2,1)} %get-tuple-element.166), channel_id=1, source_target_pairs={{0,3},{1,0},{2,1},{3,2},{4,7},{5,4},{6,5},{7,6},{8,11},{9,8},{10,9... | collective-permute-start | bytes 1179656 | tf_op jit(solution)/shard_map/ppermute | solution.py:34
  219.0 27.9 %all-to-all-start.4 = ((bf16[32,128,128]{2,1,0:T(8,128)(2,1)}), bf16[32,128,128]{2,1,0:T(8,128)(2,1)S(1)}, u32[]{:S(2)}, u32[]{:S(2)}) async-start(bf16[32,128,128]{2,1,0:T(8,128)(2,1)} %copy-done.20), calls=%async_computation.4 | async-start | bytes 2097152 | tf_op jit(solution)/shard_map/all_to_all | solution.py:29
  235.3 80.1 %collective-permute-start.37 = (bf16[192,768]{1,0:T(8,128)(2,1)}, bf16[192,768]{1,0:T(8,128)(2,1)}, u32[]{:S(2)}, u32[]{:S(2)}) collective-permute-start(bf16[192,768]{1,0:T(8,128)(2,1)} %get-tuple-element.169), channel_id=1, source_target_pairs={{0,3},{1,0},{2,1},{3,2},{4,7},{5,4},{6,5},{7,6},{8,11},{9,8},{10,9... | collective-permute-start | bytes 884744 | tf_op jit(solution)/shard_map/ppermute | solution.py:34
  285.7 42.0 %all-to-all-start.6 = ((bf16[32,96,128]{2,1,0:T(8,128)(2,1)}), bf16[32,96,128]{2,1,0:T(8,128)(2,1)S(1)}, u32[]{:S(2)}, u32[]{:S(2)}) async-start(bf16[32,96,128]{2,1,0:T(8,128)(2,1)} %attend_back.3), calls=%async_computation.6 | async-start | bytes 1572864 | tf_op jit(solution)/shard_map/all_to_all | solution.py:29
  289.5 148.5 %reduce-scatter.2.cloned.1.call-start = ((), (), s32[]{:S(2)}) async-start(), calls=%async_computation.12 | async-start | bytes 5677056 | tf_op jit(solution)/shard_map/reduce_scatter | solution.py:608
  334.4 25.1 %collective-permute-start.40 = (bf16[128,768]{1,0:T(8,128)(2,1)}, bf16[128,768]{1,0:T(8,128)(2,1)S(1)}, u32[]{:S(2)}, u32[]{:S(2)}) collective-permute-start(bf16[128,768]{1,0:T(8,128)(2,1)} %get-tuple-element.200), channel_id=1, source_target_pairs={{0,2},{1,3},{2,0},{3,1},{4,6},{5,7},{6,4},{7,5},{8,10},{9,11},{10,... | collective-permute-start | bytes 589832 | tf_op jit(solution)/shard_map/ppermute | solution.py:34
  335.2 24.4 %collective-permute-start.39 = (bf16[128,768]{1,0:T(8,128)(2,1)}, bf16[128,768]{1,0:T(8,128)(2,1)S(1)}, u32[]{:S(2)}, u32[]{:S(2)}) collective-permute-start(bf16[128,768]{1,0:T(8,128)(2,1)} %get-tuple-element.201), channel_id=1, source_target_pairs={{0,1},{1,2},{2,3},{3,0},{4,5},{5,6},{6,7},{7,4},{8,9},{9,10},{10,1... | collective-permute-start | bytes 589832 | tf_op jit(solution)/shard_map/ppermute | solution.py:34
  368.6 28.6 %all-to-all-start.7 = ((bf16[4,392,576]{2,1,0:T(8,128)(2,1)}), bf16[4,392,576]{2,1,0:T(8,128)(2,1)S(1)}, u32[]{:S(2)}, u32[]{:S(2)}) async-start(bf16[4,392,576]{2,1,0:T(8,128)(2,1)} %pad_maximum_fusion.4), calls=%async_computation.7 | async-start | bytes 4014080 | tf_op jit(solution)/shard_map/all_to_all | solution.py:29
  372.3 123.6 %all-gather.5.cloned.1.call-start = ((), (), s32[]{:S(2)}) async-start(), calls=%async_computation.13 | async-start | bytes 5677056 | tf_op jit(solution)/shard_map/all_gather | solution.py:644
  439.5 34.1 %all-to-all-start.9 = ((bf16[32,48,576]{2,1,0:T(8,128)(2,1)}), bf16[32,48,576]{2,1,0:T(8,128)(2,1)S(1)}, u32[]{:S(2)}, u32[]{:S(2)}) async-start(bf16[32,48,576]{2,1,0:T(8,128)(2,1)} %broadcast_in_dim.129), calls=%async_computation.9 | async-start | bytes 3932160 | tf_op jit(solution)/shard_map/all_to_all | solution.py:29
  (129 other events, 1400.2 us)
Sparse Core Ops, SparseCore 0:
  47.2 48.3 all-gather.2
  327.9 88.2 reduce-scatter.1
  438.2 57.7 all-gather.4
